TPU v7x, 256 devices: a whole 4x4x8 slice. The times are simulated.
256 devices in a mesh: lev: 8 (over y, core), wave: 32 (over z, x).
Axes of the slice: x: 4, y: 4, z: 8, core: 2. Of those that a mesh axis runs over, the one named last changes fastest.
Arguments:
- state: float32 [256, 2, 8, 2, 32, 256], P('wave', None, None, None, 'lev'), may hold values from -6 to 6
- wave_table: int32 [256], replicated, may hold values from 0 to 255, as said below
- lat_table: int32 [384], replicated, may hold values from 0 to 383, as said below
- lat_weight: float32 [384], replicated, may hold values from 0.5 to 2
- legendre: bfloat16 [256, 384, 256], P('wave'), may hold values from -0.375 to 0.375
- w_in: bfloat16 [64, 512], replicated, may hold values from -0.75 to 0.75
- b_in: float32 [512], replicated, may hold values from -3 to 3
- w_lat: float32 [512], replicated, may hold values from -4 to 4
- w_mid: bfloat16 [512, 512], replicated, may hold values from -0.25 to 0.25
- b_mid: float32 [512], replicated, may hold values from -3 to 3
- w_out: bfloat16 [512, 64], replicated, may hold values from -0.25 to 0.25
- target: float32 [32], P('lev'), may hold values from -4 to 4
- coupling: float32 [256, 32, 32], replicated, may hold values from -1 to 1
Outputs:
- new_state: float32 [256, 2, 8, 2, 32, 256], P('wave', None, None, None, 'lev')
- grid_tend: bfloat16 [8, 64, 384, 768], P('lev', None, 'wave')
Inputs may be any that keep to these rules, and one draw needn't show every extreme that they name: `wave_table`: a permutation in which slots 2k and 2k+1 hold a wavenumber m and 255-m. `lat_table`: a permutation in which slots 2k and 2k+1 hold a latitude i and 383-i.
All inputs are finite; a program needn't handle non-finite values.
Results may differ from a plain program's by a relative error of at most 0.0075.
Values may be sent and summed in bfloat16 or wider, within the bound.
No kernel may reach another device: no remote copies, remote signals or barrier semaphores. Data moves between devices by JAX's collectives and lax.ppermute only.
A program may use at most 128 MiB of HBM per device.

v0:
```python
import math

import jax
import jax.numpy as jnp
from jax import lax
from jax.sharding import PartitionSpec as P

MW = 256
NTOT = 256
NLAT = 384
NLON = 768


time_step = 0.5
nudge_rate = 0.5
diffusion = 0.5


def for_sending(value):

    def short(part):
        return part.astype(jnp.bfloat16) if part.dtype == jnp.float32 else part

    return jax.tree.map(short, value)


def tables(wave_table):
    longitude = jnp.arange(NLON, dtype=jnp.int32)
    phase_int = wave_table[:, None] * longitude[None, :] % NLON
    angles = phase_int.astype(jnp.float32) * (2.0 * math.pi / NLON)
    return (jnp.cos(angles).astype(jnp.bfloat16), jnp.sin(angles).astype(jnp.bfloat16))


def per_device(
    state,
    wave_table,
    lat_table,
    lat_weight,
    legendre,
    w_in,
    b_in,
    w_lat,
    w_mid,
    b_mid,
    w_out,
    target,
    coupling,
):
    wave_slots, _, members, fields, lev_rows, degrees = state.shape
    wave_count = lax.axis_size("wave")
    lev_count = lax.axis_size("lev")
    wave_pos = lax.axis_index("wave")
    lev_pos = lax.axis_index("lev")
    band_rows = lat_table.shape[0] // wave_count
    levels = lev_rows * lev_count
    own_members = members // lev_count
    own_waves = lax.dynamic_slice_in_dim(wave_table, wave_pos * wave_slots, wave_slots)
    degree = jnp.arange(degrees, dtype=jnp.int32)
    live_mask = (degree[None, :] >= own_waves[:, None]).astype(jnp.float32)
    live_full = live_mask[:, None, None, None, None, :]
    own_zero = (own_waves == 0).astype(jnp.float32)
    zero_slot = (wave_table == 0).astype(jnp.float32)
    cosine_table, sine_table = tables(wave_table)
    both_tables = jnp.stack([cosine_table, -sine_table], axis=1).reshape(MW * 2, NLON)
    band_lats = lax.dynamic_slice_in_dim(lat_table, wave_pos * band_rows, band_rows)
    band_weight = jnp.take(lat_weight, band_lats)
    legendre_band = jnp.take(legendre, lat_table, axis=1)
    weight_slots = jnp.take(lat_weight, lat_table)
    weight_total = jnp.sum(lat_weight)
    state_bf = (state * live_full).astype(jnp.bfloat16)
    fourier_slots = jnp.einsum(
        "mrn,mtn->mrt",
        state_bf.reshape(wave_slots, -1, degrees),
        legendre_band,
        preferred_element_type=jnp.float32,
    ).astype(jnp.bfloat16)
    fourier = fourier_slots.reshape(wave_slots, 2, members, fields, lev_rows, wave_count, band_rows)
    band_coef = lax.all_to_all(fourier, "wave", split_axis=5, concat_axis=0, tiled=True)
    synthesis = lax.dot_general(
        band_coef.reshape(MW * 2, -1),
        both_tables,
        (((0,), (0,)), ((), ())),
        preferred_element_type=jnp.float32,
    )
    grid_bf = (
        (synthesis * MW ** (-0.5))
        .astype(jnp.bfloat16)
        .reshape(members, fields, lev_rows, band_rows, NLON)
    )
    columns = lax.all_to_all(grid_bf, "lev", split_axis=0, concat_axis=2, tiled=True)
    features = columns.reshape(own_members, fields * levels, band_rows * NLON)
    coslat = jnp.sin((band_lats.astype(jnp.float32) + 0.5) * (math.pi / NLAT))
    column_cos = jnp.repeat(coslat, NLON)
    hidden = (
        jnp.einsum("kh,ekc->ehc", w_in, features, preferred_element_type=jnp.float32)
        + b_in[None, :, None]
        + column_cos[None, None, :] * w_lat[None, :, None]
    )
    hidden = jax.nn.silu(hidden).astype(jnp.bfloat16)
    hidden = jax.nn.silu(
        jnp.einsum("kh,ekc->ehc", w_mid, hidden, preferred_element_type=jnp.float32)
        + b_mid[None, :, None]
    ).astype(jnp.bfloat16)
    tendency = jnp.einsum("hk,ehc->ekc", w_out, hidden, preferred_element_type=jnp.float32).astype(
        jnp.bfloat16
    )
    grid_tend = tendency.reshape(own_members, fields * levels, band_rows, NLON)
    returned = lax.all_to_all(
        tendency.reshape(own_members, fields, levels, band_rows, NLON),
        "lev",
        split_axis=2,
        concat_axis=0,
        tiled=True,
    )
    lat_scale = band_weight * ((2.0 * MW) ** 0.5 / NLON)
    coef = lax.dot_general(
        both_tables,
        returned.reshape(-1, NLON),
        (((1,), (1,)), ((), ())),
        preferred_element_type=jnp.float32,
    )
    tendw = (coef.reshape(MW, 2, members, fields, lev_rows, band_rows) * lat_scale).astype(
        jnp.bfloat16
    )
    part_state = jnp.einsum(
        "melt,m,t->el", band_coef[:, 0, :, 0, :, 0, :].astype(jnp.float32), zero_slot, band_weight
    )
    part_tend = jnp.einsum("melt,m->el", tendw[:, 0, :, 0].astype(jnp.float32), zero_slot)
    mean_state, mean_tend = lax.psum((part_state, part_tend), "wave")
    spectral = lax.all_to_all(tendw, "wave", split_axis=0, concat_axis=5, tiled=True)
    global_mean = (mean_state + time_step * mean_tend) / weight_total
    nudge_add = nudge_rate * (target[None, :] - global_mean)
    legconst = jnp.einsum(
        "mtn,t->mn", legendre_band, weight_slots, preferred_element_type=jnp.float32
    )
    spec_tend = jnp.einsum(
        "mrt,mtn->mrn",
        spectral.reshape(wave_slots, -1, spectral.shape[5]),
        legendre_band,
        preferred_element_type=jnp.float32,
    ).reshape(state.shape)
    extra_term = nudge_add[None, :, :, None] * (own_zero[:, None] * legconst)[:, None, None, :]
    spec_tend = spec_tend.at[:, 0, :, 0].add(extra_term)
    explicit = (state + time_step * spec_tend) * live_full
    temp_rhs = explicit[:, :, :, 0]
    mode_rows = degrees // lev_count
    mode_block = lax.dynamic_slice_in_dim(coupling, lev_pos * mode_rows, mode_rows, 0)
    modes_turned = jnp.transpose(mode_block, (1, 2, 0))
    coupled = jnp.sum(
        modes_turned[None, None, None]
        * lax.all_to_all(
            temp_rhs.astype(jnp.bfloat16), "lev", split_axis=4, concat_axis=3, tiled=True
        ).astype(temp_rhs.dtype)[:, :, :, None],
        axis=4,
    )
    new_temp = lax.all_to_all(
        for_sending(coupled), "lev", split_axis=3, concat_axis=4, tiled=True
    ).astype(coupled.dtype)
    shrink = 1.0 / (1.0 + diffusion * (degree * (degree + 1)).astype(jnp.float32) / (NTOT * NTOT))
    new_hum = explicit[:, :, :, 1] * shrink
    return (jnp.stack([new_temp, new_hum], axis=3), grid_tend)


def solution(mesh):
    placed = (
        P("wave", None, None, None, "lev", None),
        P(),
        P(),
        P(),
        P("wave", None, None),
        P(),
        P(),
        P(),
        P(),
        P(),
        P(),
        P("lev"),
        P(),
    )
    return jax.shard_map(
        per_device,
        mesh=mesh,
        in_specs=placed,
        out_specs=(P("wave", None, None, None, "lev", None), P("lev", None, "wave", None)),
        check_vma=False,
    )
```

profile of v0, /device:TPU:1, one launch (start us, length us, event | category | flops | bytes accessed | tf_op | source)
XLA Modules:
  0.0 478.4 jit_solution(10405820274307148573)
XLA Ops:
  0.7 0.8 compare_select_fusion
  1.5 3.6 gather_fusion.2
  5.1 1.2 broadcast_select_fusion.1
  6.3 1.3 compare_convert_fusion
  7.7 8.1 %gather_fusion = bf16[384,8,256]{2,0,1:T(8,128)(2,1)} fusion(bf16[8,384,256]{2,1,0:T(8,128)(2,1)S(1)} %copy-done, s32[1024]{0:T(1024)S(1)} %pad_clamp_fusion.1), kind=kCustom, calls=%fused_computation | custom fusion | bytes 3147264 | tf_op jit(solution)/shard_map/jit(_take)/gather | solution.py:67
  15.8 0.6 multiply_convert_fusion.3
  16.4 2.0 fusion.14
  18.4 20.0 %reshape.323 = bf16[8,2,8,2,4,32,12]{6,5,4,3,2,1,0:T(8,128)(2,1)} reshape(bf16[8,128,384]{2,1,0:T(8,128)(2,1)S(1)} %fusion.14) | data formatting | bytes 1572864 | tf_op jit(solution)/shard_map/reshape | solution.py:77
  38.5 8.3 %copy.168 = bf16[8,2,8,2,4,32,12]{6,4,3,2,1,0,5:T(4,128)(2,1)} copy(bf16[8,2,8,2,4,32,12]{6,5,4,3,2,1,0:T(8,128)(2,1)} %reshape.323) | data formatting | bytes 1572864 | tf_op jit(solution)/shard_map/reshape | solution.py:77
  46.8 17.3 %reshape.376 = bf16[32,2,6144]{2,1,0:T(2,128)(2,1)} reshape(bf16[32,8,2,8,2,4,12]{6,5,4,3,2,1,0:T(4,128)(2,1)} %bitcast.158) | data formatting | bytes 1572864
  64.1 12.3 %all-to-all-start = ((bf16[32,2,6144]{2,1,0:T(2,128)(2,1)}), bf16[32,2,6144]{2,1,0:T(2,128)(2,1)S(1)}, u32[]{:S(2)}, u32[]{:S(2)}) async-start(bf16[32,2,6144]{2,1,0:T(2,128)(2,1)} %reshape.376), calls=%async_computation | async-start | bytes 1572864 | tf_op jit(solution)/shard_map/all_to_all | solution.py:78
  76.4 3.2 fusion.24
  79.7 3.2 cosine_convert_fusion
  82.9 0.7 copy-done.9
  83.7 0.8 copy.116
  84.5 1.2 reshape.325
  85.7 11.8 %all-to-all-done = bf16[32,2,6144]{2,1,0:T(2,128)(2,1)S(1)} async-done(((bf16[32,2,6144]{2,1,0:T(2,128)(2,1)}), bf16[32,2,6144]{2,1,0:T(2,128)(2,1)S(1)}, u32[]{:S(2)}, u32[]{:S(2)}) %all-to-all-start) | async-done | bytes 786464 | tf_op jit(solution)/shard_map/all_to_all | solution.py:78
  97.5 20.4 %reshape.377 = bf16[32,8,2,8,2,4,12]{6,5,4,3,2,1,0:T(4,128)(2,1)} reshape(bf16[32,2,6144]{2,1,0:T(2,128)(2,1)S(1)} %all-to-all-done) | data formatting | bytes 1572864
  117.8 8.4 %bitcast_bitcast_fusion = bf16[32,8,2,8,2,4,1,12]{7,5,4,3,2,1,0,6:T(4,128)(2,1)} fusion(bf16[32,8,2,8,2,4,12]{6,5,4,3,2,1,0:T(4,128)(2,1)} %reshape.377), kind=kLoop, calls=%fused_computation.85 | loop fusion | bytes 1572864 | tf_op jit(solution)/shard_map/all_to_all | solution.py:78
  126.2 16.2 %reshape.324 = bf16[512,768]{1,0:T(8,128)(2,1)S(1)} reshape(bf16[32,8,2,8,2,4,1,12]{7,5,4,3,2,1,0,6:T(4,128)(2,1)} %bitcast_bitcast_fusion) | data formatting | bytes 1572864 | tf_op jit(solution)/shard_map/reshape | solution.py:80
  142.5 0.8 multiply_convert_fusion.1
  143.6 1.6 copy.117
  145.2 7.5 %all-to-all-start.1 = ((bf16[8,2,4,12,768]{4,2,3,1,0:T(4,128)(2,1)}), bf16[8,2,4,12,768]{4,2,3,1,0:T(4,128)(2,1)S(1)}, u32[]{:S(2)}, u32[]{:S(2)}) async-start(bf16[8,2,4,12,768]{4,2,3,1,0:T(4,128)(2,1)} %copy.117), calls=%async_computation.1 | async-start | bytes 2359296 | tf_op jit(solution)/shard_map/all_to_all | solution.py:90
  153.0 16.2 %all-to-all-done.1 = bf16[8,2,4,12,768]{4,2,3,1,0:T(4,128)(2,1)S(1)} async-done(((bf16[8,2,4,12,768]{4,2,3,1,0:T(4,128)(2,1)}), bf16[8,2,4,12,768]{4,2,3,1,0:T(4,128)(2,1)S(1)}, u32[]{:S(2)}, u32[]{:S(2)}) %all-to-all-start.1) | async-done | bytes 1179680 | tf_op jit(solution)/shard_map/all_to_all | solution.py:90
  170.1 8.0 %fusion.5 = bf16[512,9216]{0,1:T(8,128)(2,1)} fusion(bf16[64,9216]{1,0:T(8,128)(2,1)S(1)} %bitcast.175, bf16[64,512]{1,0:T(8,128)(2,1)S(1)} %copy-done.22, f32[512]{0:T(512)S(1)} %copy-done.24, f32[9216]{0:T(1024)S(1)} %mul.200, f32[512]{0:T(512)S(1)} %copy-done.25), kind=kOutput, calls=%fused_computation.15 | convolution fusion | flops 641728512 | bytes 10723328 | tf_op jit(solution)/shard_map/kh,ekc->ehc/dot_general | solution.py:95
  178.1 13.3 %convolution_convert_fusion = bf16[9216,64]{0,1:T(8,128)(2,1)S(1)} fusion(bf16[512,64]{0,1:T(8,128)(2,1)S(1)} %copy-done.23, bf16[512,9216]{0,1:T(8,128)(2,1)} %fusion.5, bf16[512,512]{1,0:T(8,128)(2,1)S(1)} %copy-done.21, f32[512]{0:T(512)S(1)} %copy-done.26), kind=kOutput, calls=%fused_computation.16 | convolution fusion | flops 5464719360 | bytes 11208704 | tf_op jit(solution)/shard_map/hk,ehc->ekc/dot_general | solution.py:104
  191.4 1.0 copy-done.3
  192.4 0.9 reshape.330
  193.3 2.2 copy.119
  195.5 4.7 all-to-all-start.2
  200.3 0.7 gather_fusion.1
  201.0 15.6 %all-to-all-done.2 = bf16[1,2,32,12,768]{4,1,3,0,2:T(2,128)(2,1)S(1)} async-done(((bf16[1,2,32,12,768]{4,1,3,0,2:T(2,128)(2,1)}), bf16[1,2,32,12,768]{4,1,3,0,2:T(2,128)(2,1)S(1)}, u32[]{:S(2)}, u32[]{:S(2)}) %all-to-all-start.2) | async-done | bytes 1179680 | tf_op jit(solution)/shard_map/all_to_all | solution.py:108
  216.7 1.0 multiply_convert_fusion.2
  217.7 10.7 %copy.121 = bf16[256,2,8,2,4,12]{5,4,3,2,1,0:T(4,128)(2,1)} copy(bf16[256,2,8,2,4,12]{0,5,4,3,2,1:T(8,128)(2,1)S(1)} %multiply_convert_fusion.2) | data formatting | bytes 1572864 | tf_op jit(solution)/shard_map/convert_element_type | solution.py:122
  228.4 17.3 %reshape.378 = bf16[32,2,6144]{2,1,0:T(2,128)(2,1)} reshape(bf16[256,2,8,2,4,12]{5,4,3,2,1,0:T(4,128)(2,1)} %copy.121) | data formatting | bytes 1572864
  245.7 4.9 %all-to-all-start.3 = ((bf16[32,2,6144]{2,1,0:T(2,128)(2,1)}), bf16[32,2,6144]{2,1,0:T(2,128)(2,1)S(1)}, u32[]{:S(2)}, u32[]{:S(2)}) async-start(bf16[32,2,6144]{2,1,0:T(2,128)(2,1)} %reshape.378), calls=%async_computation.3 | async-start | bytes 1572864 | tf_op jit(solution)/shard_map/all_to_all | solution.py:130
  250.7 0.6 reduce_sum.28
  251.3 1.8 fusion.7
  253.2 3.7 slice.64
  256.9 3.7 copy.150
  261.8 62.9 %all-reduce = (f32[8,4]{1,0:T(8,128)S(1)}, f32[8,4]{1,0:T(8,128)S(1)}) all-reduce(f32[8,4]{1,0:T(8,128)S(1)} %bitcast.177, f32[8,4]{1,0:T(8,128)S(1)} %bitcast.178), channel_id=1, replica_groups=mesh['lev'=8,'wave'=32] {'wave'}, use_global_device_ids=true, to_apply=%region_0.1 | all-reduce | flops 64 | bytes 512 | tf_op jit(solution)/shard_map/psum | solution.py:129
  324.7 0.7 subtract_multiply_fusion
  325.3 20.8 %reshape.379 = bf16[256,2,8,2,4,12]{5,4,3,2,1,0:T(4,128)(2,1)} reshape(bf16[32,2,6144]{2,1,0:T(2,128)(2,1)S(1)} %all-to-all-done.3) | data formatting | bytes 1572864
  346.2 20.0 %copy.166 = bf16[32,8,2,8,2,4,12]{6,0,5,4,3,2,1:T(8,128)(2,1)} copy(bf16[32,8,2,8,2,4,12]{6,5,4,3,2,1,0:T(4,128)(2,1)} %bitcast.159) | data formatting | bytes 1572864 | tf_op jit(solution)/shard_map/all_to_all | solution.py:130
  366.2 15.1 %reshape.331 = bf16[8,128,384]{2,1,0:T(8,128)(2,1)S(1)} reshape(bf16[8,2,8,2,4,32,12]{6,5,4,3,2,1,0:T(8,128)(2,1)} %bitcast.160) | data formatting | bytes 1572864 | tf_op jit(solution)/shard_map/reshape | solution.py:138
  381.9 0.6 copy.148
  383.1 0.6 add_multiply_fusion
  383.8 1.0 copy-done.7
  384.8 5.3 %copy.128 = bf16[8,2,8,4,256]{0,3,2,1,4:T(4,128)(2,1)} copy(bf16[8,2,8,4,256]{4,0,3,2,1:T(8,128)(2,1)S(1)} %fusion.25) | data formatting | bytes 524288 | tf_op jit(solution)/shard_map/convert_element_type | solution.py:152
  390.1 6.6 %reshape.380 = bf16[8,2,8192]{2,1,0:T(2,128)(2,1)} reshape(bf16[256,2,8,4,8]{4,3,2,1,0:T(4,128)(2,1)} %bitcast.161) | data formatting | bytes 524288
  396.7 17.8 %all-to-all-start.4 = ((bf16[8,2,8192]{2,1,0:T(2,128)(2,1)}), bf16[8,2,8192]{2,1,0:T(2,128)(2,1)S(1)}, u32[]{:S(2)}, u32[]{:S(2)}) async-start(bf16[8,2,8192]{2,1,0:T(2,128)(2,1)} %reshape.380), calls=%async_computation.4 | async-start | bytes 524288 | tf_op jit(solution)/shard_map/all_to_all | solution.py:151
  414.7 1.1 copy.167
  415.8 5.1 %all-to-all-done.4 = bf16[8,2,8192]{2,1,0:T(2,128)(2,1)S(1)} async-done(((bf16[8,2,8192]{2,1,0:T(2,128)(2,1)}), bf16[8,2,8192]{2,1,0:T(2,128)(2,1)S(1)}, u32[]{:S(2)}, u32[]{:S(2)}) %all-to-all-start.4) | async-done | bytes 262176 | tf_op jit(solution)/shard_map/all_to_all | solution.py:151
  420.9 5.9 %reshape.381 = bf16[256,2,8,4,8]{4,3,2,1,0:T(4,128)(2,1)} reshape(bf16[8,2,8192]{2,1,0:T(2,128)(2,1)S(1)} %all-to-all-done.4) | data formatting | bytes 524288
  426.8 6.2 %copy.129 = bf16[8,2,8,4,256]{4,2,3,1,0:T(8,128)(2,1)S(1)} copy(bf16[8,2,8,4,256]{0,3,2,1,4:T(4,128)(2,1)} %bitcast.162) | data formatting | bytes 524288 | tf_op jit(solution)/shard_map/all_to_all | solution.py:151
  433.0 1.7 reshape.336
  434.8 2.0 copy.130
  437.1 20.7 %multiply_reduce_fusion = bf16[8,2,8,32,32]{4,3,2,1,0:T(8,128)(2,1)S(1)} fusion(f32[8,2,8,32,32]{4,3,2,1,0:T(8,128)S(1)} %copy.131, f32[32,32,32]{2,1,0:T(8,128)S(1)} %dynamic-slice_bitcast_fusion), kind=kLoop, calls=%fused_computation.3 | loop fusion | flops 8257536 | bytes 917504 | tf_op jit(solution)/shard_map/reduce_sum | solution.py:149
  458.2 1.7 reshape.382
  459.9 4.4 all-to-all-start.5
  464.3 6.5 %all-to-all-done.5 = bf16[8,2,8192]{2,1,0:T(2,128)(2,1)S(1)} async-done(((bf16[8,2,8192]{2,1,0:T(2,128)(2,1)}), bf16[8,2,8192]{2,1,0:T(2,128)(2,1)S(1)}, u32[]{:S(2)}, u32[]{:S(2)}) %all-to-all-start.5) | async-done | bytes 262176 | tf_op jit(solution)/shard_map/all_to_all | solution.py:156
  471.8 2.6 copy.147
  474.4 2.2 reshape.375
  476.8 1.4 copy.136
  (86 shorter events, 6.3 us)
Async XLA Ops:
  0.6 7.1 %copy-start = (bf16[8,384,256]{2,1,0:T(8,128)(2,1)S(1)}, bf16[8,384,256]{2,1,0:T(8,128)(2,1)}, u32[]{:S(2)}) copy-start(bf16[8,384,256]{2,1,0:T(8,128)(2,1)} %param.19) | copy-start | bytes 4718596
  6.3 10.0 %copy-start.18 = (pred[384]{0:T(512)(128)(4,1)}, pred[384]{0:T(512)(128)(4,1)S(1)}, u32[]{:S(2)}) copy-start(pred[384]{0:T(512)(128)(4,1)S(1)} %get-tuple-element.33) | copy-start | bytes 1156
  7.7 8.1 %copy-start.5 = (f32[8,2,8,2,4,256]{5,4,3,2,1,0:T(4,128)S(1)}, f32[8,2,8,2,4,256]{5,4,3,2,1,0:T(4,128)}, u32[]{:S(2)}) copy-start(f32[8,2,8,2,4,256]{5,4,3,2,1,0:T(4,128)} %param.15) | copy-start | bytes 3145732
  46.8 29.6 %copy-start.15 = (s32[256]{0:T(256)S(1)}, s32[256]{0:T(256)}, u32[]{:S(2)}) copy-start(s32[256]{0:T(256)} %param.16) | copy-start | bytes 3076
  64.1 33.4 %all-to-all-start = ((bf16[32,2,6144]{2,1,0:T(2,128)(2,1)}), bf16[32,2,6144]{2,1,0:T(2,128)(2,1)S(1)}, u32[]{:S(2)}, u32[]{:S(2)}) async-start(bf16[32,2,6144]{2,1,0:T(2,128)(2,1)} %reshape.376), calls=%async_computation | async-start | bytes 1572864 | tf_op jit(solution)/shard_map/all_to_all | solution.py:78
  82.9 0.8 copy-start.9
  126.2 16.2 %copy-start.12 = (bf16[512,768]{1,0:T(8,128)(2,1)S(1)}, bf16[512,768]{1,0:T(8,128)(2,1)}, u32[]{:S(2)}) copy-start(bf16[512,768]{1,0:T(8,128)(2,1)} %reshape.325) | copy-start | bytes 2359300
  143.6 9.1 %copy-start.14 = (s32[384]{0:T(512)S(1)}, s32[384]{0:T(512)}, u32[]{:S(2)}) copy-start(s32[384]{0:T(512)} %param.17) | copy-start | bytes 4612
  145.2 24.0 %all-to-all-start.1 = ((bf16[8,2,4,12,768]{4,2,3,1,0:T(4,128)(2,1)}), bf16[8,2,4,12,768]{4,2,3,1,0:T(4,128)(2,1)S(1)}, u32[]{:S(2)}, u32[]{:S(2)}) async-start(bf16[8,2,4,12,768]{4,2,3,1,0:T(4,128)(2,1)} %copy.117), calls=%async_computation.1 | async-start | bytes 2359296 | tf_op jit(solution)/shard_map/all_to_all | solution.py:90
  169.2 0.8 copy-start.22
  169.2 0.8 copy-start.24
  169.2 0.8 copy-start.25
  170.0 8.0 %copy-start.21 = (bf16[512,512]{1,0:T(8,128)(2,1)S(1)}, bf16[512,512]{1,0:T(8,128)(2,1)}, u32[]{:S(2)}) copy-start(bf16[512,512]{1,0:T(8,128)(2,1)} %param.23) | copy-start | bytes 1572868
  170.0 8.1 %copy-start.23 = (bf16[512,64]{0,1:T(8,128)(2,1)S(1)}, bf16[512,64]{0,1:T(8,128)(2,1)}, u32[]{:S(2)}) copy-start(bf16[512,64]{0,1:T(8,128)(2,1)} %param.25) | copy-start | bytes 196612
  170.0 8.0 %copy-start.26 = (f32[512]{0:T(512)S(1)}, f32[512]{0:T(512)}, u32[]{:S(2)}) copy-start(f32[512]{0:T(512)} %param.24) | copy-start | bytes 6148
  191.4 1.0 copy-start.3
  193.3 7.0 %copy-start.2 = (f32[384]{0:T(512)S(1)}, f32[384]{0:T(512)}, u32[]{:S(2)}) copy-start(f32[384]{0:T(512)} %param.18) | copy-start | bytes 4612
  195.5 21.2 %copy-start.10 = (bf16[256,1,768]{2,0,1:T(8,128)(2,1)S(1)}, bf16[256,1,768]{2,0,1:T(8,128)(2,1)}, u32[]{:S(2)}) copy-start(bf16[256,1,768]{2,0,1:T(8,128)(2,1)} %copy-done.9) | copy-start | bytes 1179652
  195.5 21.2 %all-to-all-start.2 = ((bf16[1,2,32,12,768]{4,1,3,0,2:T(2,128)(2,1)}), bf16[1,2,32,12,768]{4,1,3,0,2:T(2,128)(2,1)S(1)}, u32[]{:S(2)}, u32[]{:S(2)}) async-start(bf16[1,2,32,12,768]{4,1,3,0,2:T(2,128)(2,1)} %copy.119), calls=%async_computation.2 | async-start | bytes 2359296 | tf_op jit(solution)/shard_map/all_to_all | solution.py:108
  228.4 22.8 %copy-start.16 = (bf16[384]{0:T(512)(128)(2,1)S(1)}, bf16[384]{0:T(512)(128)(2,1)}, u32[]{:S(2)}) copy-start(bf16[384]{0:T(512)(128)(2,1)} %get-tuple-element.32) | copy-start | bytes 2308
  228.4 22.8 %copy-start.19 = (pred[384]{0:T(512)(128)(4,1)S(1)}, pred[384]{0:T(512)(128)(4,1)}, u32[]{:S(2)}) copy-start(pred[384]{0:T(512)(128)(4,1)} %copy-done.18) | copy-start | bytes 1156
  245.7 7.4 %copy-start.17 = (f32[8]{0:T(128)S(1)}, f32[8]{0:T(128)}, u32[]{:S(2)}) copy-start(f32[8]{0:T(128)} %get-tuple-element.30) | copy-start | bytes 100
  245.7 79.7 %all-to-all-start.3 = ((bf16[32,2,6144]{2,1,0:T(2,128)(2,1)}), bf16[32,2,6144]{2,1,0:T(2,128)(2,1)S(1)}, u32[]{:S(2)}, u32[]{:S(2)}) async-start(bf16[32,2,6144]{2,1,0:T(2,128)(2,1)} %reshape.378), calls=%async_computation.3 | async-start | bytes 1572864 | tf_op jit(solution)/shard_map/all_to_all | solution.py:130
  256.9 67.8 %copy-start.20 = (f32[4]{0:T(128)S(1)}, f32[4]{0:T(128)}, u32[]{:S(2)}) copy-start(f32[4]{0:T(128)} %param.26) | copy-start | bytes 52
  366.2 15.1 %copy-start.11 = (bf16[384,8,256]{2,0,1:T(8,128)(2,1)S(1)}, bf16[384,8,256]{2,0,1:T(8,128)(2,1)}, u32[]{:S(2)}) copy-start(bf16[384,8,256]{2,0,1:T(8,128)(2,1)} %gather_fusion) | copy-start | bytes 4718596
  381.9 1.2 copy-start.6
  383.7 1.0 copy-start.7
  390.1 24.3 %copy-start.13 = (f32[256,32,32]{0,2,1:T(8,128)S(1)}, f32[256,32,32]{0,2,1:T(8,128)}, u32[]{:S(2)}) copy-start(f32[256,32,32]{0,2,1:T(8,128)} %param.27) | copy-start | bytes 3145732
  390.1 24.6 %copy-start.4 = (bf16[9216,64]{0,1:T(8,128)(2,1)S(1)}, bf16[9216,64]{0,1:T(8,128)(2,1)}, u32[]{:S(2)}) copy-start(bf16[9216,64]{0,1:T(8,128)(2,1)} %copy-done.3) | copy-start | bytes 3538948
  396.7 24.2 %all-to-all-start.4 = ((bf16[8,2,8192]{2,1,0:T(2,128)(2,1)}), bf16[8,2,8192]{2,1,0:T(2,128)(2,1)S(1)}, u32[]{:S(2)}, u32[]{:S(2)}) async-start(bf16[8,2,8192]{2,1,0:T(2,128)(2,1)} %reshape.380), calls=%async_computation.4 | async-start | bytes 524288 | tf_op jit(solution)/shard_map/all_to_all | solution.py:151
  458.2 6.0 %copy-start.8 = (f32[8,2,8,2,4,256]{5,0,4,3,2,1:T(8,128)S(1)}, f32[8,2,8,2,4,256]{5,0,4,3,2,1:T(8,128)}, u32[]{:S(2)}) copy-start(f32[8,2,8,2,4,256]{5,0,4,3,2,1:T(8,128)} %copy-done.7) | copy-start | bytes 3145732
  459.9 10.9 %all-to-all-start.5 = ((bf16[8,2,8192]{2,1,0:T(2,128)(2,1)}), bf16[8,2,8192]{2,1,0:T(2,128)(2,1)S(1)}, u32[]{:S(2)}, u32[]{:S(2)}) async-start(bf16[8,2,8192]{2,1,0:T(2,128)(2,1)} %reshape.382), calls=%async_computation.5 | async-start | bytes 524288 | tf_op jit(solution)/shard_map/all_to_all | solution.py:156
  474.4 3.8 copy-start.1
where the time goes:
time: 487 us; the launch traced here: 478 us
  local copies, waits for them, and re-layouts  245 us (50%)
  blocking collectives  62.9 us (13%)
  waiting for transfers between devices  55.3 us (11%)
  starting transfers between devices  51.5 us (11%)
  other arithmetic  34.1 us (7%)
  matrix products  28.4 us (6%)
    unnamed x65, local copies, waits for them, and re-layouts  99.3 us
    psum x1, blocking collectives, per_device(): mean_state, mean_tend = lax.psum((part_state, part_tend), 'wave')  62.9 us
    reshape x2, local copies, waits for them, and re-layouts, per_device(): fourier_slots.reshape(wave_slots, 2, members, fields, lev_rows, wave_coun...  28.4 us
    reduce_sum x1, other arithmetic, per_device(): jnp.sum(modes_turned[None, None, None] * lax.all_to_all(temp_rhs.astype(j...  20.7 us
    all_to_all x1, local copies, waits for them, and re-layouts, per_device(): lax.all_to_all(tendw, 'wave', split_axis=0, concat_axis=5, tiled=True)  20 us
    all_to_all x1, starting transfers between devices, per_device(): lax.all_to_all(temp_rhs.astype(jnp.bfloat16), 'lev', split_axis=4, concat...  17.8 us
    all_to_all x1, waiting for transfers between devices, per_device(): lax.all_to_all(grid_bf, 'lev', split_axis=0, concat_axis=2, tiled=True)  16.2 us
    reshape x1, local copies, waits for them, and re-layouts, per_device(): band_coef.reshape(MW * 2, -1)  16.2 us
  transfers between devices with their start and end apart: 6, of which 5 were waited for; matrix products, arithmetic and copies ran while one was open for 5% of the time, Pallas kernels for 0%

commit v1 on v0

v1 whole, which is shorter than its diff:
```python
import math

import jax
import jax.numpy as jnp
from jax import lax
from jax.experimental import pallas as pl
from jax.experimental.pallas import tpu as pltpu
from jax.sharding import PartitionSpec as P

F32 = jnp.float32
BF16 = jnp.bfloat16
WAVES = 32
LEVS = 8
MW = 256
NTOT = 256
NLAT = 384
NLON = 768
HID = 512
SLOTS = MW // WAVES
BAND = NLAT // WAVES
PAIRS = BAND // 2
LEVELS = 32
FEAT = 64
ROWL = LEVELS // LEVS
time_step = 0.5
nudge_rate = 0.5
diffusion = 0.5

VMEM = pl.BlockSpec(memory_space=pltpu.VMEM)
SMEM = pl.BlockSpec(memory_space=pltpu.SMEM)
HBM = pl.BlockSpec(memory_space=pltpu.HBM)


def call(body, outs, scratch, flops, operands, specs, name):
    operands = [
        pltpu.with_memory_space_constraint(o, pltpu.HBM) if spec in (HBM, SMEM) else o
        for o, spec in zip(operands, specs)
    ]
    return pl.pallas_call(
        body,
        out_shape=outs,
        in_specs=specs,
        out_specs=jax.tree.map(lambda o: HBM if isinstance(o, pl.MemoryRef) else VMEM, outs),
        scratch_shapes=scratch,
        compiler_params=pltpu.CompilerParams(vmem_limit_bytes=40 * 2**20),
        cost_estimate=pl.CostEstimate(flops=flops, bytes_accessed=2 * 10**6, transcendentals=0),
        name=name,
    )(*operands)


def out(shape, dtype):
    return jax.ShapeDtypeStruct(shape, dtype)


def live_row(waves_ref, first, j):
    lane = lax.broadcasted_iota(jnp.int32, (1, NTOT), 1)
    return (lane >= waves_ref[first + j]).astype(F32)


def pack_state(waves_ref, target_ref, state_hbm, send_ref, rows_ref, state_ref, sems):
    copies = [
        pltpu.make_async_copy(state_hbm.at[j], state_ref.at[j], sems.at[j]) for j in range(SLOTS)
    ]
    for copy in copies:
        copy.start()
    first = lax.axis_index("wave") * SLOTS
    lane = lax.broadcasted_iota(jnp.int32, (16, NTOT), 1)
    row = lax.broadcasted_iota(jnp.int32, (16, NTOT), 0)
    rider = jnp.zeros((16, NTOT), F32)
    for i in range(ROWL):
        rider = jnp.where((lane == 0) & (row == i), target_ref[i], rider)
    for j in range(SLOTS):
        live = live_row(waves_ref, first, j)
        extra = None
        if j < 2:
            extra = rider * jnp.full((16, NTOT), waves_ref[first + j] > 127, jnp.int32).astype(F32)
        copies[j].wait()
        for e in range(LEVS):
            for c in range(2):
                for f in range(2):
                    rows_ref[e, j, c * 8 + f * 4 : c * 8 + f * 4 + 4, :] = state_ref[j, c, e, f]
            block = rows_ref[e, j] * live
            send_ref[e, j] = (block if extra is None else block + extra).astype(BF16)


def sine_of(q):
    a = q * (2.0 * math.pi / NLON)
    b = a * a
    total = jnp.full_like(b, -2.5052108e-8)
    for factor in (2.7557319e-6, -1.9841270e-4, 8.3333333e-3, -1.6666667e-1, 1.0):
        total = total * b + factor
    return total * a


def prepare(
    lats_ref, weights_ref, lat_ref, weight_ref, waves_ref, legendre_ref, w_in_ref, b_in_ref, w_lat_ref, w_mid_ref,
    b_mid_ref, band_ref, const_ref, cos_t_hbm, sin_t_hbm, cos_hbm, sin_hbm, first_hbm, mid_hbm, bias_hbm, scale_hbm,
    hot_ref, cos_t_ref, sin_t_ref, cos_ref, sin_ref, first_ref, mid_ref, bias_ref, scale_ref, sems,
):
    pairs = (
        (cos_t_ref, cos_t_hbm),
        (sin_t_ref, sin_t_hbm),
        (cos_ref, cos_hbm),
        (sin_ref, sin_hbm),
        (first_ref, first_hbm),
        (mid_ref, mid_hbm),
        (bias_ref, bias_hbm),
        (scale_ref, scale_hbm),
    )
    copies = [pltpu.make_async_copy(a, b, sems.at[i]) for i, (a, b) in enumerate(pairs)]
    x = lax.broadcasted_iota(jnp.int32, (NLON, MW), 0)
    product = (x * waves_ref[...]).astype(F32)
    phase = product - NLON * jnp.floor(product * (1.0 / NLON) + 0.5)
    size = jnp.abs(phase)
    cosine = sine_of(NLON // 4 - size)
    sine = sine_of(jnp.where(size > NLON // 4, jnp.where(phase > 0, 1.0, -1.0) * (NLON // 2) - phase, phase))
    sine = -sine
    cos_t_ref[...] = (cosine * MW**-0.5).astype(BF16)
    copies[0].start()
    sin_t_ref[...] = (sine * MW**-0.5).astype(BF16)
    copies[1].start()
    cos_ref[...] = cosine.T.astype(BF16)
    copies[2].start()
    sin_ref[...] = sine.T.astype(BF16)
    copies[3].start()
    first_ref[...] = jnp.zeros_like(first_ref)
    half_in = (w_in_ref[...].astype(F32) * 0.5).astype(BF16)
    first_ref[0, :FEAT, :] = half_in
    first_ref[1, FEAT:, :] = half_in
    copies[4].start()
    mid_ref[...] = (w_mid_ref[...].astype(F32) * 0.5).astype(BF16)
    copies[5].start()
    lane = lax.broadcasted_iota(jnp.int32, (1, BAND * FEAT), 1)
    scale = jnp.zeros((1, BAND * FEAT), F32)
    own = lax.axis_index("wave") * BAND
    for b in range(BAND):
        t = lats_ref[own + b]
        here = (lane >= b * FEAT) & (lane < (b + 1) * FEAT)
        scale = jnp.where(here, weights_ref[t] * ((2.0 * MW) ** 0.5 / NLON), scale)
        at = jnp.full((1, HID), t, jnp.int32).astype(F32)
        coslat = jnp.sin((at + 0.5) * (math.pi / NLAT))
        bias_ref[b : b + 1, :] = 0.5 * (b_in_ref[...] + coslat * w_lat_ref[...])
    bias_ref[BAND : BAND + 1, :] = 0.5 * b_mid_ref[...]
    copies[6].start()
    scale_ref[...] = scale
    copies[7].start()

    t = lax.broadcasted_iota(jnp.int32, (NLAT, NLAT), 0)
    hot = (t == lat_ref[...]).astype(F32).T
    for i in range(NLAT // 128):
        hot_ref[i] = hot[:, i * 128 : (i + 1) * 128]
    pick = []
    for parity in range(2):
        parts = [
            jnp.concatenate(
                [hot_ref[i, pl.ds(2 * p + parity, WAVES, stride=BAND), :] for p in range(PAIRS)], axis=0
            )
            for i in range(NLAT // 128)
        ]
        pick.append(jnp.concatenate(parts, axis=1).astype(BF16))
    weight = weight_ref[...]
    high = weight.astype(BF16)
    low = (weight - high.astype(F32)).astype(BF16)
    row = lax.broadcasted_iota(jnp.int32, (16, NLAT), 0)
    both = jnp.where(row == 0, high.astype(F32), jnp.where(row == 1, low.astype(F32), 0.0))
    both = both.astype(BF16)
    for j in range(SLOTS):
        block = legendre_ref[j]
        for parity in range(2):
            band_ref[j, :, parity * NTOT : (parity + 1) * NTOT] = jnp.dot(
                pick[parity], block, preferred_element_type=F32
            ).astype(BF16)
        sums = jnp.dot(both, block, preferred_element_type=F32)
        const_ref[j : j + 1, :] = jnp.sum(sums, axis=0, keepdims=True)
    for copy in copies:
        copy.wait()


def to_fourier(
    waves_ref, recv_ref, band_ref, fourier_ref, state_ref, target_ref, rows_ref, both_ref, total_ref
):
    first = lax.axis_index("wave") * SLOTS
    both_ref[...] = jnp.zeros_like(both_ref)
    target = jnp.zeros((LEVELS, 1), F32)
    for j in range(SLOTS):
        live = live_row(waves_ref, first, j)
        k = j % 2
        for src in range(LEVS):
            block = recv_ref[src, j].astype(F32)
            for c in range(2):
                for f in range(2):
                    at = f * LEVELS + src * ROWL
                    rows_ref[k, c, at : at + 4, :] = block[c * 8 + f * 4 : c * 8 + f * 4 + 4, :]
        for c in range(2):
            if j < 2 and c == 0:
                here = jnp.full((LEVELS, 1), waves_ref[first + j] > 127, jnp.int32).astype(F32)
                target = target + here * rows_ref[k, 0, :LEVELS, :1]
            part = (rows_ref[k, c] * live).astype(BF16)
            state_ref[j, c] = part
            both_ref[k, c * 128 : c * 128 + 64, :NTOT] = part
            both_ref[k, c * 128 + 64 : c * 128 + 128, NTOT:] = part
        sums = lax.dot_general(
            band_ref[j], both_ref[k], (((1,), (1,)), ((), ())), preferred_element_type=F32
        )
        for c in range(2):
            for p in range(PAIRS):
                total_ref[c * PAIRS + p, pl.ds(j, WAVES, stride=SLOTS), :] = sums[
                    p * WAVES : (p + 1) * WAVES, c * 128 : (c + 1) * 128
                ]
    target_ref[...] = jnp.broadcast_to(target, (LEVELS, 128))
    for i in range(2 * PAIRS):
        fourier_ref[:, i * 128 : (i + 1) * 128] = total_ref[i].astype(BF16)


def half_silu(u):
    return (u + u * jnp.tanh(u)).astype(BF16)


TILE = 256


def dot_lanes(a, b):
    return lax.dot_general(a, b, (((1,), (1,)), ((), ())), preferred_element_type=F32)


def columns(
    coef_ref, cos_t_hbm, sin_t_hbm, first_hbm, bias_hbm, mid_hbm, last_hbm, cos_hbm, sin_hbm, scale_hbm,
    tendw_ref, grid_hbm, values_ref, grid_ref,
    cos_t_ref, sin_t_ref, first_ref, bias_ref, mid_ref, last_ref, cos_ref, sin_ref, scale_ref, sems, grid_sems,
):
    pairs = (
        (cos_t_hbm, cos_t_ref),
        (sin_t_hbm, sin_t_ref),
        (first_hbm, first_ref),
        (bias_hbm, bias_ref),
        (mid_hbm, mid_ref),
        (last_hbm, last_ref),
        (cos_hbm, cos_ref),
        (sin_hbm, sin_ref),
        (scale_hbm, scale_ref),
    )
    copies = [pltpu.make_async_copy(a, b, sems.at[i]) for i, (a, b) in enumerate(pairs)]
    for copy in copies:
        copy.start()

    def grid_copy(p):
        rows = pl.ds(2 * p, 2)
        return pltpu.make_async_copy(grid_ref.at[rows], grid_hbm.at[rows], grid_sems.at[p])

    half = BAND * FEAT
    copies[0].wait()
    copies[1].wait()
    values = jnp.dot(cos_t_ref[...], coef_ref[:, :half], preferred_element_type=F32)
    values += jnp.dot(sin_t_ref[...], coef_ref[:, half:], preferred_element_type=F32)
    for p in range(PAIRS):
        values_ref[p] = values[:, p * 128 : (p + 1) * 128].astype(BF16)
    for copy in copies[2:6]:
        copy.wait()

    def pair(p, carry):
        for tile in range(NLON // TILE):
            rows = slice(tile * TILE, (tile + 1) * TILE)
            v = values_ref[p, rows, :]
            hidden = [
                half_silu(
                    jnp.dot(v, first_ref[q], preferred_element_type=F32)
                    + bias_ref[pl.ds(2 * p + q, 1), :]
                )
                for q in range(2)
            ]
            hidden = [
                half_silu(
                    jnp.dot(h, mid_ref[...], preferred_element_type=F32)
                    + bias_ref[BAND : BAND + 1, :]
                )
                for h in hidden
            ]
            for q in range(2):
                grid_ref[2 * p + q, :, rows] = dot_lanes(last_ref[...], hidden[q]).astype(BF16)
        grid_copy(p).start()
        return carry

    lax.fori_loop(0, PAIRS, pair, 0)
    for copy in copies[6:]:
        copy.wait()
    tend = grid_ref[...].reshape(half, NLON)
    scale = scale_ref[...]
    for c, table in enumerate((cos_ref, sin_ref)):
        tendw_ref[:, c * half : (c + 1) * half] = (dot_lanes(table[...], tend) * scale).astype(BF16)
    for p in range(PAIRS):
        grid_copy(p).wait()


def to_spectral(
    waves_ref, recv_ref, band_ref, state_ref, const_ref, weight_ref, target_ref, coupling_ref,
    send_ref, wide_ref, temp_ref, rows_ref, matrix_ref,
):
    first = lax.axis_index("wave") * SLOTS
    for i in range(2 * PAIRS):
        wide_ref[i] = recv_ref[:, i * 128 : (i + 1) * 128].astype(F32)
    for i in range(2):
        matrix_ref[i] = coupling_ref[:, i * 128 : (i + 1) * 128]
    target = target_ref[:, :1]
    weight_total = jnp.sum(weight_ref[...], axis=1, keepdims=True)
    degree = lax.broadcasted_iota(jnp.int32, (1, NTOT), 1)
    shrink = 1.0 / (1.0 + diffusion * (degree * (degree + 1)).astype(F32) / (NTOT * NTOT))
    for j in range(SLOTS):
        live = live_row(waves_ref, first, j)
        is_zero = (jnp.full((1, NTOT), waves_ref[first + j], jnp.int32) == 0).astype(F32)
        block = jnp.concatenate(
            [
                jnp.concatenate(
                    [wide_ref[c * PAIRS + p, pl.ds(j, WAVES, stride=SLOTS), :] for c in range(2)],
                    axis=1,
                )
                for p in range(PAIRS)
            ],
            axis=0,
        )
        turned = block.T
        tend_sum = jnp.sum(turned[:128], axis=1, keepdims=True)
        parts = turned.astype(BF16)
        even = jnp.concatenate([parts[:64], parts[128:192]], axis=0)
        odd = jnp.concatenate([parts[64:128], parts[192:]], axis=0)
        spec = jnp.dot(even, band_ref[j, :, :NTOT], preferred_element_type=F32)
        spec += jnp.dot(odd, band_ref[j, :, NTOT:], preferred_element_type=F32)
        const = const_ref[j : j + 1, :]
        for c in range(2):
            old = state_ref[j, c].astype(F32)
            old_temp, old_hum = old[:LEVELS], old[LEVELS:]
            temp = spec[c * 64 : c * 64 + 32]
            hum = spec[c * 64 + 32 : c * 64 + 64]
            if c == 0:
                mean = jnp.sum(old_temp * const, axis=1, keepdims=True)
                mean += time_step * (tend_sum[:32] + tend_sum[64:96])
                nudge = nudge_rate * (target - mean / weight_total)
                temp = temp + nudge * (const * is_zero)
            temp_ref[j * 2 + c] = (old_temp + time_step * temp) * live
            hum = (old_hum + time_step * hum) * (live * shrink)
            for d in range(LEVS):
                rows_ref[d, j, c * 8 + 4 : c * 8 + 8, :] = hum[d * 4 : d * 4 + 4]
    group = 4
    for g in range(2 * SLOTS // group):

        def step(k, totals):
            matrix = jnp.concatenate(
                [matrix_ref[i, pl.ds(k, LEVELS, stride=LEVELS), :] for i in range(2)], axis=1
            )
            return tuple(
                totals[q] + matrix * temp_ref[g * group + q, pl.ds(k, 1), :] for q in range(group)
            )

        zero = jnp.zeros((LEVELS, NTOT), F32)
        totals = lax.fori_loop(0, LEVELS, step, (zero,) * group, unroll=4)
        for q in range(group):
            j, c = divmod(g * group + q, 2)
            for d in range(LEVS):
                rows_ref[d, j, c * 8 : c * 8 + 4, :] = totals[q][d * 4 : d * 4 + 4]
    send_ref[...] = rows_ref[...].astype(BF16)


def unpack_state(recv_ref, state_ref):
    for e in range(LEVS):
        for j in range(SLOTS):
            block = recv_ref[e, j].astype(F32)
            for c in range(2):
                for f in range(2):
                    state_ref[j, c, e, f] = block[c * 8 + f * 4 : c * 8 + f * 4 + 4, :]


def per_device(
    state,
    wave_table,
    lat_table,
    lat_weight,
    legendre,
    w_in,
    b_in,
    w_lat,
    w_mid,
    b_mid,
    w_out,
    target,
    coupling,
):
    message = (LEVS, SLOTS, 16, NTOT)
    sent = call(
        pack_state,
        out(message, BF16),
        [
            pltpu.VMEM(message, F32),
            pltpu.VMEM(state.shape, F32),
            pltpu.SemaphoreType.DMA((SLOTS,)),
        ],
        10**8,
        (wave_table, target, state),
        [SMEM] * 2 + [HBM],
        "pack_state",
    )
    members = lax.all_to_all(sent, "lev", 0, 0, tiled=True)
    table, turned, weights = (NLON, MW), (MW, NLON), (2, 2 * FEAT, HID)
    made = [
        (table, BF16),
        (table, BF16),
        (turned, BF16),
        (turned, BF16),
        (weights, BF16),
        ((HID, HID), BF16),
        ((16, HID), F32),
        ((1, BAND * FEAT), F32),
    ]
    band, const, cos_t, sin_t, cos, sin, first, mid, bias, scale = call(
        prepare,
        (
            out((SLOTS, PAIRS * WAVES, 2 * NTOT), BF16),
            out((SLOTS, NTOT), F32),
            *(pltpu.HBM(*m) for m in made),
        ),
        [
            pltpu.VMEM((NLAT // 128, NLAT, 128), F32),
            *(pltpu.VMEM(*m) for m in made),
            pltpu.SemaphoreType.DMA((len(made),)),
        ],
        6 * 10**9,
        (
            lat_table,
            lat_weight,
            lat_table[None],
            lat_weight[None],
            wave_table[None],
            legendre,
            w_in,
            b_in[None],
            w_lat[None],
            w_mid,
            b_mid[None],
        ),
        [SMEM] * 2 + [VMEM] * 9,
        "prepare",
    )
    fourier, state_bf, target_all = call(
        to_fourier,
        (
            out((MW, 2 * BAND * FEAT), BF16),
            out((SLOTS, 2, FEAT, NTOT), BF16),
            out((LEVELS, 128), F32),
        ),
        [
            pltpu.VMEM((2, 2, FEAT, NTOT), F32),
            pltpu.VMEM((2, NTOT, 2 * NTOT), BF16),
            pltpu.VMEM((2 * PAIRS, MW, 128), F32),
        ],
        10**9,
        (wave_table, members, band),
        [SMEM] + [VMEM] * 2,
        "to_fourier",
    )
    coef = lax.all_to_all(fourier, "wave", 0, 0, tiled=True)
    tendw, grid = call(
        columns,
        (
            out((MW, 2 * BAND * FEAT), BF16),
            pltpu.HBM((BAND, FEAT, NLON), BF16),
        ),
        [
            pltpu.VMEM((PAIRS, NLON, 128), BF16),
            pltpu.VMEM((BAND, FEAT, NLON), BF16),
            *(pltpu.VMEM(v.shape, v.dtype) for v in (cos_t, sin_t, first, bias, mid, w_out.T, cos, sin, scale)),
            pltpu.SemaphoreType.DMA((9,)),
            pltpu.SemaphoreType.DMA((PAIRS,)),
        ],
        10**10,
        (coef, cos_t, sin_t, first, bias, mid, w_out.T, cos, sin, scale),
        [VMEM] + [HBM] * 9,
        "columns",
    )
    back = lax.all_to_all(tendw, "wave", 0, 0, tiled=True)
    moved = call(
        to_spectral,
        out(message, BF16),
        [
            pltpu.VMEM((2 * PAIRS, MW, 128), F32),
            pltpu.VMEM((2 * SLOTS, LEVELS, NTOT), F32),
            pltpu.VMEM(message, F32),
            pltpu.VMEM((2, LEVELS * LEVELS, 128), F32),
        ],
        10**9,
        (
            wave_table,
            back,
            band,
            state_bf,
            const,
            lat_weight[None],
            target_all,
            jnp.transpose(coupling, (1, 2, 0)).reshape(LEVELS * LEVELS, NTOT),
        ),
        [SMEM] + [VMEM] * 7,
        "to_spectral",
    )
    returned = lax.all_to_all(moved, "lev", 0, 0, tiled=True)
    new_state = call(
        unpack_state,
        out(state.shape, F32),
        [],
        10**8,
        (returned,),
        [VMEM],
        "unpack_state",
    )
    return new_state, jnp.transpose(grid, (1, 0, 2))[None]


def solution(mesh):
    placed = (
        P("wave", None, None, None, "lev", None),
        P(),
        P(),
        P(),
        P("wave", None, None),
        P(),
        P(),
        P(),
        P(),
        P(),
        P(),
        P("lev"),
        P(),
    )
    return jax.shard_map(
        per_device,
        mesh=mesh,
        in_specs=placed,
        out_specs=(P("wave", None, None, None, "lev", None), P("lev", None, "wave", None)),
        check_vma=False,
    )
```

time: 487 us -> 117 us (0.24); the launches traced: 478 us -> 116 us
  local copies, waits for them, and re-layouts: 245 us -> 1.45 us
  waiting for transfers between devices: 55.3 us -> 3.56 us
  starting transfers between devices: 51.5 us -> 6.65 us
  other arithmetic: 34.1 us -> 0 us
  Pallas kernels: 0 us -> 31.1 us
  matrix products: 28.4 us -> 0 us
  blocking collectives: 62.9 us -> 72.6 us
    unnamed x65 -> x20, local copies, waits for them, and re-layouts: 99.3 us -> 1.45 us
    all_to_all x0 -> x3, blocking collectives: none -> 72.6 us  [the longest x1 31.2 us: per_device(): coef = lax.all_to_all(fourier, 'wave', 0, 0, tiled=True)]
    reshape x11 -> x0, local copies, waits for them, and re-layouts: 67.6 us -> none  [the longest x2 28.4 us: per_device(): fourier_slots.reshape(wave_slots, 2, members, fields, lev_rows, wave_coun...]
    psum x1 -> x0, blocking collectives: 62.9 us -> none  [per_device(): mean_state, mean_tend = lax.psum((part_state, part_tend), 'wave')]
    all_to_all x6 -> x1, waiting for transfers between devices: 55.3 us -> 3.56 us  [per_device(): members = lax.all_to_all(sent, 'lev', 0, 0, tiled=True)]
    all_to_all x6 -> x1, starting transfers between devices: 51.5 us -> 6.65 us  [per_device(): members = lax.all_to_all(sent, 'lev', 0, 0, tiled=True)]
    all_to_all x5 -> x0, local copies, waits for them, and re-layouts: 35.2 us -> none  [the longest x1 20 us: per_device(): lax.all_to_all(tendw, 'wave', split_axis=0, concat_axis=5, tiled=True)]
    pallas_call x0 -> x6, Pallas kernels: none -> 31.1 us  [call(): pl.pallas_call(body, out_shape=outs, in_specs=specs, out_specs=jax.tree.m...]
  transfers between devices with their start and end apart: 6 -> 1, of which waited for: 5 -> 1; matrix products, arithmetic and copies ran while one was open for 5% -> 0% of each run, Pallas kernels for 0% -> 4%
where the time goes in v1:
time: 117 us; the launch traced here: 116 us
  blocking collectives  72.6 us (62%)
  Pallas kernels  31.1 us (27%)
  starting transfers between devices  6.65 us (6%)
  waiting for transfers between devices  3.56 us (3%)
  local copies, waits for them, and re-layouts  1.45 us (1%)
    all_to_all x1, blocking collectives, per_device(): coef = lax.all_to_all(fourier, 'wave', 0, 0, tiled=True)  31.2 us
    pallas_call x6, Pallas kernels, call(): pl.pallas_call(body, out_shape=outs, in_specs=specs, out_specs=jax.tree.m...  31.1 us
    all_to_all x1, blocking collectives, per_device(): back = lax.all_to_all(tendw, 'wave', 0, 0, tiled=True)  25.5 us
    all_to_all x1, blocking collectives, per_device(): returned = lax.all_to_all(moved, 'lev', 0, 0, tiled=True)  15.9 us
    all_to_all x1, starting transfers between devices, per_device(): members = lax.all_to_all(sent, 'lev', 0, 0, tiled=True)  6.65 us
    all_to_all x1, waiting for transfers between devices, per_device(): members = lax.all_to_all(sent, 'lev', 0, 0, tiled=True)  3.56 us
  transfers between devices with their start and end apart: 1, of which 1 were waited for; matrix products, arithmetic and copies ran while one was open for 0% of the time, Pallas kernels for 4%

profile of v1, /device:TPU:1, one launch (start us, length us, event | category | flops | bytes accessed | tf_op | source)
XLA Modules:
  0.0 116.2 jit_solution(8120454486420471003)
XLA Ops:
  0.6 0.0 copy-start.1
  0.6 0.0 copy-start.9
  0.7 0.0 copy-start.8
  0.7 0.0 copy-start.7
  0.7 0.0 copy-start.3
  0.7 0.0 copy-start.6
  0.7 0.0 copy-start.5
  0.7 0.0 copy-start.4
  0.7 3.0 %pack_state.1 = bf16[8,8,16,256]{3,2,1,0:T(8,128)(2,1)} custom-call(s32[256]{0:T(256)} %waves_ref.5, f32[4]{0:T(128)} %target_ref.1, f32[8,2,8,2,4,256]{5,4,3,2,1,0:T(4,128)} %state_hbm.1), custom_call_target="tpu_custom_call" | custom-call | flops 100000000 | bytes 2000000 | tf_op jit(solution)/shard_map/pack_state/pallas_call | solution.py:39
  3.7 6.6 %all-to-all-start = ((bf16[8,8,16,256]{3,2,1,0:T(8,128)(2,1)}), bf16[8,8,16,256]{3,2,1,0:T(8,128)(2,1)S(1)}, u32[]{:S(2)}, u32[]{:S(2)}) async-start(bf16[8,8,16,256]{3,2,1,0:T(8,128)(2,1)} %pack_state.1), calls=%async_computation | async-start | bytes 1048576 | tf_op jit(solution)/shard_map/all_to_all | solution.py:400
  10.4 0.0 copy-done.9
  10.4 0.0 copy-done.8
  10.4 0.0 copy-done.1
  10.4 0.0 copy-done.7
  10.4 0.0 copy-done.3
  10.4 0.0 copy-done.6
  10.4 0.0 copy-done.5
  10.5 0.0 copy-done.4
  10.5 0.0 copy-start.2
  10.5 1.4 %copy-done.2 = bf16[8,384,256]{2,1,0:T(8,128)(2,1)S(1)} copy-done((bf16[8,384,256]{2,1,0:T(8,128)(2,1)S(1)}, bf16[8,384,256]{2,1,0:T(8,128)(2,1)}, u32[]{:S(2)}) %copy-start.2) | copy-done | bytes 1572888
  11.9 4.4 %prepare.1 = (bf16[8,192,512]{2,1,0:T(8,128)(2,1)S(1)}, f32[8,256]{1,0:T(8,128)S(1)}, bf16[768,256]{1,0:T(8,128)(2,1)}, bf16[768,256]{1,0:T(8,128)(2,1)}, bf16[2...) custom-call(s32[384]{0:T(512)} %lats_ref.1, ...), custom_call_target="tpu_custom_call" | custom-call | flops 6000000000 | bytes 2000000 | tf_op jit(solution)/shard_map/prepare/pallas_call | solution.py:39
  16.3 3.6 %all-to-all-done.recv_ref = bf16[8,8,16,256]{3,2,1,0:T(8,128)(2,1)S(1)} async-done(((bf16[8,8,16,256]{3,2,1,0:T(8,128)(2,1)}), bf16[8,8,16,256]{3,2,1,0:T(8,128)(2,1)S(1)}, u32[]{:S(2)}, u32[]{:S(2)}) %all-to-all-start) | async-done | bytes 524320 | tf_op jit(solution)/shard_map/all_to_all | solution.py:400
  19.9 1.7 %to_fourier.1 = (bf16[256,1536]{1,0:T(8,128)(2,1)S(1)}, bf16[8,2,64,256]{3,2,1,0:T(8,128)(2,1)S(1)}, f32[32,128]{1,0:T(8,128)S(1)}) custom-call(s32[256]{0:T(256)} %waves_ref.5, bf16[8,8,16,256]{3,2,1,0:T(8,128)(2,1)S(1)} %all-to-all-done.recv_ref, bf16[8,192,512]{2,1,0:T(8,128)(2,1)S(1)} %get-tuple-element.17.band_ref), custom_call_target="tpu_custom_call" | custom-call | flops 1000000000 | bytes 2000000 | tf_op jit(solution)/shard_map/to_fourier/pallas_call | solution.py:39
  21.6 31.2 %all_to_all.32 = bf16[32,8,1536]{2,1,0:T(8,128)(2,1)S(1)} all-to-all(bf16[32,8,1536]{2,1,0:T(8,128)(2,1)S(1)} %bitcast.19), channel_id=1, replica_groups=mesh['lev'=8,'wave'=32] {'wave'}, dimensions={0} | all-to-all | bytes 1572864 | tf_op jit(solution)/shard_map/all_to_all | solution.py:458
  52.8 14.4 %columns.1 = (bf16[256,1536]{1,0:T(8,128)(2,1)S(1)}, bf16[12,64,768]{2,1,0:T(8,128)(2,1)}) custom-call(bf16[256,1536]{1,0:T(8,128)(2,1)S(1)} %bitcast.17, bf16[768,256]{1,0:T(8,128)(2,1)} %get-tuple-element.19.cos_t_hbm, bf16[768,256]{1,0:T(8,128)(2,1)} %get-tuple-element.20.sin_t_hbm, bf16[2,128,512]{2,1,0:T(8,128)(2,1)} %get-tuple-element.21.first_hbm, ...), custom_call_target="tpu_custom_call" | custom-call | flops 10000000000 | bytes 2000000 | tf_op jit(solution)/shard_map/columns/pallas_call | solution.py:39
  67.1 0.0 copy-start
  67.2 25.5 %all_to_all.33 = bf16[32,8,1536]{2,1,0:T(8,128)(2,1)S(1)} all-to-all(bf16[32,8,1536]{2,1,0:T(8,128)(2,1)S(1)} %bitcast.18), channel_id=1, replica_groups=mesh['lev'=8,'wave'=32] {'wave'}, dimensions={0} | all-to-all | bytes 1572864 | tf_op jit(solution)/shard_map/all_to_all | solution.py:477
  92.7 0.0 copy-done
  92.7 6.6 %to_spectral.1 = bf16[8,8,16,256]{3,2,1,0:T(8,128)(2,1)S(1)} custom-call(s32[256]{0:T(256)} %waves_ref.5, bf16[256,1536]{1,0:T(8,128)(2,1)S(1)} %bitcast.15, bf16[8,192,512]{2,1,0:T(8,128)(2,1)S(1)} %get-tuple-element.17.band_ref, bf16[8,2,64,256]{3,2,1,0:T(8,128)(2,1)S(1)} %get-tuple-element.28.state_ref, f32[8,256]{1,0:T(8,128)S(1)} %get-tuple-element.29.const_ref, ...), custom_call_target="tpu_custom_call" | custom-call | flops 1000000000 | bytes 2000000 | tf_op jit(solution)/shard_map/to_spectral/pallas_call | solution.py:39
  99.3 15.9 %all_to_all.34.recv_ref = bf16[8,8,16,256]{3,2,1,0:T(8,128)(2,1)S(1)} all-to-all(bf16[8,8,16,256]{3,2,1,0:T(8,128)(2,1)S(1)} %to_spectral.1), channel_id=1, replica_groups=mesh['lev'=8,'wave'=32] {'lev'}, dimensions={0} | all-to-all | bytes 1048576 | tf_op jit(solution)/shard_map/all_to_all | solution.py:501
  115.1 1.0 unpack_state.1
  (2 shorter events, 0.0 us)
Async XLA Ops:
  0.6 9.8 %copy-start.1 = (s32[256]{0:T(256)S(1)}, s32[256]{0:T(256)}, u32[]{:S(2)}) copy-start(s32[256]{0:T(256)} %waves_ref.5) | copy-start | bytes 3076
  0.6 9.7 %copy-start.9 = (f32[384]{0:T(512)S(1)}, f32[384]{0:T(512)}, u32[]{:S(2)}) copy-start(f32[384]{0:T(512)} %weights_ref.1) | copy-start | bytes 4612
  0.7 9.7 %copy-start.8 = (s32[384]{0:T(512)S(1)}, s32[384]{0:T(512)}, u32[]{:S(2)}) copy-start(s32[384]{0:T(512)} %lats_ref.1) | copy-start | bytes 4612
  0.7 9.7 %copy-start.7 = (f32[512]{0:T(512)S(1)}, f32[512]{0:T(512)}, u32[]{:S(2)}) copy-start(f32[512]{0:T(512)} %param.22) | copy-start | bytes 6148
  0.7 9.7 %copy-start.3 = (bf16[512,512]{1,0:T(8,128)(2,1)S(1)}, bf16[512,512]{1,0:T(8,128)(2,1)}, u32[]{:S(2)}) copy-start(bf16[512,512]{1,0:T(8,128)(2,1)} %w_mid_ref.1) | copy-start | bytes 1572868
  0.7 9.7 %copy-start.6 = (f32[512]{0:T(512)S(1)}, f32[512]{0:T(512)}, u32[]{:S(2)}) copy-start(f32[512]{0:T(512)} %param.20) | copy-start | bytes 6148
  0.7 9.7 %copy-start.5 = (f32[512]{0:T(512)S(1)}, f32[512]{0:T(512)}, u32[]{:S(2)}) copy-start(f32[512]{0:T(512)} %param.19) | copy-start | bytes 6148
  0.7 9.7 %copy-start.4 = (bf16[64,512]{1,0:T(8,128)(2,1)S(1)}, bf16[64,512]{1,0:T(8,128)(2,1)}, u32[]{:S(2)}) copy-start(bf16[64,512]{1,0:T(8,128)(2,1)} %w_in_ref.1) | copy-start | bytes 196612
  3.7 16.1 %all-to-all-start = ((bf16[8,8,16,256]{3,2,1,0:T(8,128)(2,1)}), bf16[8,8,16,256]{3,2,1,0:T(8,128)(2,1)S(1)}, u32[]{:S(2)}, u32[]{:S(2)}) async-start(bf16[8,8,16,256]{3,2,1,0:T(8,128)(2,1)} %pack_state.1), calls=%async_computation | async-start | bytes 1048576 | tf_op jit(solution)/shard_map/all_to_all | solution.py:400
  10.5 1.4 %copy-start.2 = (bf16[8,384,256]{2,1,0:T(8,128)(2,1)S(1)}, bf16[8,384,256]{2,1,0:T(8,128)(2,1)}, u32[]{:S(2)}) copy-start(bf16[8,384,256]{2,1,0:T(8,128)(2,1)} %legendre_ref.1) | copy-start | bytes 4718596
  67.1 25.5 %copy-start = (f32[256,32,32]{0,2,1:T(8,128)S(1)}, f32[256,32,32]{0,2,1:T(8,128)}, u32[]{:S(2)}) copy-start(f32[256,32,32]{0,2,1:T(8,128)} %param.25) | copy-start | bytes 3145732

commit v2 on v1

--- a/solution.py
+++ b/solution.py
@@ -57,30 +57,54 @@
     return (lane >= waves_ref[first + j]).astype(F32)
 
 
-def pack_state(waves_ref, target_ref, state_hbm, send_ref, rows_ref, state_ref, sems):
+def fold(first, second, q, m, extra):
+    lane = lax.broadcasted_iota(jnp.int32, first.shape, 1)
+    turned = pltpu.roll(second, m, axis=1)
+    block = lax.broadcasted_iota(jnp.int32, extra.shape, 1)
+    extra = jnp.where(block == q, pltpu.roll(turned[:, 128:], q + 1, axis=1), extra)
+    return jnp.where(lane >= m, first, turned), extra
+
+
+def unfold(both, extra, q, m):
+    lane = lax.broadcasted_iota(jnp.int32, both.shape, 1)
+    block = lax.broadcasted_iota(jnp.int32, extra.shape, 1)
+    last = jnp.where(block == 127, pltpu.roll(extra, 127 - q, axis=1), both[:, 128:])
+    turned = jnp.concatenate([both[:, :128], last], axis=1)
+    turned = pltpu.roll(turned, (NTOT - m) & (NTOT - 1), axis=1)
+    return jnp.where(lane >= m, both, 0.0), jnp.where(lane >= NTOT - 1 - m, turned, 0.0)
+
+
+def pack_state(
+    waves_hbm, target_hbm, state_hbm, send_ref, rows_ref, state_ref, waves_ref, target_ref, sems, small_sems
+):
     copies = [
         pltpu.make_async_copy(state_hbm.at[j], state_ref.at[j], sems.at[j]) for j in range(SLOTS)
     ]
-    for copy in copies:
+    waves_copy = pltpu.make_async_copy(waves_hbm, waves_ref, small_sems.at[0])
+    target_copy = pltpu.make_async_copy(target_hbm, target_ref, small_sems.at[1])
+    for copy in (*copies, waves_copy, target_copy):
         copy.start()
+    target_copy.wait()
+    waves_copy.wait()
     first = lax.axis_index("wave") * SLOTS
-    lane = lax.broadcasted_iota(jnp.int32, (16, NTOT), 1)
-    row = lax.broadcasted_iota(jnp.int32, (16, NTOT), 0)
-    rider = jnp.zeros((16, NTOT), F32)
+    lane = lax.broadcasted_iota(jnp.int32, (16, 128), 1)
+    row = lax.broadcasted_iota(jnp.int32, (16, 128), 0)
+    rider = jnp.zeros((16, 128), F32)
     for i in range(ROWL):
-        rider = jnp.where((lane == 0) & (row == i), target_ref[i], rider)
-    for j in range(SLOTS):
-        live = live_row(waves_ref, first, j)
-        extra = None
-        if j < 2:
-            extra = rider * jnp.full((16, NTOT), waves_ref[first + j] > 127, jnp.int32).astype(F32)
-        copies[j].wait()
-        for e in range(LEVS):
-            for c in range(2):
-                for f in range(2):
-                    rows_ref[e, j, c * 8 + f * 4 : c * 8 + f * 4 + 4, :] = state_ref[j, c, e, f]
-            block = rows_ref[e, j] * live
-            send_ref[e, j] = (block if extra is None else block + extra).astype(BF16)
+        rider = jnp.where((lane == SLOTS // 2) & (row == i), target_ref[i], rider)
+    extra = jnp.concatenate([rider] * LEVS, axis=0)
+    for q in range(SLOTS // 2):
+        for j in (2 * q, 2 * q + 1):
+            copies[j].wait()
+            for e in range(LEVS):
+                for c in range(2):
+                    for f in range(2):
+                        at = c * 8 + f * 4
+                        rows_ref[j, e, at : at + 4, :] = state_ref[j, c, e, f]
+        flat = [rows_ref[j].reshape(LEVS * 16, NTOT) for j in (2 * q, 2 * q + 1)]
+        both, extra = fold(*flat, q, waves_ref[first + 2 * q], extra)
+        send_ref[:, :, q * NTOT : (q + 1) * NTOT] = both.astype(BF16).reshape(LEVS, 16, NTOT)
+    send_ref[:, :, 4 * NTOT :] = extra.astype(BF16).reshape(LEVS, 16, 128)
 
 
 def sine_of(q):
@@ -93,9 +117,9 @@
 
 
 def prepare(
-    lats_ref, weights_ref, lat_ref, weight_ref, waves_ref, legendre_ref, w_in_ref, b_in_ref, w_lat_ref, w_mid_ref,
+    lats_ref, weights_ref, lat_ref, weight_ref, waves_ref, legendre_hbm, w_in_ref, b_in_ref, w_lat_ref, w_mid_ref,
     b_mid_ref, band_ref, const_ref, cos_t_hbm, sin_t_hbm, cos_hbm, sin_hbm, first_hbm, mid_hbm, bias_hbm, scale_hbm,
-    hot_ref, cos_t_ref, sin_t_ref, cos_ref, sin_ref, first_ref, mid_ref, bias_ref, scale_ref, sems,
+    hot_ref, cos_t_ref, sin_t_ref, cos_ref, sin_ref, first_ref, mid_ref, bias_ref, scale_ref, legendre_ref, sems, in_sem,
 ):
     pairs = (
         (cos_t_ref, cos_t_hbm),
@@ -108,6 +132,8 @@
         (scale_ref, scale_hbm),
     )
     copies = [pltpu.make_async_copy(a, b, sems.at[i]) for i, (a, b) in enumerate(pairs)]
+    legendre_copy = pltpu.make_async_copy(legendre_hbm, legendre_ref, in_sem)
+    legendre_copy.start()
     x = lax.broadcasted_iota(jnp.int32, (NLON, MW), 0)
     product = (x * waves_ref[...]).astype(F32)
     phase = product - NLON * jnp.floor(product * (1.0 / NLON) + 0.5)
@@ -164,6 +190,7 @@
     row = lax.broadcasted_iota(jnp.int32, (16, NLAT), 0)
     both = jnp.where(row == 0, high.astype(F32), jnp.where(row == 1, low.astype(F32), 0.0))
     both = both.astype(BF16)
+    legendre_copy.wait()
     for j in range(SLOTS):
         block = legendre_ref[j]
         for parity in range(2):
@@ -181,21 +208,27 @@
 ):
     first = lax.axis_index("wave") * SLOTS
     both_ref[...] = jnp.zeros_like(both_ref)
-    target = jnp.zeros((LEVELS, 1), F32)
+    extra = recv_ref[:, :, 4 * NTOT :].astype(F32)
+    for src in range(LEVS):
+        at = src * ROWL
+        target_ref[at : at + ROWL, :] = jnp.broadcast_to(
+            extra[src, :ROWL, SLOTS // 2 : SLOTS // 2 + 1], (ROWL, 128)
+        )
+    extra = extra.reshape(LEVS * 16, 128)
     for j in range(SLOTS):
-        live = live_row(waves_ref, first, j)
         k = j % 2
+        q = j // 2
+        if k == 0:
+            both = recv_ref[:, :, q * NTOT : (q + 1) * NTOT].astype(F32).reshape(LEVS * 16, NTOT)
+            split = unfold(both, extra, q, waves_ref[first + j])
         for src in range(LEVS):
-            block = recv_ref[src, j].astype(F32)
+            block = split[k][src * 16 : (src + 1) * 16]
             for c in range(2):
                 for f in range(2):
                     at = f * LEVELS + src * ROWL
                     rows_ref[k, c, at : at + 4, :] = block[c * 8 + f * 4 : c * 8 + f * 4 + 4, :]
         for c in range(2):
-            if j < 2 and c == 0:
-                here = jnp.full((LEVELS, 1), waves_ref[first + j] > 127, jnp.int32).astype(F32)
-                target = target + here * rows_ref[k, 0, :LEVELS, :1]
-            part = (rows_ref[k, c] * live).astype(BF16)
+            part = rows_ref[k, c].astype(BF16)
             state_ref[j, c] = part
             both_ref[k, c * 128 : c * 128 + 64, :NTOT] = part
             both_ref[k, c * 128 + 64 : c * 128 + 128, NTOT:] = part
@@ -207,7 +240,6 @@
                 total_ref[c * PAIRS + p, pl.ds(j, WAVES, stride=SLOTS), :] = sums[
                     p * WAVES : (p + 1) * WAVES, c * 128 : (c + 1) * 128
                 ]
-    target_ref[...] = jnp.broadcast_to(target, (LEVELS, 128))
     for i in range(2 * PAIRS):
         fourier_ref[:, i * 128 : (i + 1) * 128] = total_ref[i].astype(BF16)
 
@@ -216,16 +248,13 @@
     return (u + u * jnp.tanh(u)).astype(BF16)
 
 
-TILE = 256
-
-
 def dot_lanes(a, b):
     return lax.dot_general(a, b, (((1,), (1,)), ((), ())), preferred_element_type=F32)
 
 
 def columns(
     coef_ref, cos_t_hbm, sin_t_hbm, first_hbm, bias_hbm, mid_hbm, last_hbm, cos_hbm, sin_hbm, scale_hbm,
-    tendw_ref, grid_hbm, values_ref, grid_ref,
+    tendw_ref, grid_hbm, values_ref, grid_ref, hidden_ref,
     cos_t_ref, sin_t_ref, first_ref, bias_ref, mid_ref, last_ref, cos_ref, sin_ref, scale_ref, sems, grid_sems,
 ):
     pairs = (
@@ -257,30 +286,14 @@
     for copy in copies[2:6]:
         copy.wait()
 
-    def pair(p, carry):
-        for tile in range(NLON // TILE):
-            rows = slice(tile * TILE, (tile + 1) * TILE)
-            v = values_ref[p, rows, :]
-            hidden = [
-                half_silu(
-                    jnp.dot(v, first_ref[q], preferred_element_type=F32)
-                    + bias_ref[pl.ds(2 * p + q, 1), :]
-                )
-                for q in range(2)
-            ]
-            hidden = [
-                half_silu(
-                    jnp.dot(h, mid_ref[...], preferred_element_type=F32)
-                    + bias_ref[BAND : BAND + 1, :]
-                )
-                for h in hidden
-            ]
-            for q in range(2):
-                grid_ref[2 * p + q, :, rows] = dot_lanes(last_ref[...], hidden[q]).astype(BF16)
+    for p in range(PAIRS):
+        for q in range(2):
+            hidden = jnp.dot(values_ref[p], first_ref[q], preferred_element_type=F32)
+            hidden_ref[q, 0] = half_silu(hidden + bias_ref[2 * p + q : 2 * p + q + 1, :])
+            hidden = jnp.dot(hidden_ref[q, 0], mid_ref[...], preferred_element_type=F32)
+            hidden_ref[q, 1] = half_silu(hidden + bias_ref[BAND : BAND + 1, :])
+            grid_ref[2 * p + q] = dot_lanes(last_ref[...], hidden_ref[q, 1]).astype(BF16)
         grid_copy(p).start()
-        return carry
-
-    lax.fori_loop(0, PAIRS, pair, 0)
     for copy in copies[6:]:
         copy.wait()
     tend = grid_ref[...].reshape(half, NLON)
@@ -293,13 +306,11 @@
 
 def to_spectral(
     waves_ref, recv_ref, band_ref, state_ref, const_ref, weight_ref, target_ref, coupling_ref,
-    send_ref, wide_ref, temp_ref, rows_ref, matrix_ref,
+    send_ref, wide_ref, temp_ref, rows_ref,
 ):
     first = lax.axis_index("wave") * SLOTS
     for i in range(2 * PAIRS):
         wide_ref[i] = recv_ref[:, i * 128 : (i + 1) * 128].astype(F32)
-    for i in range(2):
-        matrix_ref[i] = coupling_ref[:, i * 128 : (i + 1) * 128]
     target = target_ref[:, :1]
     weight_total = jnp.sum(weight_ref[...], axis=1, keepdims=True)
     degree = lax.broadcasted_iota(jnp.int32, (1, NTOT), 1)
@@ -338,34 +349,46 @@
             temp_ref[j * 2 + c] = (old_temp + time_step * temp) * live
             hum = (old_hum + time_step * hum) * (live * shrink)
             for d in range(LEVS):
-                rows_ref[d, j, c * 8 + 4 : c * 8 + 8, :] = hum[d * 4 : d * 4 + 4]
+                rows_ref[j, d, c * 8 + 4 : c * 8 + 8, :] = hum[d * 4 : d * 4 + 4]
     group = 4
     for g in range(2 * SLOTS // group):
-
-        def step(k, totals):
-            matrix = jnp.concatenate(
-                [matrix_ref[i, pl.ds(k, LEVELS, stride=LEVELS), :] for i in range(2)], axis=1
-            )
-            return tuple(
-                totals[q] + matrix * temp_ref[g * group + q, pl.ds(k, 1), :] for q in range(group)
-            )
-
-        zero = jnp.zeros((LEVELS, NTOT), F32)
-        totals = lax.fori_loop(0, LEVELS, step, (zero,) * group, unroll=4)
-        for q in range(group):
-            j, c = divmod(g * group + q, 2)
-            for d in range(LEVS):
-                rows_ref[d, j, c * 8 : c * 8 + 4, :] = totals[q][d * 4 : d * 4 + 4]
-    send_ref[...] = rows_ref[...].astype(BF16)
-
-
-def unpack_state(recv_ref, state_ref):
-    for e in range(LEVS):
-        for j in range(SLOTS):
-            block = recv_ref[e, j].astype(F32)
-            for c in range(2):
-                for f in range(2):
-                    state_ref[j, c, e, f] = block[c * 8 + f * 4 : c * 8 + f * 4 + 4, :]
+        for half in range(2):
+            lanes = slice(half * 128, (half + 1) * 128)
+            temps = [temp_ref[g * group + i, :, lanes] for i in range(group)]
+            for level in range(LEVELS):
+                matrix = coupling_ref[level * LEVELS : (level + 1) * LEVELS, lanes]
+                for i in range(group):
+                    j, c = divmod(g * group + i, 2)
+                    at = c * 8 + level % ROWL
+                    rows_ref[j, level // ROWL, at : at + 1, lanes] = jnp.sum(
+                        matrix * temps[i], axis=0, keepdims=True
+                    )
+    extra = jnp.zeros((LEVS * 16, 128), F32)
+    for q in range(SLOTS // 2):
+        flat = [rows_ref[j].reshape(LEVS * 16, NTOT) for j in (2 * q, 2 * q + 1)]
+        both, extra = fold(*flat, q, waves_ref[first + 2 * q], extra)
+        send_ref[:, :, q * NTOT : (q + 1) * NTOT] = both.astype(BF16).reshape(LEVS, 16, NTOT)
+    send_ref[:, :, 4 * NTOT :] = extra.astype(BF16).reshape(LEVS, 16, 128)
+
+
+def unpack_state(waves_ref, recv_ref, state_hbm, state_ref, sems):
+    copies = [
+        pltpu.make_async_copy(state_ref.at[j], state_hbm.at[j], sems.at[j]) for j in range(SLOTS)
+    ]
+    first = lax.axis_index("wave") * SLOTS
+    extra = recv_ref[:, :, 4 * NTOT :].astype(F32).reshape(LEVS * 16, 128)
+    for q in range(SLOTS // 2):
+        both = recv_ref[:, :, q * NTOT : (q + 1) * NTOT].astype(F32).reshape(LEVS * 16, NTOT)
+        split = unfold(both, extra, q, waves_ref[first + 2 * q])
+        for k in range(2):
+            for e in range(LEVS):
+                for c in range(2):
+                    for f in range(2):
+                        at = e * 16 + c * 8 + f * 4
+                        state_ref[2 * q + k, c, e, f] = split[k][at : at + 4, :]
+            copies[2 * q + k].start()
+    for copy in copies:
+        copy.wait()
 
 
 def per_device(
@@ -383,18 +406,22 @@
     target,
     coupling,
 ):
-    message = (LEVS, SLOTS, 16, NTOT)
+    message = (LEVS, 16, SLOTS // 2 * NTOT + 128)
+    rows = (SLOTS, LEVS, 16, NTOT)
     sent = call(
         pack_state,
         out(message, BF16),
         [
-            pltpu.VMEM(message, F32),
+            pltpu.VMEM(rows, F32),
             pltpu.VMEM(state.shape, F32),
+            pltpu.SMEM((MW,), jnp.int32),
+            pltpu.SMEM((ROWL,), F32),
             pltpu.SemaphoreType.DMA((SLOTS,)),
+            pltpu.SemaphoreType.DMA((2,)),
         ],
         10**8,
         (wave_table, target, state),
-        [SMEM] * 2 + [HBM],
+        [HBM] * 3,
         "pack_state",
     )
     members = lax.all_to_all(sent, "lev", 0, 0, tiled=True)
@@ -419,7 +446,9 @@
         [
             pltpu.VMEM((NLAT // 128, NLAT, 128), F32),
             *(pltpu.VMEM(*m) for m in made),
+            pltpu.VMEM(legendre.shape, BF16),
             pltpu.SemaphoreType.DMA((len(made),)),
+            pltpu.SemaphoreType.DMA,
         ],
         6 * 10**9,
         (
@@ -435,7 +464,7 @@
             w_mid,
             b_mid[None],
         ),
-        [SMEM] * 2 + [VMEM] * 9,
+        [SMEM] * 2 + [VMEM] * 3 + [HBM] + [VMEM] * 5,
         "prepare",
     )
     fourier, state_bf, target_all = call(
@@ -465,6 +494,7 @@
         [
             pltpu.VMEM((PAIRS, NLON, 128), BF16),
             pltpu.VMEM((BAND, FEAT, NLON), BF16),
+            pltpu.VMEM((2, 2, NLON, HID), BF16),
             *(pltpu.VMEM(v.shape, v.dtype) for v in (cos_t, sin_t, first, bias, mid, w_out.T, cos, sin, scale)),
             pltpu.SemaphoreType.DMA((9,)),
             pltpu.SemaphoreType.DMA((PAIRS,)),
@@ -481,8 +511,7 @@
         [
             pltpu.VMEM((2 * PAIRS, MW, 128), F32),
             pltpu.VMEM((2 * SLOTS, LEVELS, NTOT), F32),
-            pltpu.VMEM(message, F32),
-            pltpu.VMEM((2, LEVELS * LEVELS, 128), F32),
+            pltpu.VMEM(rows, F32),
         ],
         10**9,
         (
@@ -501,11 +530,11 @@
     returned = lax.all_to_all(moved, "lev", 0, 0, tiled=True)
     new_state = call(
         unpack_state,
-        out(state.shape, F32),
-        [],
+        pltpu.HBM(state.shape, F32),
+        [pltpu.VMEM(state.shape, F32), pltpu.SemaphoreType.DMA((SLOTS,))],
         10**8,
-        (returned,),
-        [VMEM],
+        (wave_table, returned),
+        [SMEM, VMEM],
         "unpack_state",
     )
     return new_state, jnp.transpose(grid, (1, 0, 2))[None]

time: 117 us -> 109 us (0.932)
  Pallas kernels: 31.1 us -> 28.4 us
  waiting for transfers between devices: 3.56 us -> 1.26 us
  local copies, waits for them, and re-layouts: 1.45 us -> 0.05 us
  blocking collectives: 72.6 us -> 71.2 us
    pallas_call x6, Pallas kernels: 31.1 us -> 28.4 us  [call(): pl.pallas_call(body, out_shape=outs, in_specs=specs, out_specs=jax.tree.m...]
    all_to_all x1, waiting for transfers between devices: 3.56 us -> 1.26 us  [per_device(): members = lax.all_to_all(sent, 'lev', 0, 0, tiled=True)]
    all_to_all x1, blocking collectives: 15.9 us -> 14.2 us  [per_device(): returned = lax.all_to_all(moved, 'lev', 0, 0, tiled=True)]
    unnamed x20 -> x18, local copies, waits for them, and re-layouts: 1.45 us -> 0.05 us
  transfers between devices with their start and end apart: 1 -> 1, of which waited for: 1 -> 1; matrix products, arithmetic and copies ran while one was open for 0% -> 0% of each run, Pallas kernels for 4% -> 5%
where the time goes in v2:
time: 109 us
  blocking collectives  71.2 us (65%)
  Pallas kernels  28.4 us (26%)
  starting transfers between devices  6.58 us (6%)
  waiting for transfers between devices  1.26 us (1%)
    all_to_all x1, blocking collectives, per_device(): coef = lax.all_to_all(fourier, 'wave', 0, 0, tiled=True)  31.3 us
    pallas_call x6, Pallas kernels, call(): pl.pallas_call(body, out_shape=outs, in_specs=specs, out_specs=jax.tree.m...  28.4 us
    all_to_all x1, blocking collectives, per_device(): back = lax.all_to_all(tendw, 'wave', 0, 0, tiled=True)  25.8 us
    all_to_all x1, blocking collectives, per_device(): returned = lax.all_to_all(moved, 'lev', 0, 0, tiled=True)  14.2 us
    all_to_all x1, starting transfers between devices, per_device(): members = lax.all_to_all(sent, 'lev', 0, 0, tiled=True)  6.58 us
  transfers between devices with their start and end apart: 1, of which 1 were waited for; matrix products, arithmetic and copies ran while one was open for 0% of the time, Pallas kernels for 5%

profile of v2, /device:TPU:1, one launch (start us, length us, event | category | flops | bytes accessed | tf_op | source)
XLA Modules:
  0.0 108.5 jit_solution(16991802873473981067)
XLA Ops:
  0.6 0.0 copy-start.1
  0.6 0.0 copy-start.8
  0.7 0.0 copy-start.7
  0.7 0.0 copy-start.6
  0.7 0.0 copy-start.2
  0.7 0.0 copy-start.5
  0.7 0.0 copy-start.4
  0.7 0.0 copy-start.3
  0.7 2.6 %pack_state.1 = bf16[8,16,1152]{2,1,0:T(8,128)(2,1)} custom-call(s32[256]{0:T(256)} %waves_ref.5, f32[4]{0:T(128)} %target_hbm.1, f32[8,2,8,2,4,256]{5,4,3,2,1,0:T(4,128)} %state_hbm.1), custom_call_target="tpu_custom_call" | custom-call | flops 100000000 | bytes 2000000 | tf_op jit(solution)/shard_map/pack_state/pallas_call | solution.py:39
  3.4 6.6 %all-to-all-start = ((bf16[8,16,1152]{2,1,0:T(8,128)(2,1)}), bf16[8,16,1152]{2,1,0:T(8,128)(2,1)S(1)}, u32[]{:S(2)}, u32[]{:S(2)}) async-start(bf16[8,16,1152]{2,1,0:T(8,128)(2,1)} %pack_state.1), calls=%async_computation | async-start | bytes 589824 | tf_op jit(solution)/shard_map/all_to_all | solution.py:427
  9.9 0.0 copy-done.8
  9.9 0.0 copy-done.7
  10.0 0.0 copy-done.1
  10.0 0.0 copy-done.6
  10.0 0.0 copy-done.2
  10.0 0.0 copy-done.5
  10.0 0.0 copy-done.4
  10.0 0.0 copy-done.3
  10.0 5.5 %prepare.1 = (bf16[8,192,512]{2,1,0:T(8,128)(2,1)S(1)}, f32[8,256]{1,0:T(8,128)S(1)}, bf16[768,256]{1,0:T(8,128)(2,1)}, bf16[768,256]{1,0:T(8,128)(2,1)}, bf16[2...) custom-call(s32[384]{0:T(512)} %lats_ref.1, ...), custom_call_target="tpu_custom_call" | custom-call | flops 6000000000 | bytes 2000000 | tf_op jit(solution)/shard_map/prepare/pallas_call | solution.py:39
  15.5 1.3 %all-to-all-done.recv_ref = bf16[8,16,1152]{2,1,0:T(8,128)(2,1)S(1)} async-done(((bf16[8,16,1152]{2,1,0:T(8,128)(2,1)}), bf16[8,16,1152]{2,1,0:T(8,128)(2,1)S(1)}, u32[]{:S(2)}, u32[]{:S(2)}) %all-to-all-start) | async-done | bytes 294944 | tf_op jit(solution)/shard_map/all_to_all | solution.py:427
  16.8 1.7 %to_fourier.1 = (bf16[256,1536]{1,0:T(8,128)(2,1)S(1)}, bf16[8,2,64,256]{3,2,1,0:T(8,128)(2,1)S(1)}, f32[32,128]{1,0:T(8,128)S(1)}) custom-call(s32[256]{0:T(256)} %waves_ref.5, bf16[8,16,1152]{2,1,0:T(8,128)(2,1)S(1)} %all-to-all-done.recv_ref, bf16[8,192,512]{2,1,0:T(8,128)(2,1)S(1)} %get-tuple-element.17.band_ref), custom_call_target="tpu_custom_call" | custom-call | flops 1000000000 | bytes 2000000 | tf_op jit(solution)/shard_map/to_fourier/pallas_call | solution.py:39
  18.5 31.3 %all_to_all.32 = bf16[32,8,1536]{2,1,0:T(8,128)(2,1)S(1)} all-to-all(bf16[32,8,1536]{2,1,0:T(8,128)(2,1)S(1)} %bitcast.19), channel_id=1, replica_groups=mesh['lev'=8,'wave'=32] {'wave'}, dimensions={0} | all-to-all | bytes 1572864 | tf_op jit(solution)/shard_map/all_to_all | solution.py:487
  49.8 13.1 %columns.1 = (bf16[256,1536]{1,0:T(8,128)(2,1)S(1)}, bf16[12,64,768]{2,1,0:T(8,128)(2,1)}) custom-call(bf16[256,1536]{1,0:T(8,128)(2,1)S(1)} %bitcast.17, bf16[768,256]{1,0:T(8,128)(2,1)} %get-tuple-element.19.cos_t_hbm, bf16[768,256]{1,0:T(8,128)(2,1)} %get-tuple-element.20.sin_t_hbm, bf16[2,128,512]{2,1,0:T(8,128)(2,1)} %get-tuple-element.21.first_hbm, ...), custom_call_target="tpu_custom_call" | custom-call | flops 10000000000 | bytes 2000000 | tf_op jit(solution)/shard_map/columns/pallas_call | solution.py:39
  62.8 0.0 copy-start
  62.8 25.8 %all_to_all.33 = bf16[32,8,1536]{2,1,0:T(8,128)(2,1)S(1)} all-to-all(bf16[32,8,1536]{2,1,0:T(8,128)(2,1)S(1)} %bitcast.18), channel_id=1, replica_groups=mesh['lev'=8,'wave'=32] {'wave'}, dimensions={0} | all-to-all | bytes 1572864 | tf_op jit(solution)/shard_map/all_to_all | solution.py:507
  88.6 0.0 copy-done
  88.6 3.7 %to_spectral.1 = bf16[8,16,1152]{2,1,0:T(8,128)(2,1)S(1)} custom-call(s32[256]{0:T(256)} %waves_ref.5, bf16[256,1536]{1,0:T(8,128)(2,1)S(1)} %bitcast.15, bf16[8,192,512]{2,1,0:T(8,128)(2,1)S(1)} %get-tuple-element.17.band_ref, bf16[8,2,64,256]{3,2,1,0:T(8,128)(2,1)S(1)} %get-tuple-element.28.state_ref, f32[8,256]{1,0:T(8,128)S(1)} %get-tuple-element.29.const_ref, ...), custom_call_target="tpu_custom_call" | custom-call | flops 1000000000 | bytes 2000000 | tf_op jit(solution)/shard_map/to_spectral/pallas_call | solution.py:39
  92.3 14.2 %all_to_all.34.recv_ref = bf16[8,16,1152]{2,1,0:T(8,128)(2,1)S(1)} all-to-all(bf16[8,16,1152]{2,1,0:T(8,128)(2,1)S(1)} %to_spectral.1), channel_id=1, replica_groups=mesh['lev'=8,'wave'=32] {'lev'}, dimensions={0} | all-to-all | bytes 589824 | tf_op jit(solution)/shard_map/all_to_all | solution.py:530
  106.5 1.8 %unpack_state.1 = f32[8,2,8,2,4,256]{5,4,3,2,1,0:T(4,128)} custom-call(s32[256]{0:T(256)} %waves_ref.5, bf16[8,16,1152]{2,1,0:T(8,128)(2,1)S(1)} %all_to_all.34.recv_ref), custom_call_target="tpu_custom_call" | custom-call | flops 100000000 | bytes 2000000 | tf_op jit(solution)/shard_map/unpack_state/pallas_call | solution.py:39
  (2 shorter events, 0.0 us)
Async XLA Ops:
  0.6 9.3 %copy-start.1 = (s32[256]{0:T(256)S(1)}, s32[256]{0:T(256)}, u32[]{:S(2)}) copy-start(s32[256]{0:T(256)} %waves_ref.5) | copy-start | bytes 3076
  0.6 9.3 %copy-start.8 = (f32[384]{0:T(512)S(1)}, f32[384]{0:T(512)}, u32[]{:S(2)}) copy-start(f32[384]{0:T(512)} %weights_ref.1) | copy-start | bytes 4612
  0.7 9.3 %copy-start.7 = (s32[384]{0:T(512)S(1)}, s32[384]{0:T(512)}, u32[]{:S(2)}) copy-start(s32[384]{0:T(512)} %lats_ref.1) | copy-start | bytes 4612
  0.7 9.3 %copy-start.6 = (f32[512]{0:T(512)S(1)}, f32[512]{0:T(512)}, u32[]{:S(2)}) copy-start(f32[512]{0:T(512)} %param.22) | copy-start | bytes 6148
  0.7 9.3 %copy-start.2 = (bf16[512,512]{1,0:T(8,128)(2,1)S(1)}, bf16[512,512]{1,0:T(8,128)(2,1)}, u32[]{:S(2)}) copy-start(bf16[512,512]{1,0:T(8,128)(2,1)} %w_mid_ref.1) | copy-start | bytes 1572868
  0.7 9.3 %copy-start.5 = (f32[512]{0:T(512)S(1)}, f32[512]{0:T(512)}, u32[]{:S(2)}) copy-start(f32[512]{0:T(512)} %param.20) | copy-start | bytes 6148
  0.7 9.3 %copy-start.4 = (f32[512]{0:T(512)S(1)}, f32[512]{0:T(512)}, u32[]{:S(2)}) copy-start(f32[512]{0:T(512)} %param.19) | copy-start | bytes 6148
  0.7 9.3 %copy-start.3 = (bf16[64,512]{1,0:T(8,128)(2,1)S(1)}, bf16[64,512]{1,0:T(8,128)(2,1)}, u32[]{:S(2)}) copy-start(bf16[64,512]{1,0:T(8,128)(2,1)} %w_in_ref.1) | copy-start | bytes 196612
  3.4 13.4 %all-to-all-start = ((bf16[8,16,1152]{2,1,0:T(8,128)(2,1)}), bf16[8,16,1152]{2,1,0:T(8,128)(2,1)S(1)}, u32[]{:S(2)}, u32[]{:S(2)}) async-start(bf16[8,16,1152]{2,1,0:T(8,128)(2,1)} %pack_state.1), calls=%async_computation | async-start | bytes 589824 | tf_op jit(solution)/shard_map/all_to_all | solution.py:427
  62.8 25.8 %copy-start = (f32[256,32,32]{0,2,1:T(8,128)S(1)}, f32[256,32,32]{0,2,1:T(8,128)}, u32[]{:S(2)}) copy-start(f32[256,32,32]{0,2,1:T(8,128)} %param.25) | copy-start | bytes 3145732

commit v3 on v2

--- a/solution.py
+++ b/solution.py
@@ -253,38 +253,19 @@
 
 
 def columns(
-    coef_ref, cos_t_hbm, sin_t_hbm, first_hbm, bias_hbm, mid_hbm, last_hbm, cos_hbm, sin_hbm, scale_hbm,
+    coef_ref, cos_t_ref, sin_t_ref, first_ref, bias_ref, mid_ref, last_ref, cos_ref, sin_ref, scale_ref,
     tendw_ref, grid_hbm, values_ref, grid_ref, hidden_ref,
-    cos_t_ref, sin_t_ref, first_ref, bias_ref, mid_ref, last_ref, cos_ref, sin_ref, scale_ref, sems, grid_sems,
+    grid_sems,
 ):
-    pairs = (
-        (cos_t_hbm, cos_t_ref),
-        (sin_t_hbm, sin_t_ref),
-        (first_hbm, first_ref),
-        (bias_hbm, bias_ref),
-        (mid_hbm, mid_ref),
-        (last_hbm, last_ref),
-        (cos_hbm, cos_ref),
-        (sin_hbm, sin_ref),
-        (scale_hbm, scale_ref),
-    )
-    copies = [pltpu.make_async_copy(a, b, sems.at[i]) for i, (a, b) in enumerate(pairs)]
-    for copy in copies:
-        copy.start()
-
     def grid_copy(p):
         rows = pl.ds(2 * p, 2)
         return pltpu.make_async_copy(grid_ref.at[rows], grid_hbm.at[rows], grid_sems.at[p])
 
     half = BAND * FEAT
-    copies[0].wait()
-    copies[1].wait()
     values = jnp.dot(cos_t_ref[...], coef_ref[:, :half], preferred_element_type=F32)
     values += jnp.dot(sin_t_ref[...], coef_ref[:, half:], preferred_element_type=F32)
     for p in range(PAIRS):
         values_ref[p] = values[:, p * 128 : (p + 1) * 128].astype(BF16)
-    for copy in copies[2:6]:
-        copy.wait()
 
     for p in range(PAIRS):
         for q in range(2):
@@ -294,8 +275,6 @@
             hidden_ref[q, 1] = half_silu(hidden + bias_ref[BAND : BAND + 1, :])
             grid_ref[2 * p + q] = dot_lanes(last_ref[...], hidden_ref[q, 1]).astype(BF16)
         grid_copy(p).start()
-    for copy in copies[6:]:
-        copy.wait()
     tend = grid_ref[...].reshape(half, NLON)
     scale = scale_ref[...]
     for c, table in enumerate((cos_ref, sin_ref)):
@@ -495,13 +474,11 @@
             pltpu.VMEM((PAIRS, NLON, 128), BF16),
             pltpu.VMEM((BAND, FEAT, NLON), BF16),
             pltpu.VMEM((2, 2, NLON, HID), BF16),
-            *(pltpu.VMEM(v.shape, v.dtype) for v in (cos_t, sin_t, first, bias, mid, w_out.T, cos, sin, scale)),
-            pltpu.SemaphoreType.DMA((9,)),
             pltpu.SemaphoreType.DMA((PAIRS,)),
         ],
         10**10,
         (coef, cos_t, sin_t, first, bias, mid, w_out.T, cos, sin, scale),
-        [VMEM] + [HBM] * 9,
+        [VMEM] * 10,
         "columns",
     )
     back = lax.all_to_all(tendw, "wave", 0, 0, tiled=True)

time: 109 us -> 108 us (level)
  Pallas kernels: 28.4 us -> 26.8 us
    pallas_call x6, Pallas kernels: 28.4 us -> 26.8 us  [call(): pl.pallas_call(body, out_shape=outs, in_specs=specs, out_specs=jax.tree.m...]
where the time goes in v3:
time: 108 us; the launch traced here: 107 us
  blocking collectives  71.4 us (66%)
  Pallas kernels  26.8 us (25%)
  starting transfers between devices  6.58 us (6%)
  waiting for transfers between devices  1.28 us (1%)
  between operations  1.09 us (1%)
    all_to_all x1, blocking collectives, per_device(): coef = lax.all_to_all(fourier, 'wave', 0, 0, tiled=True)  31.4 us
    pallas_call x6, Pallas kernels, call(): pl.pallas_call(body, out_shape=outs, in_specs=specs, out_specs=jax.tree.m...  26.8 us
    all_to_all x1, blocking collectives, per_device(): back = lax.all_to_all(tendw, 'wave', 0, 0, tiled=True)  25.8 us
    all_to_all x1, blocking collectives, per_device(): returned = lax.all_to_all(moved, 'lev', 0, 0, tiled=True)  14.2 us
    all_to_all x1, starting transfers between devices, per_device(): members = lax.all_to_all(sent, 'lev', 0, 0, tiled=True)  6.58 us
  transfers between devices with their start and end apart: 1, of which 1 were waited for; matrix products, arithmetic and copies ran while one was open for 0% of the time, Pallas kernels for 5%

profile of v3, /device:TPU:1, one launch (start us, length us, event | category | flops | bytes accessed | tf_op | source)
XLA Modules:
  0.0 107.2 jit_solution(14729770667576869549)
XLA Ops:
  0.6 0.0 copy-start.1
  0.6 0.0 copy-start.17
  0.7 0.0 copy-start.16
  0.7 0.0 copy-start.7
  0.7 0.0 copy-start.2
  0.7 0.0 copy-start.6
  0.7 0.0 copy-start.5
  0.7 0.0 copy-start.3
  0.7 2.6 %pack_state.1 = bf16[8,16,1152]{2,1,0:T(8,128)(2,1)} custom-call(s32[256]{0:T(256)} %waves_ref.5, f32[4]{0:T(128)} %target_hbm.1, f32[8,2,8,2,4,256]{5,4,3,2,1,0:T(4,128)} %state_hbm.1), custom_call_target="tpu_custom_call" | custom-call | flops 100000000 | bytes 2000000 | tf_op jit(solution)/shard_map/pack_state/pallas_call | solution.py:39
  3.4 6.6 %all-to-all-start = ((bf16[8,16,1152]{2,1,0:T(8,128)(2,1)}), bf16[8,16,1152]{2,1,0:T(8,128)(2,1)S(1)}, u32[]{:S(2)}, u32[]{:S(2)}) async-start(bf16[8,16,1152]{2,1,0:T(8,128)(2,1)} %pack_state.1), calls=%async_computation | async-start | bytes 589824 | tf_op jit(solution)/shard_map/all_to_all | solution.py:406
  9.9 0.0 copy-done.17
  9.9 0.0 copy-done.16
  10.0 0.0 copy-done.1
  10.0 0.0 copy-done.7
  10.0 0.0 copy-done.2
  10.0 0.0 copy-done.6
  10.0 0.0 copy-done.5
  10.0 0.0 copy-done.3
  10.0 5.5 %prepare.1 = (bf16[8,192,512]{2,1,0:T(8,128)(2,1)S(1)}, f32[8,256]{1,0:T(8,128)S(1)}, bf16[768,256]{1,0:T(8,128)(2,1)}, bf16[768,256]{1,0:T(8,128)(2,1)}, bf16[2...) custom-call(s32[384]{0:T(512)} %lats_ref.1, ...), custom_call_target="tpu_custom_call" | custom-call | flops 6000000000 | bytes 2000000 | tf_op jit(solution)/shard_map/prepare/pallas_call | solution.py:39
  15.5 1.3 %all-to-all-done.recv_ref = bf16[8,16,1152]{2,1,0:T(8,128)(2,1)S(1)} async-done(((bf16[8,16,1152]{2,1,0:T(8,128)(2,1)}), bf16[8,16,1152]{2,1,0:T(8,128)(2,1)S(1)}, u32[]{:S(2)}, u32[]{:S(2)}) %all-to-all-start) | async-done | bytes 294944 | tf_op jit(solution)/shard_map/all_to_all | solution.py:406
  16.8 0.0 copy-start.11
  16.8 0.0 copy-start.12
  16.8 0.0 copy-start.13
  16.8 1.9 %to_fourier.1 = (bf16[256,1536]{1,0:T(8,128)(2,1)S(1)}, bf16[8,2,64,256]{3,2,1,0:T(8,128)(2,1)S(1)}, f32[32,128]{1,0:T(8,128)S(1)}) custom-call(s32[256]{0:T(256)} %waves_ref.5, bf16[8,16,1152]{2,1,0:T(8,128)(2,1)S(1)} %all-to-all-done.recv_ref, bf16[8,192,512]{2,1,0:T(8,128)(2,1)S(1)} %get-tuple-element.17.band_ref), custom_call_target="tpu_custom_call" | custom-call | flops 1000000000 | bytes 2000000 | tf_op jit(solution)/shard_map/to_fourier/pallas_call | solution.py:39
  18.6 0.0 copy-start.4
  18.6 0.0 copy-start.8
  18.7 0.0 copy-start.9
  18.7 0.0 copy-start.10
  18.7 0.0 copy-start.14
  18.7 0.0 copy-start.15
  18.7 31.4 %all_to_all.32 = bf16[32,8,1536]{2,1,0:T(8,128)(2,1)S(1)} all-to-all(bf16[32,8,1536]{2,1,0:T(8,128)(2,1)S(1)} %bitcast.19), channel_id=1, replica_groups=mesh['lev'=8,'wave'=32] {'wave'}, dimensions={0} | all-to-all | bytes 1572864 | tf_op jit(solution)/shard_map/all_to_all | solution.py:466
  50.1 0.0 copy-done.11
  50.1 0.0 copy-done.12
  50.1 0.0 copy-done.13
  50.1 0.0 copy-done.4
  50.1 0.0 copy-done.8
  50.1 0.0 copy-done.9
  50.1 0.0 copy-done.10
  50.1 0.0 copy-done.14
  50.2 0.0 copy-done.15
  50.2 11.3 %columns.1 = (bf16[256,1536]{1,0:T(8,128)(2,1)S(1)}, bf16[12,64,768]{2,1,0:T(8,128)(2,1)}) custom-call(bf16[256,1536]{1,0:T(8,128)(2,1)S(1)} %bitcast.17, bf16[768,256]{1,0:T(8,128)(2,1)S(1)} %copy-done.9, bf16[768,256]{1,0:T(8,128)(2,1)S(1)} %copy-done.10, bf16[2,128,512]{2,1,0:T(8,128)(2,1)S(1)} %copy-done.13, f32[16,512]{1,0:T(8,128)S(1)} %copy-done.14, ...), custom_call_target="tpu_custom_call" | custom-call | flops 10000000000 | bytes 2000000 | tf_op jit(solution)/shard_map/columns/pallas_call | solution.py:39
  61.5 0.0 copy-start
  61.5 25.8 %all_to_all.33 = bf16[32,8,1536]{2,1,0:T(8,128)(2,1)S(1)} all-to-all(bf16[32,8,1536]{2,1,0:T(8,128)(2,1)S(1)} %bitcast.18), channel_id=1, replica_groups=mesh['lev'=8,'wave'=32] {'wave'}, dimensions={0} | all-to-all | bytes 1572864 | tf_op jit(solution)/shard_map/all_to_all | solution.py:484
  87.3 0.0 copy-done
  87.3 3.7 %to_spectral.1 = bf16[8,16,1152]{2,1,0:T(8,128)(2,1)S(1)} custom-call(s32[256]{0:T(256)} %waves_ref.5, bf16[256,1536]{1,0:T(8,128)(2,1)S(1)} %bitcast.15, bf16[8,192,512]{2,1,0:T(8,128)(2,1)S(1)} %get-tuple-element.17.band_ref, bf16[8,2,64,256]{3,2,1,0:T(8,128)(2,1)S(1)} %get-tuple-element.28.state_ref, f32[8,256]{1,0:T(8,128)S(1)} %get-tuple-element.29.const_ref, ...), custom_call_target="tpu_custom_call" | custom-call | flops 1000000000 | bytes 2000000 | tf_op jit(solution)/shard_map/to_spectral/pallas_call | solution.py:39
  91.0 14.2 %all_to_all.34.recv_ref = bf16[8,16,1152]{2,1,0:T(8,128)(2,1)S(1)} all-to-all(bf16[8,16,1152]{2,1,0:T(8,128)(2,1)S(1)} %to_spectral.1), channel_id=1, replica_groups=mesh['lev'=8,'wave'=32] {'lev'}, dimensions={0} | all-to-all | bytes 589824 | tf_op jit(solution)/shard_map/all_to_all | solution.py:507
  105.2 1.8 %unpack_state.1 = f32[8,2,8,2,4,256]{5,4,3,2,1,0:T(4,128)} custom-call(s32[256]{0:T(256)} %waves_ref.5, bf16[8,16,1152]{2,1,0:T(8,128)(2,1)S(1)} %all_to_all.34.recv_ref), custom_call_target="tpu_custom_call" | custom-call | flops 100000000 | bytes 2000000 | tf_op jit(solution)/shard_map/unpack_state/pallas_call | solution.py:39
  (2 shorter events, 0.0 us)
Async XLA Ops:
  0.6 9.3 %copy-start.1 = (s32[256]{0:T(256)S(1)}, s32[256]{0:T(256)}, u32[]{:S(2)}) copy-start(s32[256]{0:T(256)} %waves_ref.5) | copy-start | bytes 3076
  0.6 9.3 %copy-start.17 = (f32[384]{0:T(512)S(1)}, f32[384]{0:T(512)}, u32[]{:S(2)}) copy-start(f32[384]{0:T(512)} %weights_ref.1) | copy-start | bytes 4612
  0.7 9.3 %copy-start.16 = (s32[384]{0:T(512)S(1)}, s32[384]{0:T(512)}, u32[]{:S(2)}) copy-start(s32[384]{0:T(512)} %lats_ref.1) | copy-start | bytes 4612
  0.7 9.3 %copy-start.7 = (f32[512]{0:T(512)S(1)}, f32[512]{0:T(512)}, u32[]{:S(2)}) copy-start(f32[512]{0:T(512)} %param.22) | copy-start | bytes 6148
  0.7 9.3 %copy-start.2 = (bf16[512,512]{1,0:T(8,128)(2,1)S(1)}, bf16[512,512]{1,0:T(8,128)(2,1)}, u32[]{:S(2)}) copy-start(bf16[512,512]{1,0:T(8,128)(2,1)} %w_mid_ref.1) | copy-start | bytes 1572868
  0.7 9.3 %copy-start.6 = (f32[512]{0:T(512)S(1)}, f32[512]{0:T(512)}, u32[]{:S(2)}) copy-start(f32[512]{0:T(512)} %param.20) | copy-start | bytes 6148
  0.7 9.3 %copy-start.5 = (f32[512]{0:T(512)S(1)}, f32[512]{0:T(512)}, u32[]{:S(2)}) copy-start(f32[512]{0:T(512)} %param.19) | copy-start | bytes 6148
  0.7 9.3 %copy-start.3 = (bf16[64,512]{1,0:T(8,128)(2,1)S(1)}, bf16[64,512]{1,0:T(8,128)(2,1)}, u32[]{:S(2)}) copy-start(bf16[64,512]{1,0:T(8,128)(2,1)} %w_in_ref.1) | copy-start | bytes 196612
  3.4 13.4 %all-to-all-start = ((bf16[8,16,1152]{2,1,0:T(8,128)(2,1)}), bf16[8,16,1152]{2,1,0:T(8,128)(2,1)S(1)}, u32[]{:S(2)}, u32[]{:S(2)}) async-start(bf16[8,16,1152]{2,1,0:T(8,128)(2,1)} %pack_state.1), calls=%async_computation | async-start | bytes 589824 | tf_op jit(solution)/shard_map/all_to_all | solution.py:406
  16.8 33.3 %copy-start.11 = (bf16[256,768]{1,0:T(8,128)(2,1)S(1)}, bf16[256,768]{1,0:T(8,128)(2,1)}, u32[]{:S(2)}) copy-start(bf16[256,768]{1,0:T(8,128)(2,1)} %get-tuple-element.24.cos_ref) | copy-start | bytes 1179652
  16.8 33.3 %copy-start.12 = (bf16[256,768]{1,0:T(8,128)(2,1)S(1)}, bf16[256,768]{1,0:T(8,128)(2,1)}, u32[]{:S(2)}) copy-start(bf16[256,768]{1,0:T(8,128)(2,1)} %get-tuple-element.25.sin_ref) | copy-start | bytes 1179652
  16.8 33.3 %copy-start.13 = (bf16[2,128,512]{2,1,0:T(8,128)(2,1)S(1)}, bf16[2,128,512]{2,1,0:T(8,128)(2,1)}, u32[]{:S(2)}) copy-start(bf16[2,128,512]{2,1,0:T(8,128)(2,1)} %get-tuple-element.21.first_ref) | copy-start | bytes 786436
  18.6 31.5 %copy-start.4 = (bf16[512,64]{0,1:T(8,128)(2,1)S(1)}, bf16[512,64]{0,1:T(8,128)(2,1)}, u32[]{:S(2)}) copy-start(bf16[512,64]{0,1:T(8,128)(2,1)} %param.23) | copy-start | bytes 196612
  18.6 31.5 %copy-start.8 = (bf16[512,512]{1,0:T(8,128)(2,1)S(1)}, bf16[512,512]{1,0:T(8,128)(2,1)}, u32[]{:S(2)}) copy-start(bf16[512,512]{1,0:T(8,128)(2,1)} %get-tuple-element.23.mid_ref) | copy-start | bytes 1572868
  18.7 31.5 %copy-start.9 = (bf16[768,256]{1,0:T(8,128)(2,1)S(1)}, bf16[768,256]{1,0:T(8,128)(2,1)}, u32[]{:S(2)}) copy-start(bf16[768,256]{1,0:T(8,128)(2,1)} %get-tuple-element.19.cos_t_ref) | copy-start | bytes 1179652
  18.7 31.5 %copy-start.10 = (bf16[768,256]{1,0:T(8,128)(2,1)S(1)}, bf16[768,256]{1,0:T(8,128)(2,1)}, u32[]{:S(2)}) copy-start(bf16[768,256]{1,0:T(8,128)(2,1)} %get-tuple-element.20.sin_t_ref) | copy-start | bytes 1179652
  18.7 31.5 %copy-start.14 = (f32[16,512]{1,0:T(8,128)S(1)}, f32[16,512]{1,0:T(8,128)}, u32[]{:S(2)}) copy-start(f32[16,512]{1,0:T(8,128)} %get-tuple-element.22.bias_ref) | copy-start | bytes 98308
  18.7 31.5 %copy-start.15 = (f32[1,768]{1,0:T(1,128)S(1)}, f32[1,768]{1,0:T(1,128)}, u32[]{:S(2)}) copy-start(f32[1,768]{1,0:T(1,128)} %get-tuple-element.26.scale_ref) | copy-start | bytes 9220
  61.5 25.8 %copy-start = (f32[256,32,32]{0,2,1:T(8,128)S(1)}, f32[256,32,32]{0,2,1:T(8,128)}, u32[]{:S(2)}) copy-start(f32[256,32,32]{0,2,1:T(8,128)} %param.25) | copy-start | bytes 3145732

commit v4 on v3

--- a/solution.py
+++ b/solution.py
@@ -27,13 +27,12 @@
 diffusion = 0.5
 
 VMEM = pl.BlockSpec(memory_space=pltpu.VMEM)
-SMEM = pl.BlockSpec(memory_space=pltpu.SMEM)
 HBM = pl.BlockSpec(memory_space=pltpu.HBM)
 
 
 def call(body, outs, scratch, flops, operands, specs, name):
     operands = [
-        pltpu.with_memory_space_constraint(o, pltpu.HBM) if spec in (HBM, SMEM) else o
+        pltpu.with_memory_space_constraint(o, pltpu.HBM) if spec is HBM else o
         for o, spec in zip(operands, specs)
     ]
     return pl.pallas_call(
@@ -52,9 +51,14 @@
     return jax.ShapeDtypeStruct(shape, dtype)
 
 
-def live_row(waves_ref, first, j):
-    lane = lax.broadcasted_iota(jnp.int32, (1, NTOT), 1)
-    return (lane >= waves_ref[first + j]).astype(F32)
+def own_waves(waves_ref):
+    lane = lax.broadcasted_iota(jnp.int32, (1, MW), 1)
+    row = waves_ref[...].astype(F32)
+    first = lax.axis_index("wave") * SLOTS
+    return [
+        jnp.sum(jnp.where(lane == first + 2 * q, row, 0.0)).astype(jnp.int32)
+        for q in range(SLOTS // 2)
+    ]
 
 
 def fold(first, second, q, m, extra):
@@ -78,7 +82,8 @@
     waves_hbm, target_hbm, state_hbm, send_ref, rows_ref, state_ref, waves_ref, target_ref, sems, small_sems
 ):
     copies = [
-        pltpu.make_async_copy(state_hbm.at[j], state_ref.at[j], sems.at[j]) for j in range(SLOTS)
+        pltpu.make_async_copy(state_hbm.at[half], state_ref.at[half], sems.at[i])
+        for i, half in enumerate((pl.ds(0, SLOTS // 2), pl.ds(SLOTS // 2, SLOTS // 2)))
     ]
     waves_copy = pltpu.make_async_copy(waves_hbm, waves_ref, small_sems.at[0])
     target_copy = pltpu.make_async_copy(target_hbm, target_ref, small_sems.at[1])
@@ -94,8 +99,9 @@
         rider = jnp.where((lane == SLOTS // 2) & (row == i), target_ref[i], rider)
     extra = jnp.concatenate([rider] * LEVS, axis=0)
     for q in range(SLOTS // 2):
+        if q % 2 == 0:
+            copies[q // 2].wait()
         for j in (2 * q, 2 * q + 1):
-            copies[j].wait()
             for e in range(LEVS):
                 for c in range(2):
                     for f in range(2):
@@ -117,9 +123,10 @@
 
 
 def prepare(
-    lats_ref, weights_ref, lat_ref, weight_ref, waves_ref, legendre_hbm, w_in_ref, b_in_ref, w_lat_ref, w_mid_ref,
+    lats_hbm, weights_hbm, lat_ref, weight_ref, waves_ref, legendre_hbm, w_in_ref, b_in_ref, w_lat_ref, w_mid_ref,
     b_mid_ref, band_ref, const_ref, cos_t_hbm, sin_t_hbm, cos_hbm, sin_hbm, first_hbm, mid_hbm, bias_hbm, scale_hbm,
-    hot_ref, cos_t_ref, sin_t_ref, cos_ref, sin_ref, first_ref, mid_ref, bias_ref, scale_ref, legendre_ref, sems, in_sem,
+    hot_ref, cos_t_ref, sin_t_ref, cos_ref, sin_ref, first_ref, mid_ref, bias_ref, scale_ref, legendre_ref, lats_ref, weights_ref,
+    sems, in_sems,
 ):
     pairs = (
         (cos_t_ref, cos_t_hbm),
@@ -132,8 +139,11 @@
         (scale_ref, scale_hbm),
     )
     copies = [pltpu.make_async_copy(a, b, sems.at[i]) for i, (a, b) in enumerate(pairs)]
-    legendre_copy = pltpu.make_async_copy(legendre_hbm, legendre_ref, in_sem)
-    legendre_copy.start()
+    legendre_copy = pltpu.make_async_copy(legendre_hbm, legendre_ref, in_sems.at[0])
+    lats_copy = pltpu.make_async_copy(lats_hbm, lats_ref, in_sems.at[1])
+    weights_copy = pltpu.make_async_copy(weights_hbm, weights_ref, in_sems.at[2])
+    for copy in (lats_copy, weights_copy, legendre_copy):
+        copy.start()
     x = lax.broadcasted_iota(jnp.int32, (NLON, MW), 0)
     product = (x * waves_ref[...]).astype(F32)
     phase = product - NLON * jnp.floor(product * (1.0 / NLON) + 0.5)
@@ -159,6 +169,8 @@
     lane = lax.broadcasted_iota(jnp.int32, (1, BAND * FEAT), 1)
     scale = jnp.zeros((1, BAND * FEAT), F32)
     own = lax.axis_index("wave") * BAND
+    lats_copy.wait()
+    weights_copy.wait()
     for b in range(BAND):
         t = lats_ref[own + b]
         here = (lane >= b * FEAT) & (lane < (b + 1) * FEAT)
@@ -206,7 +218,7 @@
 def to_fourier(
     waves_ref, recv_ref, band_ref, fourier_ref, state_ref, target_ref, rows_ref, both_ref, total_ref
 ):
-    first = lax.axis_index("wave") * SLOTS
+    waves = own_waves(waves_ref)
     both_ref[...] = jnp.zeros_like(both_ref)
     extra = recv_ref[:, :, 4 * NTOT :].astype(F32)
     for src in range(LEVS):
@@ -220,7 +232,7 @@
         q = j // 2
         if k == 0:
             both = recv_ref[:, :, q * NTOT : (q + 1) * NTOT].astype(F32).reshape(LEVS * 16, NTOT)
-            split = unfold(both, extra, q, waves_ref[first + j])
+            split = unfold(both, extra, q, waves[q])
         for src in range(LEVS):
             block = split[k][src * 16 : (src + 1) * 16]
             for c in range(2):
@@ -287,7 +299,7 @@
     waves_ref, recv_ref, band_ref, state_ref, const_ref, weight_ref, target_ref, coupling_ref,
     send_ref, wide_ref, temp_ref, rows_ref,
 ):
-    first = lax.axis_index("wave") * SLOTS
+    waves = own_waves(waves_ref)
     for i in range(2 * PAIRS):
         wide_ref[i] = recv_ref[:, i * 128 : (i + 1) * 128].astype(F32)
     target = target_ref[:, :1]
@@ -295,8 +307,9 @@
     degree = lax.broadcasted_iota(jnp.int32, (1, NTOT), 1)
     shrink = 1.0 / (1.0 + diffusion * (degree * (degree + 1)).astype(F32) / (NTOT * NTOT))
     for j in range(SLOTS):
-        live = live_row(waves_ref, first, j)
-        is_zero = (jnp.full((1, NTOT), waves_ref[first + j], jnp.int32) == 0).astype(F32)
+        m = waves[j // 2] if j % 2 == 0 else MW - 1 - waves[j // 2]
+        live = (degree >= m).astype(F32)
+        is_zero = (jnp.full((1, NTOT), m, jnp.int32) == 0).astype(F32)
         block = jnp.concatenate(
             [
                 jnp.concatenate(
@@ -345,27 +358,30 @@
     extra = jnp.zeros((LEVS * 16, 128), F32)
     for q in range(SLOTS // 2):
         flat = [rows_ref[j].reshape(LEVS * 16, NTOT) for j in (2 * q, 2 * q + 1)]
-        both, extra = fold(*flat, q, waves_ref[first + 2 * q], extra)
+        both, extra = fold(*flat, q, waves[q], extra)
         send_ref[:, :, q * NTOT : (q + 1) * NTOT] = both.astype(BF16).reshape(LEVS, 16, NTOT)
     send_ref[:, :, 4 * NTOT :] = extra.astype(BF16).reshape(LEVS, 16, 128)
 
 
 def unpack_state(waves_ref, recv_ref, state_hbm, state_ref, sems):
     copies = [
-        pltpu.make_async_copy(state_ref.at[j], state_hbm.at[j], sems.at[j]) for j in range(SLOTS)
+        pltpu.make_async_copy(
+            state_ref.at[pl.ds(2 * q, 2)], state_hbm.at[pl.ds(2 * q, 2)], sems.at[q]
+        )
+        for q in range(SLOTS // 2)
     ]
-    first = lax.axis_index("wave") * SLOTS
+    waves = own_waves(waves_ref)
     extra = recv_ref[:, :, 4 * NTOT :].astype(F32).reshape(LEVS * 16, 128)
     for q in range(SLOTS // 2):
         both = recv_ref[:, :, q * NTOT : (q + 1) * NTOT].astype(F32).reshape(LEVS * 16, NTOT)
-        split = unfold(both, extra, q, waves_ref[first + 2 * q])
+        split = unfold(both, extra, q, waves[q])
         for k in range(2):
             for e in range(LEVS):
                 for c in range(2):
                     for f in range(2):
                         at = e * 16 + c * 8 + f * 4
                         state_ref[2 * q + k, c, e, f] = split[k][at : at + 4, :]
-            copies[2 * q + k].start()
+        copies[q].start()
     for copy in copies:
         copy.wait()
 
@@ -395,7 +411,7 @@
             pltpu.VMEM(state.shape, F32),
             pltpu.SMEM((MW,), jnp.int32),
             pltpu.SMEM((ROWL,), F32),
-            pltpu.SemaphoreType.DMA((SLOTS,)),
+            pltpu.SemaphoreType.DMA((2,)),
             pltpu.SemaphoreType.DMA((2,)),
         ],
         10**8,
@@ -426,8 +442,10 @@
             pltpu.VMEM((NLAT // 128, NLAT, 128), F32),
             *(pltpu.VMEM(*m) for m in made),
             pltpu.VMEM(legendre.shape, BF16),
+            pltpu.SMEM((NLAT,), jnp.int32),
+            pltpu.SMEM((NLAT,), F32),
             pltpu.SemaphoreType.DMA((len(made),)),
-            pltpu.SemaphoreType.DMA,
+            pltpu.SemaphoreType.DMA((3,)),
         ],
         6 * 10**9,
         (
@@ -443,7 +461,7 @@
             w_mid,
             b_mid[None],
         ),
-        [SMEM] * 2 + [VMEM] * 3 + [HBM] + [VMEM] * 5,
+        [HBM] * 2 + [VMEM] * 3 + [HBM] + [VMEM] * 5,
         "prepare",
     )
     fourier, state_bf, target_all = call(
@@ -459,8 +477,8 @@
             pltpu.VMEM((2 * PAIRS, MW, 128), F32),
         ],
         10**9,
-        (wave_table, members, band),
-        [SMEM] + [VMEM] * 2,
+        (wave_table[None], members, band),
+        [VMEM] * 3,
         "to_fourier",
     )
     coef = lax.all_to_all(fourier, "wave", 0, 0, tiled=True)
@@ -492,7 +510,7 @@
         ],
         10**9,
         (
-            wave_table,
+            wave_table[None],
             back,
             band,
             state_bf,
@@ -501,17 +519,17 @@
             target_all,
             jnp.transpose(coupling, (1, 2, 0)).reshape(LEVELS * LEVELS, NTOT),
         ),
-        [SMEM] + [VMEM] * 7,
+        [VMEM] * 8,
         "to_spectral",
     )
     returned = lax.all_to_all(moved, "lev", 0, 0, tiled=True)
     new_state = call(
         unpack_state,
         pltpu.HBM(state.shape, F32),
-        [pltpu.VMEM(state.shape, F32), pltpu.SemaphoreType.DMA((SLOTS,))],
+        [pltpu.VMEM(state.shape, F32), pltpu.SemaphoreType.DMA((SLOTS // 2,))],
         10**8,
-        (wave_table, returned),
-        [SMEM, VMEM],
+        (wave_table[None], returned),
+        [VMEM] * 2,
         "unpack_state",
     )
     return new_state, jnp.transpose(grid, (1, 0, 2))[None]

time: 108 us -> 105 us (0.972)
  Pallas kernels: 26.8 us -> 23.9 us
    pallas_call x6, Pallas kernels: 26.8 us -> 23.9 us  [call(): pl.pallas_call(body, out_shape=outs, in_specs=specs, out_specs=jax.tree.m...]
where the time goes in v4:
time: 105 us; the launch traced here: 104 us
  blocking collectives  70.7 us (67%)
  Pallas kernels  23.9 us (23%)
  starting transfers between devices  6.58 us (6%)
  waiting for transfers between devices  1.98 us (2%)
  between operations  1.09 us (1%)
    all_to_all x1, blocking collectives, per_device(): coef = lax.all_to_all(fourier, 'wave', 0, 0, tiled=True)  31.4 us
    all_to_all x1, blocking collectives, per_device(): back = lax.all_to_all(tendw, 'wave', 0, 0, tiled=True)  25.8 us
    pallas_call x6, Pallas kernels, call(): pl.pallas_call(body, out_shape=outs, in_specs=specs, out_specs=jax.tree.m...  23.9 us
    all_to_all x1, blocking collectives, per_device(): returned = lax.all_to_all(moved, 'lev', 0, 0, tiled=True)  13.5 us
    all_to_all x1, starting transfers between devices, per_device(): members = lax.all_to_all(sent, 'lev', 0, 0, tiled=True)  6.58 us
  transfers between devices with their start and end apart: 1, of which 1 were waited for; matrix products, arithmetic and copies ran while one was open for 0% of the time, Pallas kernels for 5%

profile of v4, /device:TPU:1, one launch (start us, length us, event | category | flops | bytes accessed | tf_op | source)
XLA Modules:
  0.0 104.4 jit_solution(8354156510098444913)
XLA Ops:
  0.6 0.0 copy-start.1
  0.6 0.0 copy-start.17
  0.7 0.0 copy-start.16
  0.7 0.0 copy-start.7
  0.7 0.0 copy-start.2
  0.7 0.0 copy-start.6
  0.7 0.0 copy-start.5
  0.7 0.0 copy-start.3
  0.7 2.3 %pack_state.1 = bf16[8,16,1152]{2,1,0:T(8,128)(2,1)} custom-call(s32[256]{0:T(256)} %waves_hbm.1, f32[4]{0:T(128)} %target_hbm.1, f32[8,2,8,2,4,256]{5,4,3,2,1,0:T(4,128)} %state_hbm.1), custom_call_target="tpu_custom_call" | custom-call | flops 100000000 | bytes 2000000 | tf_op jit(solution)/shard_map/pack_state/pallas_call | solution.py:38
  3.0 6.6 %all-to-all-start = ((bf16[8,16,1152]{2,1,0:T(8,128)(2,1)}), bf16[8,16,1152]{2,1,0:T(8,128)(2,1)S(1)}, u32[]{:S(2)}, u32[]{:S(2)}) async-start(bf16[8,16,1152]{2,1,0:T(8,128)(2,1)} %pack_state.1), calls=%async_computation | async-start | bytes 589824 | tf_op jit(solution)/shard_map/all_to_all | solution.py:422
  9.6 0.0 copy-done.17
  9.6 0.0 copy-done.16
  9.6 0.0 copy-done.1
  9.6 0.0 copy-done.7
  9.6 0.0 copy-done.2
  9.6 0.0 copy-done.6
  9.7 0.0 copy-done.5
  9.7 0.0 copy-done.3
  9.7 4.8 %prepare.1 = (bf16[8,192,512]{2,1,0:T(8,128)(2,1)S(1)}, f32[8,256]{1,0:T(8,128)S(1)}, bf16[768,256]{1,0:T(8,128)(2,1)}, bf16[768,256]{1,0:T(8,128)(2,1)}, bf16[2...) custom-call(s32[384]{0:T(512)} %lats_hbm.1, ...), custom_call_target="tpu_custom_call" | custom-call | flops 6000000000 | bytes 2000000 | tf_op jit(solution)/shard_map/prepare/pallas_call | solution.py:38
  14.4 2.0 %all-to-all-done.recv_ref = bf16[8,16,1152]{2,1,0:T(8,128)(2,1)S(1)} async-done(((bf16[8,16,1152]{2,1,0:T(8,128)(2,1)}), bf16[8,16,1152]{2,1,0:T(8,128)(2,1)S(1)}, u32[]{:S(2)}, u32[]{:S(2)}) %all-to-all-start) | async-done | bytes 294944 | tf_op jit(solution)/shard_map/all_to_all | solution.py:422
  16.4 0.0 copy-start.11
  16.4 0.0 copy-start.12
  16.4 0.0 copy-start.13
  16.4 1.3 %to_fourier.1 = (bf16[256,1536]{1,0:T(8,128)(2,1)S(1)}, bf16[8,2,64,256]{3,2,1,0:T(8,128)(2,1)S(1)}, f32[32,128]{1,0:T(8,128)S(1)}) custom-call(s32[1,256]{1,0:T(1,128)S(1)} %bitcast.21, bf16[8,16,1152]{2,1,0:T(8,128)(2,1)S(1)} %all-to-all-done.recv_ref, bf16[8,192,512]{2,1,0:T(8,128)(2,1)S(1)} %get-tuple-element.17.band_ref), custom_call_target="tpu_custom_call" | custom-call | flops 1000000000 | bytes 2000000 | tf_op jit(solution)/shard_map/to_fourier/pallas_call | solution.py:38
  17.7 0.0 copy-start.4
  17.7 0.0 copy-start.8
  17.7 0.0 copy-start.9
  17.7 0.0 copy-start.10
  17.7 0.0 copy-start.14
  17.7 0.0 copy-start.15
  17.8 31.4 %all_to_all.32 = bf16[32,8,1536]{2,1,0:T(8,128)(2,1)S(1)} all-to-all(bf16[32,8,1536]{2,1,0:T(8,128)(2,1)S(1)} %bitcast.19), channel_id=1, replica_groups=mesh['lev'=8,'wave'=32] {'wave'}, dimensions={0} | all-to-all | bytes 1572864 | tf_op jit(solution)/shard_map/all_to_all | solution.py:484
  49.1 0.0 copy-done.11
  49.1 0.0 copy-done.12
  49.1 0.0 copy-done.13
  49.2 0.0 copy-done.4
  49.2 0.0 copy-done.8
  49.2 0.0 copy-done.9
  49.2 0.0 copy-done.10
  49.2 0.0 copy-done.14
  49.2 0.0 copy-done.15
  49.2 11.3 %columns.1 = (bf16[256,1536]{1,0:T(8,128)(2,1)S(1)}, bf16[12,64,768]{2,1,0:T(8,128)(2,1)}) custom-call(bf16[256,1536]{1,0:T(8,128)(2,1)S(1)} %bitcast.17, bf16[768,256]{1,0:T(8,128)(2,1)S(1)} %copy-done.9, bf16[768,256]{1,0:T(8,128)(2,1)S(1)} %copy-done.10, bf16[2,128,512]{2,1,0:T(8,128)(2,1)S(1)} %copy-done.13, f32[16,512]{1,0:T(8,128)S(1)} %copy-done.14, ...), custom_call_target="tpu_custom_call" | custom-call | flops 10000000000 | bytes 2000000 | tf_op jit(solution)/shard_map/columns/pallas_call | solution.py:38
  60.6 0.0 copy-start
  60.6 25.8 %all_to_all.33 = bf16[32,8,1536]{2,1,0:T(8,128)(2,1)S(1)} all-to-all(bf16[32,8,1536]{2,1,0:T(8,128)(2,1)S(1)} %bitcast.18), channel_id=1, replica_groups=mesh['lev'=8,'wave'=32] {'wave'}, dimensions={0} | all-to-all | bytes 1572864 | tf_op jit(solution)/shard_map/all_to_all | solution.py:502
  86.4 0.0 copy-done
  86.4 3.1 %to_spectral.1 = bf16[8,16,1152]{2,1,0:T(8,128)(2,1)S(1)} custom-call(s32[1,256]{1,0:T(1,128)S(1)} %bitcast.22, bf16[256,1536]{1,0:T(8,128)(2,1)S(1)} %bitcast.15, bf16[8,192,512]{2,1,0:T(8,128)(2,1)S(1)} %get-tuple-element.17.band_ref, bf16[8,2,64,256]{3,2,1,0:T(8,128)(2,1)S(1)} %get-tuple-element.28.state_ref, f32[8,256]{1,0:T(8,128)S(1)} %get-tuple-element.29.const_ref, ...), custom_call_target="tpu_custom_call" | custom-call | flops 1000000000 | bytes 2000000 | tf_op jit(solution)/shard_map/to_spectral/pallas_call | solution.py:38
  89.4 13.5 %all_to_all.34.recv_ref = bf16[8,16,1152]{2,1,0:T(8,128)(2,1)S(1)} all-to-all(bf16[8,16,1152]{2,1,0:T(8,128)(2,1)S(1)} %to_spectral.1), channel_id=1, replica_groups=mesh['lev'=8,'wave'=32] {'lev'}, dimensions={0} | all-to-all | bytes 589824 | tf_op jit(solution)/shard_map/all_to_all | solution.py:525
  102.9 1.2 %unpack_state.1 = f32[8,2,8,2,4,256]{5,4,3,2,1,0:T(4,128)} custom-call(s32[1,256]{1,0:T(1,128)S(1)} %bitcast.23, bf16[8,16,1152]{2,1,0:T(8,128)(2,1)S(1)} %all_to_all.34.recv_ref), custom_call_target="tpu_custom_call" | custom-call | flops 100000000 | bytes 2000000 | tf_op jit(solution)/shard_map/unpack_state/pallas_call | solution.py:38
  (2 shorter events, 0.0 us)
Async XLA Ops:
  0.6 9.0 %copy-start.1 = (s32[256]{0:T(256)S(1)}, s32[256]{0:T(256)}, u32[]{:S(2)}) copy-start(s32[256]{0:T(256)} %waves_hbm.1) | copy-start | bytes 3076
  0.6 8.9 %copy-start.17 = (f32[384]{0:T(512)S(1)}, f32[384]{0:T(512)}, u32[]{:S(2)}) copy-start(f32[384]{0:T(512)} %weights_hbm.1) | copy-start | bytes 4612
  0.7 8.9 %copy-start.16 = (s32[384]{0:T(512)S(1)}, s32[384]{0:T(512)}, u32[]{:S(2)}) copy-start(s32[384]{0:T(512)} %lats_hbm.1) | copy-start | bytes 4612
  0.7 9.0 %copy-start.7 = (f32[512]{0:T(512)S(1)}, f32[512]{0:T(512)}, u32[]{:S(2)}) copy-start(f32[512]{0:T(512)} %param.22) | copy-start | bytes 6148
  0.7 9.0 %copy-start.2 = (bf16[512,512]{1,0:T(8,128)(2,1)S(1)}, bf16[512,512]{1,0:T(8,128)(2,1)}, u32[]{:S(2)}) copy-start(bf16[512,512]{1,0:T(8,128)(2,1)} %w_mid_ref.1) | copy-start | bytes 1572868
  0.7 9.0 %copy-start.6 = (f32[512]{0:T(512)S(1)}, f32[512]{0:T(512)}, u32[]{:S(2)}) copy-start(f32[512]{0:T(512)} %param.20) | copy-start | bytes 6148
  0.7 9.0 %copy-start.5 = (f32[512]{0:T(512)S(1)}, f32[512]{0:T(512)}, u32[]{:S(2)}) copy-start(f32[512]{0:T(512)} %param.19) | copy-start | bytes 6148
  0.7 9.0 %copy-start.3 = (bf16[64,512]{1,0:T(8,128)(2,1)S(1)}, bf16[64,512]{1,0:T(8,128)(2,1)}, u32[]{:S(2)}) copy-start(bf16[64,512]{1,0:T(8,128)(2,1)} %w_in_ref.1) | copy-start | bytes 196612
  3.0 13.4 %all-to-all-start = ((bf16[8,16,1152]{2,1,0:T(8,128)(2,1)}), bf16[8,16,1152]{2,1,0:T(8,128)(2,1)S(1)}, u32[]{:S(2)}, u32[]{:S(2)}) async-start(bf16[8,16,1152]{2,1,0:T(8,128)(2,1)} %pack_state.1), calls=%async_computation | async-start | bytes 589824 | tf_op jit(solution)/shard_map/all_to_all | solution.py:422
  16.4 32.7 %copy-start.11 = (bf16[256,768]{1,0:T(8,128)(2,1)S(1)}, bf16[256,768]{1,0:T(8,128)(2,1)}, u32[]{:S(2)}) copy-start(bf16[256,768]{1,0:T(8,128)(2,1)} %get-tuple-element.24.cos_ref) | copy-start | bytes 1179652
  16.4 32.7 %copy-start.12 = (bf16[256,768]{1,0:T(8,128)(2,1)S(1)}, bf16[256,768]{1,0:T(8,128)(2,1)}, u32[]{:S(2)}) copy-start(bf16[256,768]{1,0:T(8,128)(2,1)} %get-tuple-element.25.sin_ref) | copy-start | bytes 1179652
  16.4 32.7 %copy-start.13 = (bf16[2,128,512]{2,1,0:T(8,128)(2,1)S(1)}, bf16[2,128,512]{2,1,0:T(8,128)(2,1)}, u32[]{:S(2)}) copy-start(bf16[2,128,512]{2,1,0:T(8,128)(2,1)} %get-tuple-element.21.first_ref) | copy-start | bytes 786436
  17.7 31.5 %copy-start.4 = (bf16[512,64]{0,1:T(8,128)(2,1)S(1)}, bf16[512,64]{0,1:T(8,128)(2,1)}, u32[]{:S(2)}) copy-start(bf16[512,64]{0,1:T(8,128)(2,1)} %param.23) | copy-start | bytes 196612
  17.7 31.5 %copy-start.8 = (bf16[512,512]{1,0:T(8,128)(2,1)S(1)}, bf16[512,512]{1,0:T(8,128)(2,1)}, u32[]{:S(2)}) copy-start(bf16[512,512]{1,0:T(8,128)(2,1)} %get-tuple-element.23.mid_ref) | copy-start | bytes 1572868
  17.7 31.5 %copy-start.9 = (bf16[768,256]{1,0:T(8,128)(2,1)S(1)}, bf16[768,256]{1,0:T(8,128)(2,1)}, u32[]{:S(2)}) copy-start(bf16[768,256]{1,0:T(8,128)(2,1)} %get-tuple-element.19.cos_t_ref) | copy-start | bytes 1179652
  17.7 31.5 %copy-start.10 = (bf16[768,256]{1,0:T(8,128)(2,1)S(1)}, bf16[768,256]{1,0:T(8,128)(2,1)}, u32[]{:S(2)}) copy-start(bf16[768,256]{1,0:T(8,128)(2,1)} %get-tuple-element.20.sin_t_ref) | copy-start | bytes 1179652
  17.7 31.5 %copy-start.14 = (f32[16,512]{1,0:T(8,128)S(1)}, f32[16,512]{1,0:T(8,128)}, u32[]{:S(2)}) copy-start(f32[16,512]{1,0:T(8,128)} %get-tuple-element.22.bias_ref) | copy-start | bytes 98308
  17.7 31.5 %copy-start.15 = (f32[1,768]{1,0:T(1,128)S(1)}, f32[1,768]{1,0:T(1,128)}, u32[]{:S(2)}) copy-start(f32[1,768]{1,0:T(1,128)} %get-tuple-element.26.scale_ref) | copy-start | bytes 9220
  60.6 25.8 %copy-start = (f32[256,32,32]{0,2,1:T(8,128)S(1)}, f32[256,32,32]{0,2,1:T(8,128)}, u32[]{:S(2)}) copy-start(f32[256,32,32]{0,2,1:T(8,128)} %param.25) | copy-start | bytes 3145732

commit v5 on v4

--- a/solution.py
+++ b/solution.py
@@ -104,9 +104,7 @@
         for j in (2 * q, 2 * q + 1):
             for e in range(LEVS):
                 for c in range(2):
-                    for f in range(2):
-                        at = c * 8 + f * 4
-                        rows_ref[j, e, at : at + 4, :] = state_ref[j, c, e, f]
+                    rows_ref[j, e, c * 8 : c * 8 + 8, :] = state_ref[j, c, e].reshape(8, NTOT)
         flat = [rows_ref[j].reshape(LEVS * 16, NTOT) for j in (2 * q, 2 * q + 1)]
         both, extra = fold(*flat, q, waves_ref[first + 2 * q], extra)
         send_ref[:, :, q * NTOT : (q + 1) * NTOT] = both.astype(BF16).reshape(LEVS, 16, NTOT)
@@ -123,10 +121,10 @@
 
 
 def prepare(
-    lats_hbm, weights_hbm, lat_ref, weight_ref, waves_ref, legendre_hbm, w_in_ref, b_in_ref, w_lat_ref, w_mid_ref,
+    lats_hbm, weights_hbm, lat_ref, weight_ref, waves_ref, legendre_hbm, coupling_hbm, w_in_ref, b_in_ref, w_lat_ref, w_mid_ref,
     b_mid_ref, band_ref, const_ref, cos_t_hbm, sin_t_hbm, cos_hbm, sin_hbm, first_hbm, mid_hbm, bias_hbm, scale_hbm,
-    hot_ref, cos_t_ref, sin_t_ref, cos_ref, sin_ref, first_ref, mid_ref, bias_ref, scale_ref, legendre_ref, lats_ref, weights_ref,
-    sems, in_sems,
+    by_level_hbm, hot_ref, cos_t_ref, sin_t_ref, cos_ref, sin_ref, first_ref, mid_ref, bias_ref, scale_ref, by_level_ref, legendre_ref, lats_ref,
+    weights_ref, coupling_ref, sems, in_sems,
 ):
     pairs = (
         (cos_t_ref, cos_t_hbm),
@@ -137,12 +135,19 @@
         (mid_ref, mid_hbm),
         (bias_ref, bias_hbm),
         (scale_ref, scale_hbm),
+        (by_level_ref, by_level_hbm),
     )
     copies = [pltpu.make_async_copy(a, b, sems.at[i]) for i, (a, b) in enumerate(pairs)]
     legendre_copy = pltpu.make_async_copy(legendre_hbm, legendre_ref, in_sems.at[0])
     lats_copy = pltpu.make_async_copy(lats_hbm, lats_ref, in_sems.at[1])
     weights_copy = pltpu.make_async_copy(weights_hbm, weights_ref, in_sems.at[2])
-    for copy in (lats_copy, weights_copy, legendre_copy):
+    coupling_copies = [
+        pltpu.make_async_copy(
+            coupling_hbm.at[:, pl.ds(i * 128, 128)], coupling_ref.at[i], in_sems.at[3 + i]
+        )
+        for i in range(2)
+    ]
+    for copy in (lats_copy, weights_copy, legendre_copy, *coupling_copies):
         copy.start()
     x = lax.broadcasted_iota(jnp.int32, (NLON, MW), 0)
     product = (x * waves_ref[...]).astype(F32)
@@ -155,9 +160,9 @@
     copies[0].start()
     sin_t_ref[...] = (sine * MW**-0.5).astype(BF16)
     copies[1].start()
-    cos_ref[...] = cosine.T.astype(BF16)
+    cos_ref[...] = cosine.astype(BF16).T
     copies[2].start()
-    sin_ref[...] = sine.T.astype(BF16)
+    sin_ref[...] = sine.astype(BF16).T
     copies[3].start()
     first_ref[...] = jnp.zeros_like(first_ref)
     half_in = (w_in_ref[...].astype(F32) * 0.5).astype(BF16)
@@ -182,6 +187,14 @@
     copies[6].start()
     scale_ref[...] = scale
     copies[7].start()
+
+    for i in range(2):
+        coupling_copies[i].wait()
+        for k in range(LEVELS):
+            by_level_ref[k, :, i * 128 : (i + 1) * 128] = coupling_ref[
+                i, pl.ds(k, LEVELS, stride=LEVELS), :
+            ]
+    copies[8].start()
 
     t = lax.broadcasted_iota(jnp.int32, (NLAT, NLAT), 0)
     hot = (t == lat_ref[...]).astype(F32).T
@@ -320,9 +333,8 @@
             ],
             axis=0,
         )
-        turned = block.T
-        tend_sum = jnp.sum(turned[:128], axis=1, keepdims=True)
-        parts = turned.astype(BF16)
+        parts = block.astype(BF16).T
+        tend_sum = jnp.sum(parts[:128].astype(F32), axis=1, keepdims=True)
         even = jnp.concatenate([parts[:64], parts[128:192]], axis=0)
         odd = jnp.concatenate([parts[64:128], parts[192:]], axis=0)
         spec = jnp.dot(even, band_ref[j, :, :NTOT], preferred_element_type=F32)
@@ -344,17 +356,15 @@
                 rows_ref[j, d, c * 8 + 4 : c * 8 + 8, :] = hum[d * 4 : d * 4 + 4]
     group = 4
     for g in range(2 * SLOTS // group):
-        for half in range(2):
-            lanes = slice(half * 128, (half + 1) * 128)
-            temps = [temp_ref[g * group + i, :, lanes] for i in range(group)]
-            for level in range(LEVELS):
-                matrix = coupling_ref[level * LEVELS : (level + 1) * LEVELS, lanes]
-                for i in range(group):
-                    j, c = divmod(g * group + i, 2)
-                    at = c * 8 + level % ROWL
-                    rows_ref[j, level // ROWL, at : at + 1, lanes] = jnp.sum(
-                        matrix * temps[i], axis=0, keepdims=True
-                    )
+        totals = [0.0] * group
+        for k in range(LEVELS):
+            matrix = coupling_ref[k]
+            for i in range(group):
+                totals[i] = totals[i] + matrix * temp_ref[g * group + i, k : k + 1, :]
+        for i in range(group):
+            j, c = divmod(g * group + i, 2)
+            for d in range(LEVS):
+                rows_ref[j, d, c * 8 : c * 8 + 4, :] = totals[i][d * 4 : d * 4 + 4]
     extra = jnp.zeros((LEVS * 16, 128), F32)
     for q in range(SLOTS // 2):
         flat = [rows_ref[j].reshape(LEVS * 16, NTOT) for j in (2 * q, 2 * q + 1)]
@@ -430,8 +440,9 @@
         ((HID, HID), BF16),
         ((16, HID), F32),
         ((1, BAND * FEAT), F32),
+        ((LEVELS, LEVELS, NTOT), F32),
     ]
-    band, const, cos_t, sin_t, cos, sin, first, mid, bias, scale = call(
+    band, const, cos_t, sin_t, cos, sin, first, mid, bias, scale, by_level = call(
         prepare,
         (
             out((SLOTS, PAIRS * WAVES, 2 * NTOT), BF16),
@@ -444,8 +455,9 @@
             pltpu.VMEM(legendre.shape, BF16),
             pltpu.SMEM((NLAT,), jnp.int32),
             pltpu.SMEM((NLAT,), F32),
+            pltpu.VMEM((2, LEVELS * LEVELS, 128), F32),
             pltpu.SemaphoreType.DMA((len(made),)),
-            pltpu.SemaphoreType.DMA((3,)),
+            pltpu.SemaphoreType.DMA((5,)),
         ],
         6 * 10**9,
         (
@@ -455,13 +467,14 @@
             lat_weight[None],
             wave_table[None],
             legendre,
+            jnp.transpose(coupling, (1, 2, 0)).reshape(LEVELS * LEVELS, NTOT),
             w_in,
             b_in[None],
             w_lat[None],
             w_mid,
             b_mid[None],
         ),
-        [HBM] * 2 + [VMEM] * 3 + [HBM] + [VMEM] * 5,
+        [HBM] * 2 + [VMEM] * 3 + [HBM] * 2 + [VMEM] * 5,
         "prepare",
     )
     fourier, state_bf, target_all = call(
@@ -517,7 +530,7 @@
             const,
             lat_weight[None],
             target_all,
-            jnp.transpose(coupling, (1, 2, 0)).reshape(LEVELS * LEVELS, NTOT),
+            by_level,
         ),
         [VMEM] * 8,
         "to_spectral",

time: 105 us -> 104 us (level)
  Pallas kernels: 23.9 us -> 22.4 us
    pallas_call x6, Pallas kernels: 23.9 us -> 22.4 us  [call(): pl.pallas_call(body, out_shape=outs, in_specs=specs, out_specs=jax.tree.m...]
  transfers between devices with their start and end apart: 1 -> 1, of which waited for: 1 -> 1; matrix products, arithmetic and copies ran while one was open for 0% -> 0% of each run, Pallas kernels for 5% -> 4%
where the time goes in v5:
time: 104 us
  blocking collectives  70.9 us (68%)
  Pallas kernels  22.4 us (22%)
  starting transfers between devices  6.58 us (6%)
  waiting for transfers between devices  2.63 us (3%)
  between operations  1.09 us (1%)
    all_to_all x1, blocking collectives, per_device(): coef = lax.all_to_all(fourier, 'wave', 0, 0, tiled=True)  31.4 us
    all_to_all x1, blocking collectives, per_device(): back = lax.all_to_all(tendw, 'wave', 0, 0, tiled=True)  25.8 us
    pallas_call x6, Pallas kernels, call(): pl.pallas_call(body, out_shape=outs, in_specs=specs, out_specs=jax.tree.m...  22.4 us
    all_to_all x1, blocking collectives, per_device(): returned = lax.all_to_all(moved, 'lev', 0, 0, tiled=True)  13.7 us
    all_to_all x1, starting transfers between devices, per_device(): members = lax.all_to_all(sent, 'lev', 0, 0, tiled=True)  6.58 us
    all_to_all x1, waiting for transfers between devices, per_device(): members = lax.all_to_all(sent, 'lev', 0, 0, tiled=True)  2.63 us
  transfers between devices with their start and end apart: 1, of which 1 were waited for; matrix products, arithmetic and copies ran while one was open for 0% of the time, Pallas kernels for 4%

profile of v5, /device:TPU:1, one launch (start us, length us, event | category | flops | bytes accessed | tf_op | source)
XLA Modules:
  0.0 103.6 jit_solution(5300918436006780074)
XLA Ops:
  0.6 0.0 copy-start.1
  0.6 0.0 copy-start.17
  0.7 0.0 copy-start.16
  0.7 0.0 copy-start.7
  0.7 0.0 copy-start.2
  0.7 0.0 copy-start.6
  0.7 0.0 copy-start.5
  0.7 0.0 copy-start.3
  0.7 2.3 %pack_state.1 = bf16[8,16,1152]{2,1,0:T(8,128)(2,1)} custom-call(s32[256]{0:T(256)} %waves_hbm.1, f32[4]{0:T(128)} %target_hbm.1, f32[8,2,8,2,4,256]{5,4,3,2,1,0:T(4,128)} %state_hbm.1), custom_call_target="tpu_custom_call" | custom-call | flops 100000000 | bytes 2000000 | tf_op jit(solution)/shard_map/pack_state/pallas_call | solution.py:38
  3.0 6.6 %all-to-all-start = ((bf16[8,16,1152]{2,1,0:T(8,128)(2,1)}), bf16[8,16,1152]{2,1,0:T(8,128)(2,1)S(1)}, u32[]{:S(2)}, u32[]{:S(2)}) async-start(bf16[8,16,1152]{2,1,0:T(8,128)(2,1)} %pack_state.1), calls=%async_computation | async-start | bytes 589824 | tf_op jit(solution)/shard_map/all_to_all | solution.py:432
  9.6 0.0 copy-done.17
  9.6 0.0 copy-done.16
  9.6 0.0 copy-done.1
  9.6 0.0 copy-done.7
  9.6 0.0 copy-done.2
  9.6 0.0 copy-done.6
  9.6 0.0 copy-done.5
  9.6 0.0 copy-done.3
  9.6 4.1 %prepare.1 = (bf16[8,192,512]{2,1,0:T(8,128)(2,1)S(1)}, f32[8,256]{1,0:T(8,128)S(1)}, bf16[768,256]{1,0:T(8,128)(2,1)}, bf16[768,256]{1,0:T(8,128)(2,1)}, bf16[2...) custom-call(s32[384]{0:T(512)} %lats_hbm.1, ...), custom_call_target="tpu_custom_call" | custom-call | flops 6000000000 | bytes 2000000 | tf_op jit(solution)/shard_map/prepare/pallas_call | solution.py:38
  13.8 2.6 %all-to-all-done.recv_ref = bf16[8,16,1152]{2,1,0:T(8,128)(2,1)S(1)} async-done(((bf16[8,16,1152]{2,1,0:T(8,128)(2,1)}), bf16[8,16,1152]{2,1,0:T(8,128)(2,1)S(1)}, u32[]{:S(2)}, u32[]{:S(2)}) %all-to-all-start) | async-done | bytes 294944 | tf_op jit(solution)/shard_map/all_to_all | solution.py:432
  16.4 0.0 copy-start.11
  16.4 0.0 copy-start.12
  16.4 0.0 copy-start.13
  16.4 1.3 %to_fourier.1 = (bf16[256,1536]{1,0:T(8,128)(2,1)S(1)}, bf16[8,2,64,256]{3,2,1,0:T(8,128)(2,1)S(1)}, f32[32,128]{1,0:T(8,128)S(1)}) custom-call(s32[1,256]{1,0:T(1,128)S(1)} %bitcast.20, bf16[8,16,1152]{2,1,0:T(8,128)(2,1)S(1)} %all-to-all-done.recv_ref, bf16[8,192,512]{2,1,0:T(8,128)(2,1)S(1)} %get-tuple-element.18.band_ref), custom_call_target="tpu_custom_call" | custom-call | flops 1000000000 | bytes 2000000 | tf_op jit(solution)/shard_map/to_fourier/pallas_call | solution.py:38
  17.7 0.0 copy-start.4
  17.7 0.0 copy-start.8
  17.7 0.0 copy-start.9
  17.7 0.0 copy-start.10
  17.7 0.0 copy-start.14
  17.7 0.0 copy-start.15
  17.7 31.4 %all_to_all.32 = bf16[32,8,1536]{2,1,0:T(8,128)(2,1)S(1)} all-to-all(bf16[32,8,1536]{2,1,0:T(8,128)(2,1)S(1)} %bitcast.18), channel_id=1, replica_groups=mesh['lev'=8,'wave'=32] {'wave'}, dimensions={0} | all-to-all | bytes 1572864 | tf_op jit(solution)/shard_map/all_to_all | solution.py:497
  49.1 0.0 copy-done.11
  49.1 0.0 copy-done.12
  49.1 0.0 copy-done.13
  49.1 0.0 copy-done.4
  49.1 0.0 copy-done.8
  49.1 0.0 copy-done.9
  49.2 0.0 copy-done.10
  49.2 0.0 copy-done.14
  49.2 0.0 copy-done.15
  49.2 11.3 %columns.1 = (bf16[256,1536]{1,0:T(8,128)(2,1)S(1)}, bf16[12,64,768]{2,1,0:T(8,128)(2,1)}) custom-call(bf16[256,1536]{1,0:T(8,128)(2,1)S(1)} %bitcast.16, bf16[768,256]{1,0:T(8,128)(2,1)S(1)} %copy-done.9, bf16[768,256]{1,0:T(8,128)(2,1)S(1)} %copy-done.10, bf16[2,128,512]{2,1,0:T(8,128)(2,1)S(1)} %copy-done.13, f32[16,512]{1,0:T(8,128)S(1)} %copy-done.14, ...), custom_call_target="tpu_custom_call" | custom-call | flops 10000000000 | bytes 2000000 | tf_op jit(solution)/shard_map/columns/pallas_call | solution.py:38
  60.5 0.0 copy-start
  60.5 25.8 %all_to_all.33 = bf16[32,8,1536]{2,1,0:T(8,128)(2,1)S(1)} all-to-all(bf16[32,8,1536]{2,1,0:T(8,128)(2,1)S(1)} %bitcast.17), channel_id=1, replica_groups=mesh['lev'=8,'wave'=32] {'wave'}, dimensions={0} | all-to-all | bytes 1572864 | tf_op jit(solution)/shard_map/all_to_all | solution.py:515
  86.3 0.0 copy-done
  86.3 2.2 %to_spectral.1 = bf16[8,16,1152]{2,1,0:T(8,128)(2,1)S(1)} custom-call(s32[1,256]{1,0:T(1,128)S(1)} %bitcast.21, bf16[256,1536]{1,0:T(8,128)(2,1)S(1)} %bitcast.15, bf16[8,192,512]{2,1,0:T(8,128)(2,1)S(1)} %get-tuple-element.18.band_ref, bf16[8,2,64,256]{3,2,1,0:T(8,128)(2,1)S(1)} %get-tuple-element.29.state_ref, f32[8,256]{1,0:T(8,128)S(1)} %get-tuple-element.30.const_ref, ...), custom_call_target="tpu_custom_call" | custom-call | flops 1000000000 | bytes 2000000 | tf_op jit(solution)/shard_map/to_spectral/pallas_call | solution.py:38
  88.5 13.7 %all_to_all.34.recv_ref = bf16[8,16,1152]{2,1,0:T(8,128)(2,1)S(1)} all-to-all(bf16[8,16,1152]{2,1,0:T(8,128)(2,1)S(1)} %to_spectral.1), channel_id=1, replica_groups=mesh['lev'=8,'wave'=32] {'lev'}, dimensions={0} | all-to-all | bytes 589824 | tf_op jit(solution)/shard_map/all_to_all | solution.py:538
  102.2 1.2 %unpack_state.1 = f32[8,2,8,2,4,256]{5,4,3,2,1,0:T(4,128)} custom-call(s32[1,256]{1,0:T(1,128)S(1)} %bitcast.22, bf16[8,16,1152]{2,1,0:T(8,128)(2,1)S(1)} %all_to_all.34.recv_ref), custom_call_target="tpu_custom_call" | custom-call | flops 100000000 | bytes 2000000 | tf_op jit(solution)/shard_map/unpack_state/pallas_call | solution.py:38
  (2 shorter events, 0.0 us)
Async XLA Ops:
  0.6 9.0 %copy-start.1 = (s32[256]{0:T(256)S(1)}, s32[256]{0:T(256)}, u32[]{:S(2)}) copy-start(s32[256]{0:T(256)} %waves_hbm.1) | copy-start | bytes 3076
  0.6 8.9 %copy-start.17 = (f32[384]{0:T(512)S(1)}, f32[384]{0:T(512)}, u32[]{:S(2)}) copy-start(f32[384]{0:T(512)} %weights_hbm.1) | copy-start | bytes 4612
  0.7 8.9 %copy-start.16 = (s32[384]{0:T(512)S(1)}, s32[384]{0:T(512)}, u32[]{:S(2)}) copy-start(s32[384]{0:T(512)} %lats_hbm.1) | copy-start | bytes 4612
  0.7 8.9 %copy-start.7 = (f32[512]{0:T(512)S(1)}, f32[512]{0:T(512)}, u32[]{:S(2)}) copy-start(f32[512]{0:T(512)} %param.22) | copy-start | bytes 6148
  0.7 8.9 %copy-start.2 = (bf16[512,512]{1,0:T(8,128)(2,1)S(1)}, bf16[512,512]{1,0:T(8,128)(2,1)}, u32[]{:S(2)}) copy-start(bf16[512,512]{1,0:T(8,128)(2,1)} %w_mid_ref.1) | copy-start | bytes 1572868
  0.7 8.9 %copy-start.6 = (f32[512]{0:T(512)S(1)}, f32[512]{0:T(512)}, u32[]{:S(2)}) copy-start(f32[512]{0:T(512)} %param.20) | copy-start | bytes 6148
  0.7 8.9 %copy-start.5 = (f32[512]{0:T(512)S(1)}, f32[512]{0:T(512)}, u32[]{:S(2)}) copy-start(f32[512]{0:T(512)} %param.19) | copy-start | bytes 6148
  0.7 8.9 %copy-start.3 = (bf16[64,512]{1,0:T(8,128)(2,1)S(1)}, bf16[64,512]{1,0:T(8,128)(2,1)}, u32[]{:S(2)}) copy-start(bf16[64,512]{1,0:T(8,128)(2,1)} %w_in_ref.1) | copy-start | bytes 196612
  3.0 13.4 %all-to-all-start = ((bf16[8,16,1152]{2,1,0:T(8,128)(2,1)}), bf16[8,16,1152]{2,1,0:T(8,128)(2,1)S(1)}, u32[]{:S(2)}, u32[]{:S(2)}) async-start(bf16[8,16,1152]{2,1,0:T(8,128)(2,1)} %pack_state.1), calls=%async_computation | async-start | bytes 589824 | tf_op jit(solution)/shard_map/all_to_all | solution.py:432
  16.4 32.7 %copy-start.11 = (bf16[256,768]{1,0:T(8,128)(2,1)S(1)}, bf16[256,768]{1,0:T(8,128)(2,1)}, u32[]{:S(2)}) copy-start(bf16[256,768]{1,0:T(8,128)(2,1)} %get-tuple-element.25.cos_ref) | copy-start | bytes 1179652
  16.4 32.7 %copy-start.12 = (bf16[256,768]{1,0:T(8,128)(2,1)S(1)}, bf16[256,768]{1,0:T(8,128)(2,1)}, u32[]{:S(2)}) copy-start(bf16[256,768]{1,0:T(8,128)(2,1)} %get-tuple-element.26.sin_ref) | copy-start | bytes 1179652
  16.4 32.7 %copy-start.13 = (bf16[2,128,512]{2,1,0:T(8,128)(2,1)S(1)}, bf16[2,128,512]{2,1,0:T(8,128)(2,1)}, u32[]{:S(2)}) copy-start(bf16[2,128,512]{2,1,0:T(8,128)(2,1)} %get-tuple-element.22.first_ref) | copy-start | bytes 786436
  17.7 31.5 %copy-start.4 = (bf16[512,64]{0,1:T(8,128)(2,1)S(1)}, bf16[512,64]{0,1:T(8,128)(2,1)}, u32[]{:S(2)}) copy-start(bf16[512,64]{0,1:T(8,128)(2,1)} %param.23) | copy-start | bytes 196612
  17.7 31.5 %copy-start.8 = (bf16[512,512]{1,0:T(8,128)(2,1)S(1)}, bf16[512,512]{1,0:T(8,128)(2,1)}, u32[]{:S(2)}) copy-start(bf16[512,512]{1,0:T(8,128)(2,1)} %get-tuple-element.24.mid_ref) | copy-start | bytes 1572868
  17.7 31.5 %copy-start.9 = (bf16[768,256]{1,0:T(8,128)(2,1)S(1)}, bf16[768,256]{1,0:T(8,128)(2,1)}, u32[]{:S(2)}) copy-start(bf16[768,256]{1,0:T(8,128)(2,1)} %get-tuple-element.20.cos_t_ref) | copy-start | bytes 1179652
  17.7 31.5 %copy-start.10 = (bf16[768,256]{1,0:T(8,128)(2,1)S(1)}, bf16[768,256]{1,0:T(8,128)(2,1)}, u32[]{:S(2)}) copy-start(bf16[768,256]{1,0:T(8,128)(2,1)} %get-tuple-element.21.sin_t_ref) | copy-start | bytes 1179652
  17.7 31.5 %copy-start.14 = (f32[16,512]{1,0:T(8,128)S(1)}, f32[16,512]{1,0:T(8,128)}, u32[]{:S(2)}) copy-start(f32[16,512]{1,0:T(8,128)} %get-tuple-element.23.bias_ref) | copy-start | bytes 98308
  17.7 31.5 %copy-start.15 = (f32[1,768]{1,0:T(1,128)S(1)}, f32[1,768]{1,0:T(1,128)}, u32[]{:S(2)}) copy-start(f32[1,768]{1,0:T(1,128)} %get-tuple-element.27.scale_ref) | copy-start | bytes 9220
  60.5 25.8 %copy-start = (f32[32,32,256]{2,1,0:T(8,128)S(1)}, f32[32,32,256]{2,1,0:T(8,128)}, u32[]{:S(2)}) copy-start(f32[32,32,256]{2,1,0:T(8,128)} %get-tuple-element.32.coupling_ref) | copy-start | bytes 3145732

commit v6 on v5

--- a/solution.py
+++ b/solution.py
@@ -310,7 +310,7 @@
 
 def to_spectral(
     waves_ref, recv_ref, band_ref, state_ref, const_ref, weight_ref, target_ref, coupling_ref,
-    send_ref, wide_ref, temp_ref, rows_ref,
+    send_ref, wide_ref, temp_ref, rows_ref, low_ref,
 ):
     waves = own_waves(waves_ref)
     for i in range(2 * PAIRS):
@@ -354,17 +354,35 @@
             hum = (old_hum + time_step * hum) * (live * shrink)
             for d in range(LEVS):
                 rows_ref[j, d, c * 8 + 4 : c * 8 + 8, :] = hum[d * 4 : d * 4 + 4]
-    group = 4
-    for g in range(2 * SLOTS // group):
+    for i in range(SLOTS):
+        at = i // 2 * 4 + i % 2
+        low_ref[i] = temp_ref[at, :, :128] + temp_ref[at + 2, :, :128]
+    group = 8
+    for g in range(3):
+        lanes = slice(0, 128) if g == 2 else slice(128, NTOT)
         totals = [0.0] * group
         for k in range(LEVELS):
-            matrix = coupling_ref[k]
+            matrix = coupling_ref[k, :, lanes]
             for i in range(group):
-                totals[i] = totals[i] + matrix * temp_ref[g * group + i, k : k + 1, :]
+                if g == 2:
+                    temp = low_ref[i, k : k + 1, :]
+                else:
+                    temp = temp_ref[g * group + i, k : k + 1, lanes]
+                totals[i] = totals[i] + matrix * temp
         for i in range(group):
-            j, c = divmod(g * group + i, 2)
-            for d in range(LEVS):
-                rows_ref[j, d, c * 8 : c * 8 + 4, :] = totals[i][d * 4 : d * 4 + 4]
+            if g == 2:
+                q, c = divmod(i, 2)
+                low = jnp.full((LEVELS, 128), waves[q], jnp.int32) < 128
+                parts = [
+                    (2 * q, jnp.where(low, totals[i], 0.0)),
+                    (2 * q + 1, jnp.where(low, 0.0, totals[i])),
+                ]
+            else:
+                j, c = divmod(g * group + i, 2)
+                parts = [(j, totals[i])]
+            for j, part in parts:
+                for d in range(LEVS):
+                    rows_ref[j, d, c * 8 : c * 8 + 4, lanes] = part[d * 4 : d * 4 + 4]
     extra = jnp.zeros((LEVS * 16, 128), F32)
     for q in range(SLOTS // 2):
         flat = [rows_ref[j].reshape(LEVS * 16, NTOT) for j in (2 * q, 2 * q + 1)]
@@ -520,6 +538,7 @@
             pltpu.VMEM((2 * PAIRS, MW, 128), F32),
             pltpu.VMEM((2 * SLOTS, LEVELS, NTOT), F32),
             pltpu.VMEM(rows, F32),
+            pltpu.VMEM((SLOTS, LEVELS, 128), F32),
         ],
         10**9,
         (

time: 104 us -> 104 us (level)
  no operation moved by 1% of the time
where the time goes in v6:
time: 104 us; the launch traced here: 103 us
  blocking collectives  70.9 us (68%)
  Pallas kernels  22.2 us (21%)
  starting transfers between devices  6.58 us (6%)
  waiting for transfers between devices  2.63 us (3%)
  between operations  1.07 us (1%)
    all_to_all x1, blocking collectives, per_device(): coef = lax.all_to_all(fourier, 'wave', 0, 0, tiled=True)  31.4 us
    all_to_all x1, blocking collectives, per_device(): back = lax.all_to_all(tendw, 'wave', 0, 0, tiled=True)  25.5 us
    pallas_call x6, Pallas kernels, call(): pl.pallas_call(body, out_shape=outs, in_specs=specs, out_specs=jax.tree.m...  22.2 us
    all_to_all x1, blocking collectives, per_device(): returned = lax.all_to_all(moved, 'lev', 0, 0, tiled=True)  13.9 us
    all_to_all x1, starting transfers between devices, per_device(): members = lax.all_to_all(sent, 'lev', 0, 0, tiled=True)  6.58 us
    all_to_all x1, waiting for transfers between devices, per_device(): members = lax.all_to_all(sent, 'lev', 0, 0, tiled=True)  2.63 us
  transfers between devices with their start and end apart: 1, of which 1 were waited for; matrix products, arithmetic and copies ran while one was open for 0% of the time, Pallas kernels for 4%

profile of v6, /device:TPU:1, one launch (start us, length us, event | category | flops | bytes accessed | tf_op | source)
XLA Modules:
  0.0 103.4 jit_solution(926759372302512964)
XLA Ops:
  0.6 0.0 copy-start.1
  0.6 0.0 copy-start.17
  0.7 0.0 copy-start.16
  0.7 0.0 copy-start.7
  0.7 0.0 copy-start.2
  0.7 0.0 copy-start.6
  0.7 0.0 copy-start.5
  0.7 0.0 copy-start.3
  0.7 2.3 %pack_state.1 = bf16[8,16,1152]{2,1,0:T(8,128)(2,1)} custom-call(s32[256]{0:T(256)} %waves_hbm.1, f32[4]{0:T(128)} %target_hbm.1, f32[8,2,8,2,4,256]{5,4,3,2,1,0:T(4,128)} %state_hbm.1), custom_call_target="tpu_custom_call" | custom-call | flops 100000000 | bytes 2000000 | tf_op jit(solution)/shard_map/pack_state/pallas_call | solution.py:38
  3.0 6.6 %all-to-all-start = ((bf16[8,16,1152]{2,1,0:T(8,128)(2,1)}), bf16[8,16,1152]{2,1,0:T(8,128)(2,1)S(1)}, u32[]{:S(2)}, u32[]{:S(2)}) async-start(bf16[8,16,1152]{2,1,0:T(8,128)(2,1)} %pack_state.1), calls=%async_computation | async-start | bytes 589824 | tf_op jit(solution)/shard_map/all_to_all | solution.py:450
  9.6 0.0 copy-done.17
  9.6 0.0 copy-done.16
  9.6 0.0 copy-done.1
  9.6 0.0 copy-done.7
  9.6 0.0 copy-done.2
  9.6 0.0 copy-done.6
  9.6 0.0 copy-done.5
  9.6 0.0 copy-done.3
  9.6 4.1 %prepare.1 = (bf16[8,192,512]{2,1,0:T(8,128)(2,1)S(1)}, f32[8,256]{1,0:T(8,128)S(1)}, bf16[768,256]{1,0:T(8,128)(2,1)}, bf16[768,256]{1,0:T(8,128)(2,1)}, bf16[2...) custom-call(s32[384]{0:T(512)} %lats_hbm.1, ...), custom_call_target="tpu_custom_call" | custom-call | flops 6000000000 | bytes 2000000 | tf_op jit(solution)/shard_map/prepare/pallas_call | solution.py:38
  13.8 2.6 %all-to-all-done.recv_ref = bf16[8,16,1152]{2,1,0:T(8,128)(2,1)S(1)} async-done(((bf16[8,16,1152]{2,1,0:T(8,128)(2,1)}), bf16[8,16,1152]{2,1,0:T(8,128)(2,1)S(1)}, u32[]{:S(2)}, u32[]{:S(2)}) %all-to-all-start) | async-done | bytes 294944 | tf_op jit(solution)/shard_map/all_to_all | solution.py:450
  16.4 0.0 copy-start.11
  16.4 0.0 copy-start.12
  16.4 0.0 copy-start.13
  16.4 1.3 %to_fourier.1 = (bf16[256,1536]{1,0:T(8,128)(2,1)S(1)}, bf16[8,2,64,256]{3,2,1,0:T(8,128)(2,1)S(1)}, f32[32,128]{1,0:T(8,128)S(1)}) custom-call(s32[1,256]{1,0:T(1,128)S(1)} %bitcast.20, bf16[8,16,1152]{2,1,0:T(8,128)(2,1)S(1)} %all-to-all-done.recv_ref, bf16[8,192,512]{2,1,0:T(8,128)(2,1)S(1)} %get-tuple-element.18.band_ref), custom_call_target="tpu_custom_call" | custom-call | flops 1000000000 | bytes 2000000 | tf_op jit(solution)/shard_map/to_fourier/pallas_call | solution.py:38
  17.7 0.0 copy-start.4
  17.7 0.0 copy-start.8
  17.7 0.0 copy-start.9
  17.7 0.0 copy-start.10
  17.7 0.0 copy-start.14
  17.7 0.0 copy-start.15
  17.7 31.4 %all_to_all.32 = bf16[32,8,1536]{2,1,0:T(8,128)(2,1)S(1)} all-to-all(bf16[32,8,1536]{2,1,0:T(8,128)(2,1)S(1)} %bitcast.18), channel_id=1, replica_groups=mesh['lev'=8,'wave'=32] {'wave'}, dimensions={0} | all-to-all | bytes 1572864 | tf_op jit(solution)/shard_map/all_to_all | solution.py:515
  49.1 0.0 copy-done.11
  49.1 0.0 copy-done.12
  49.1 0.0 copy-done.13
  49.1 0.0 copy-done.4
  49.1 0.0 copy-done.8
  49.1 0.0 copy-done.9
  49.2 0.0 copy-done.10
  49.2 0.0 copy-done.14
  49.2 0.0 copy-done.15
  49.2 11.3 %columns.1 = (bf16[256,1536]{1,0:T(8,128)(2,1)S(1)}, bf16[12,64,768]{2,1,0:T(8,128)(2,1)}) custom-call(bf16[256,1536]{1,0:T(8,128)(2,1)S(1)} %bitcast.16, bf16[768,256]{1,0:T(8,128)(2,1)S(1)} %copy-done.9, bf16[768,256]{1,0:T(8,128)(2,1)S(1)} %copy-done.10, bf16[2,128,512]{2,1,0:T(8,128)(2,1)S(1)} %copy-done.13, f32[16,512]{1,0:T(8,128)S(1)} %copy-done.14, ...), custom_call_target="tpu_custom_call" | custom-call | flops 10000000000 | bytes 2000000 | tf_op jit(solution)/shard_map/columns/pallas_call | solution.py:38
  60.5 0.0 copy-start
  60.5 25.5 %all_to_all.33 = bf16[32,8,1536]{2,1,0:T(8,128)(2,1)S(1)} all-to-all(bf16[32,8,1536]{2,1,0:T(8,128)(2,1)S(1)} %bitcast.17), channel_id=1, replica_groups=mesh['lev'=8,'wave'=32] {'wave'}, dimensions={0} | all-to-all | bytes 1572864 | tf_op jit(solution)/shard_map/all_to_all | solution.py:533
  86.1 0.0 copy-done
  86.1 2.0 %to_spectral.1 = bf16[8,16,1152]{2,1,0:T(8,128)(2,1)S(1)} custom-call(s32[1,256]{1,0:T(1,128)S(1)} %bitcast.21, bf16[256,1536]{1,0:T(8,128)(2,1)S(1)} %bitcast.15, bf16[8,192,512]{2,1,0:T(8,128)(2,1)S(1)} %get-tuple-element.18.band_ref, bf16[8,2,64,256]{3,2,1,0:T(8,128)(2,1)S(1)} %get-tuple-element.29.state_ref, f32[8,256]{1,0:T(8,128)S(1)} %get-tuple-element.30.const_ref, ...), custom_call_target="tpu_custom_call" | custom-call | flops 1000000000 | bytes 2000000 | tf_op jit(solution)/shard_map/to_spectral/pallas_call | solution.py:38
  88.1 13.9 %all_to_all.34.recv_ref = bf16[8,16,1152]{2,1,0:T(8,128)(2,1)S(1)} all-to-all(bf16[8,16,1152]{2,1,0:T(8,128)(2,1)S(1)} %to_spectral.1), channel_id=1, replica_groups=mesh['lev'=8,'wave'=32] {'lev'}, dimensions={0} | all-to-all | bytes 589824 | tf_op jit(solution)/shard_map/all_to_all | solution.py:557
  102.0 1.2 %unpack_state.1 = f32[8,2,8,2,4,256]{5,4,3,2,1,0:T(4,128)} custom-call(s32[1,256]{1,0:T(1,128)S(1)} %bitcast.22, bf16[8,16,1152]{2,1,0:T(8,128)(2,1)S(1)} %all_to_all.34.recv_ref), custom_call_target="tpu_custom_call" | custom-call | flops 100000000 | bytes 2000000 | tf_op jit(solution)/shard_map/unpack_state/pallas_call | solution.py:38
  (2 shorter events, 0.0 us)
Async XLA Ops:
  0.6 9.0 %copy-start.1 = (s32[256]{0:T(256)S(1)}, s32[256]{0:T(256)}, u32[]{:S(2)}) copy-start(s32[256]{0:T(256)} %waves_hbm.1) | copy-start | bytes 3076
  0.6 8.9 %copy-start.17 = (f32[384]{0:T(512)S(1)}, f32[384]{0:T(512)}, u32[]{:S(2)}) copy-start(f32[384]{0:T(512)} %weights_hbm.1) | copy-start | bytes 4612
  0.7 8.9 %copy-start.16 = (s32[384]{0:T(512)S(1)}, s32[384]{0:T(512)}, u32[]{:S(2)}) copy-start(s32[384]{0:T(512)} %lats_hbm.1) | copy-start | bytes 4612
  0.7 8.9 %copy-start.7 = (f32[512]{0:T(512)S(1)}, f32[512]{0:T(512)}, u32[]{:S(2)}) copy-start(f32[512]{0:T(512)} %param.22) | copy-start | bytes 6148
  0.7 8.9 %copy-start.2 = (bf16[512,512]{1,0:T(8,128)(2,1)S(1)}, bf16[512,512]{1,0:T(8,128)(2,1)}, u32[]{:S(2)}) copy-start(bf16[512,512]{1,0:T(8,128)(2,1)} %w_mid_ref.1) | copy-start | bytes 1572868
  0.7 8.9 %copy-start.6 = (f32[512]{0:T(512)S(1)}, f32[512]{0:T(512)}, u32[]{:S(2)}) copy-start(f32[512]{0:T(512)} %param.20) | copy-start | bytes 6148
  0.7 8.9 %copy-start.5 = (f32[512]{0:T(512)S(1)}, f32[512]{0:T(512)}, u32[]{:S(2)}) copy-start(f32[512]{0:T(512)} %param.19) | copy-start | bytes 6148
  0.7 8.9 %copy-start.3 = (bf16[64,512]{1,0:T(8,128)(2,1)S(1)}, bf16[64,512]{1,0:T(8,128)(2,1)}, u32[]{:S(2)}) copy-start(bf16[64,512]{1,0:T(8,128)(2,1)} %w_in_ref.1) | copy-start | bytes 196612
  3.0 13.4 %all-to-all-start = ((bf16[8,16,1152]{2,1,0:T(8,128)(2,1)}), bf16[8,16,1152]{2,1,0:T(8,128)(2,1)S(1)}, u32[]{:S(2)}, u32[]{:S(2)}) async-start(bf16[8,16,1152]{2,1,0:T(8,128)(2,1)} %pack_state.1), calls=%async_computation | async-start | bytes 589824 | tf_op jit(solution)/shard_map/all_to_all | solution.py:450
  16.4 32.7 %copy-start.11 = (bf16[256,768]{1,0:T(8,128)(2,1)S(1)}, bf16[256,768]{1,0:T(8,128)(2,1)}, u32[]{:S(2)}) copy-start(bf16[256,768]{1,0:T(8,128)(2,1)} %get-tuple-element.25.cos_ref) | copy-start | bytes 1179652
  16.4 32.7 %copy-start.12 = (bf16[256,768]{1,0:T(8,128)(2,1)S(1)}, bf16[256,768]{1,0:T(8,128)(2,1)}, u32[]{:S(2)}) copy-start(bf16[256,768]{1,0:T(8,128)(2,1)} %get-tuple-element.26.sin_ref) | copy-start | bytes 1179652
  16.4 32.7 %copy-start.13 = (bf16[2,128,512]{2,1,0:T(8,128)(2,1)S(1)}, bf16[2,128,512]{2,1,0:T(8,128)(2,1)}, u32[]{:S(2)}) copy-start(bf16[2,128,512]{2,1,0:T(8,128)(2,1)} %get-tuple-element.22.first_ref) | copy-start | bytes 786436
  17.7 31.5 %copy-start.4 = (bf16[512,64]{0,1:T(8,128)(2,1)S(1)}, bf16[512,64]{0,1:T(8,128)(2,1)}, u32[]{:S(2)}) copy-start(bf16[512,64]{0,1:T(8,128)(2,1)} %param.23) | copy-start | bytes 196612
  17.7 31.5 %copy-start.8 = (bf16[512,512]{1,0:T(8,128)(2,1)S(1)}, bf16[512,512]{1,0:T(8,128)(2,1)}, u32[]{:S(2)}) copy-start(bf16[512,512]{1,0:T(8,128)(2,1)} %get-tuple-element.24.mid_ref) | copy-start | bytes 1572868
  17.7 31.5 %copy-start.9 = (bf16[768,256]{1,0:T(8,128)(2,1)S(1)}, bf16[768,256]{1,0:T(8,128)(2,1)}, u32[]{:S(2)}) copy-start(bf16[768,256]{1,0:T(8,128)(2,1)} %get-tuple-element.20.cos_t_ref) | copy-start | bytes 1179652
  17.7 31.5 %copy-start.10 = (bf16[768,256]{1,0:T(8,128)(2,1)S(1)}, bf16[768,256]{1,0:T(8,128)(2,1)}, u32[]{:S(2)}) copy-start(bf16[768,256]{1,0:T(8,128)(2,1)} %get-tuple-element.21.sin_t_ref) | copy-start | bytes 1179652
  17.7 31.5 %copy-start.14 = (f32[16,512]{1,0:T(8,128)S(1)}, f32[16,512]{1,0:T(8,128)}, u32[]{:S(2)}) copy-start(f32[16,512]{1,0:T(8,128)} %get-tuple-element.23.bias_ref) | copy-start | bytes 98308
  17.7 31.5 %copy-start.15 = (f32[1,768]{1,0:T(1,128)S(1)}, f32[1,768]{1,0:T(1,128)}, u32[]{:S(2)}) copy-start(f32[1,768]{1,0:T(1,128)} %get-tuple-element.27.scale_ref) | copy-start | bytes 9220
  60.5 25.6 %copy-start = (f32[32,32,256]{2,1,0:T(8,128)S(1)}, f32[32,32,256]{2,1,0:T(8,128)}, u32[]{:S(2)}) copy-start(f32[32,32,256]{2,1,0:T(8,128)} %get-tuple-element.32.coupling_ref) | copy-start | bytes 3145732

commit v7 on v6

--- a/solution.py
+++ b/solution.py
@@ -357,21 +357,21 @@
     for i in range(SLOTS):
         at = i // 2 * 4 + i % 2
         low_ref[i] = temp_ref[at, :, :128] + temp_ref[at + 2, :, :128]
-    group = 8
-    for g in range(3):
-        lanes = slice(0, 128) if g == 2 else slice(128, NTOT)
+    group = 4
+    for g in range(6):
+        lanes = slice(0, 128) if g >= 4 else slice(128, NTOT)
         totals = [0.0] * group
         for k in range(LEVELS):
             matrix = coupling_ref[k, :, lanes]
             for i in range(group):
-                if g == 2:
-                    temp = low_ref[i, k : k + 1, :]
+                if g >= 4:
+                    temp = low_ref[(g - 4) * group + i, k : k + 1, :]
                 else:
                     temp = temp_ref[g * group + i, k : k + 1, lanes]
                 totals[i] = totals[i] + matrix * temp
         for i in range(group):
-            if g == 2:
-                q, c = divmod(i, 2)
+            if g >= 4:
+                q, c = divmod((g - 4) * group + i, 2)
                 low = jnp.full((LEVELS, 128), waves[q], jnp.int32) < 128
                 parts = [
                     (2 * q, jnp.where(low, totals[i], 0.0)),

time: 104 us -> 104 us (level)
  no operation moved by 1% of the time
where the time goes in v7:
time: 104 us; the launch traced here: 103 us
  blocking collectives  70.9 us (68%)
  Pallas kernels  22.1 us (21%)
  starting transfers between devices  6.58 us (6%)
  waiting for transfers between devices  2.63 us (3%)
  between operations  1.07 us (1%)
    all_to_all x1, blocking collectives, per_device(): coef = lax.all_to_all(fourier, 'wave', 0, 0, tiled=True)  31.4 us
    all_to_all x1, blocking collectives, per_device(): back = lax.all_to_all(tendw, 'wave', 0, 0, tiled=True)  25.5 us
    pallas_call x6, Pallas kernels, call(): pl.pallas_call(body, out_shape=outs, in_specs=specs, out_specs=jax.tree.m...  22.1 us
    all_to_all x1, blocking collectives, per_device(): returned = lax.all_to_all(moved, 'lev', 0, 0, tiled=True)  13.9 us
    all_to_all x1, starting transfers between devices, per_device(): members = lax.all_to_all(sent, 'lev', 0, 0, tiled=True)  6.58 us
    all_to_all x1, waiting for transfers between devices, per_device(): members = lax.all_to_all(sent, 'lev', 0, 0, tiled=True)  2.63 us
  transfers between devices with their start and end apart: 1, of which 1 were waited for; matrix products, arithmetic and copies ran while one was open for 0% of the time, Pallas kernels for 4%

profile of v7, /device:TPU:1, one launch (start us, length us, event | category | flops | bytes accessed | tf_op | source)
XLA Modules:
  0.0 103.4 jit_solution(15099352030771365279)
XLA Ops:
  0.6 0.0 copy-start.1
  0.6 0.0 copy-start.17
  0.7 0.0 copy-start.16
  0.7 0.0 copy-start.7
  0.7 0.0 copy-start.2
  0.7 0.0 copy-start.6
  0.7 0.0 copy-start.5
  0.7 0.0 copy-start.3
  0.7 2.3 %pack_state.1 = bf16[8,16,1152]{2,1,0:T(8,128)(2,1)} custom-call(s32[256]{0:T(256)} %waves_hbm.1, f32[4]{0:T(128)} %target_hbm.1, f32[8,2,8,2,4,256]{5,4,3,2,1,0:T(4,128)} %state_hbm.1), custom_call_target="tpu_custom_call" | custom-call | flops 100000000 | bytes 2000000 | tf_op jit(solution)/shard_map/pack_state/pallas_call | solution.py:38
  3.0 6.6 %all-to-all-start = ((bf16[8,16,1152]{2,1,0:T(8,128)(2,1)}), bf16[8,16,1152]{2,1,0:T(8,128)(2,1)S(1)}, u32[]{:S(2)}, u32[]{:S(2)}) async-start(bf16[8,16,1152]{2,1,0:T(8,128)(2,1)} %pack_state.1), calls=%async_computation | async-start | bytes 589824 | tf_op jit(solution)/shard_map/all_to_all | solution.py:450
  9.6 0.0 copy-done.17
  9.6 0.0 copy-done.16
  9.6 0.0 copy-done.1
  9.6 0.0 copy-done.7
  9.6 0.0 copy-done.2
  9.6 0.0 copy-done.6
  9.6 0.0 copy-done.5
  9.6 0.0 copy-done.3
  9.6 4.1 %prepare.1 = (bf16[8,192,512]{2,1,0:T(8,128)(2,1)S(1)}, f32[8,256]{1,0:T(8,128)S(1)}, bf16[768,256]{1,0:T(8,128)(2,1)}, bf16[768,256]{1,0:T(8,128)(2,1)}, bf16[2...) custom-call(s32[384]{0:T(512)} %lats_hbm.1, ...), custom_call_target="tpu_custom_call" | custom-call | flops 6000000000 | bytes 2000000 | tf_op jit(solution)/shard_map/prepare/pallas_call | solution.py:38
  13.8 2.6 %all-to-all-done.recv_ref = bf16[8,16,1152]{2,1,0:T(8,128)(2,1)S(1)} async-done(((bf16[8,16,1152]{2,1,0:T(8,128)(2,1)}), bf16[8,16,1152]{2,1,0:T(8,128)(2,1)S(1)}, u32[]{:S(2)}, u32[]{:S(2)}) %all-to-all-start) | async-done | bytes 294944 | tf_op jit(solution)/shard_map/all_to_all | solution.py:450
  16.4 0.0 copy-start.11
  16.4 0.0 copy-start.12
  16.4 0.0 copy-start.13
  16.4 1.3 %to_fourier.1 = (bf16[256,1536]{1,0:T(8,128)(2,1)S(1)}, bf16[8,2,64,256]{3,2,1,0:T(8,128)(2,1)S(1)}, f32[32,128]{1,0:T(8,128)S(1)}) custom-call(s32[1,256]{1,0:T(1,128)S(1)} %bitcast.20, bf16[8,16,1152]{2,1,0:T(8,128)(2,1)S(1)} %all-to-all-done.recv_ref, bf16[8,192,512]{2,1,0:T(8,128)(2,1)S(1)} %get-tuple-element.18.band_ref), custom_call_target="tpu_custom_call" | custom-call | flops 1000000000 | bytes 2000000 | tf_op jit(solution)/shard_map/to_fourier/pallas_call | solution.py:38
  17.7 0.0 copy-start.4
  17.7 0.0 copy-start.8
  17.7 0.0 copy-start.9
  17.7 0.0 copy-start.10
  17.7 0.0 copy-start.14
  17.7 0.0 copy-start.15
  17.7 31.4 %all_to_all.32 = bf16[32,8,1536]{2,1,0:T(8,128)(2,1)S(1)} all-to-all(bf16[32,8,1536]{2,1,0:T(8,128)(2,1)S(1)} %bitcast.18), channel_id=1, replica_groups=mesh['lev'=8,'wave'=32] {'wave'}, dimensions={0} | all-to-all | bytes 1572864 | tf_op jit(solution)/shard_map/all_to_all | solution.py:515
  49.1 0.0 copy-done.11
  49.1 0.0 copy-done.12
  49.1 0.0 copy-done.13
  49.1 0.0 copy-done.4
  49.1 0.0 copy-done.8
  49.1 0.0 copy-done.9
  49.2 0.0 copy-done.10
  49.2 0.0 copy-done.14
  49.2 0.0 copy-done.15
  49.2 11.3 %columns.1 = (bf16[256,1536]{1,0:T(8,128)(2,1)S(1)}, bf16[12,64,768]{2,1,0:T(8,128)(2,1)}) custom-call(bf16[256,1536]{1,0:T(8,128)(2,1)S(1)} %bitcast.16, bf16[768,256]{1,0:T(8,128)(2,1)S(1)} %copy-done.9, bf16[768,256]{1,0:T(8,128)(2,1)S(1)} %copy-done.10, bf16[2,128,512]{2,1,0:T(8,128)(2,1)S(1)} %copy-done.13, f32[16,512]{1,0:T(8,128)S(1)} %copy-done.14, ...), custom_call_target="tpu_custom_call" | custom-call | flops 10000000000 | bytes 2000000 | tf_op jit(solution)/shard_map/columns/pallas_call | solution.py:38
  60.5 0.0 copy-start
  60.5 25.5 %all_to_all.33 = bf16[32,8,1536]{2,1,0:T(8,128)(2,1)S(1)} all-to-all(bf16[32,8,1536]{2,1,0:T(8,128)(2,1)S(1)} %bitcast.17), channel_id=1, replica_groups=mesh['lev'=8,'wave'=32] {'wave'}, dimensions={0} | all-to-all | bytes 1572864 | tf_op jit(solution)/shard_map/all_to_all | solution.py:533
  86.1 0.0 copy-done
  86.1 2.0 %to_spectral.1 = bf16[8,16,1152]{2,1,0:T(8,128)(2,1)S(1)} custom-call(s32[1,256]{1,0:T(1,128)S(1)} %bitcast.21, bf16[256,1536]{1,0:T(8,128)(2,1)S(1)} %bitcast.15, bf16[8,192,512]{2,1,0:T(8,128)(2,1)S(1)} %get-tuple-element.18.band_ref, bf16[8,2,64,256]{3,2,1,0:T(8,128)(2,1)S(1)} %get-tuple-element.29.state_ref, f32[8,256]{1,0:T(8,128)S(1)} %get-tuple-element.30.const_ref, ...), custom_call_target="tpu_custom_call" | custom-call | flops 1000000000 | bytes 2000000 | tf_op jit(solution)/shard_map/to_spectral/pallas_call | solution.py:38
  88.0 13.9 %all_to_all.34.recv_ref = bf16[8,16,1152]{2,1,0:T(8,128)(2,1)S(1)} all-to-all(bf16[8,16,1152]{2,1,0:T(8,128)(2,1)S(1)} %to_spectral.1), channel_id=1, replica_groups=mesh['lev'=8,'wave'=32] {'lev'}, dimensions={0} | all-to-all | bytes 589824 | tf_op jit(solution)/shard_map/all_to_all | solution.py:557
  102.0 1.2 %unpack_state.1 = f32[8,2,8,2,4,256]{5,4,3,2,1,0:T(4,128)} custom-call(s32[1,256]{1,0:T(1,128)S(1)} %bitcast.22, bf16[8,16,1152]{2,1,0:T(8,128)(2,1)S(1)} %all_to_all.34.recv_ref), custom_call_target="tpu_custom_call" | custom-call | flops 100000000 | bytes 2000000 | tf_op jit(solution)/shard_map/unpack_state/pallas_call | solution.py:38
  (2 shorter events, 0.0 us)
Async XLA Ops:
  0.6 9.0 %copy-start.1 = (s32[256]{0:T(256)S(1)}, s32[256]{0:T(256)}, u32[]{:S(2)}) copy-start(s32[256]{0:T(256)} %waves_hbm.1) | copy-start | bytes 3076
  0.6 8.9 %copy-start.17 = (f32[384]{0:T(512)S(1)}, f32[384]{0:T(512)}, u32[]{:S(2)}) copy-start(f32[384]{0:T(512)} %weights_hbm.1) | copy-start | bytes 4612
  0.7 8.9 %copy-start.16 = (s32[384]{0:T(512)S(1)}, s32[384]{0:T(512)}, u32[]{:S(2)}) copy-start(s32[384]{0:T(512)} %lats_hbm.1) | copy-start | bytes 4612
  0.7 8.9 %copy-start.7 = (f32[512]{0:T(512)S(1)}, f32[512]{0:T(512)}, u32[]{:S(2)}) copy-start(f32[512]{0:T(512)} %param.22) | copy-start | bytes 6148
  0.7 8.9 %copy-start.2 = (bf16[512,512]{1,0:T(8,128)(2,1)S(1)}, bf16[512,512]{1,0:T(8,128)(2,1)}, u32[]{:S(2)}) copy-start(bf16[512,512]{1,0:T(8,128)(2,1)} %w_mid_ref.1) | copy-start | bytes 1572868
  0.7 8.9 %copy-start.6 = (f32[512]{0:T(512)S(1)}, f32[512]{0:T(512)}, u32[]{:S(2)}) copy-start(f32[512]{0:T(512)} %param.20) | copy-start | bytes 6148
  0.7 8.9 %copy-start.5 = (f32[512]{0:T(512)S(1)}, f32[512]{0:T(512)}, u32[]{:S(2)}) copy-start(f32[512]{0:T(512)} %param.19) | copy-start | bytes 6148
  0.7 8.9 %copy-start.3 = (bf16[64,512]{1,0:T(8,128)(2,1)S(1)}, bf16[64,512]{1,0:T(8,128)(2,1)}, u32[]{:S(2)}) copy-start(bf16[64,512]{1,0:T(8,128)(2,1)} %w_in_ref.1) | copy-start | bytes 196612
  3.0 13.4 %all-to-all-start = ((bf16[8,16,1152]{2,1,0:T(8,128)(2,1)}), bf16[8,16,1152]{2,1,0:T(8,128)(2,1)S(1)}, u32[]{:S(2)}, u32[]{:S(2)}) async-start(bf16[8,16,1152]{2,1,0:T(8,128)(2,1)} %pack_state.1), calls=%async_computation | async-start | bytes 589824 | tf_op jit(solution)/shard_map/all_to_all | solution.py:450
  16.4 32.7 %copy-start.11 = (bf16[256,768]{1,0:T(8,128)(2,1)S(1)}, bf16[256,768]{1,0:T(8,128)(2,1)}, u32[]{:S(2)}) copy-start(bf16[256,768]{1,0:T(8,128)(2,1)} %get-tuple-element.25.cos_ref) | copy-start | bytes 1179652
  16.4 32.7 %copy-start.12 = (bf16[256,768]{1,0:T(8,128)(2,1)S(1)}, bf16[256,768]{1,0:T(8,128)(2,1)}, u32[]{:S(2)}) copy-start(bf16[256,768]{1,0:T(8,128)(2,1)} %get-tuple-element.26.sin_ref) | copy-start | bytes 1179652
  16.4 32.7 %copy-start.13 = (bf16[2,128,512]{2,1,0:T(8,128)(2,1)S(1)}, bf16[2,128,512]{2,1,0:T(8,128)(2,1)}, u32[]{:S(2)}) copy-start(bf16[2,128,512]{2,1,0:T(8,128)(2,1)} %get-tuple-element.22.first_ref) | copy-start | bytes 786436
  17.7 31.5 %copy-start.4 = (bf16[512,64]{0,1:T(8,128)(2,1)S(1)}, bf16[512,64]{0,1:T(8,128)(2,1)}, u32[]{:S(2)}) copy-start(bf16[512,64]{0,1:T(8,128)(2,1)} %param.23) | copy-start | bytes 196612
  17.7 31.5 %copy-start.8 = (bf16[512,512]{1,0:T(8,128)(2,1)S(1)}, bf16[512,512]{1,0:T(8,128)(2,1)}, u32[]{:S(2)}) copy-start(bf16[512,512]{1,0:T(8,128)(2,1)} %get-tuple-element.24.mid_ref) | copy-start | bytes 1572868
  17.7 31.5 %copy-start.9 = (bf16[768,256]{1,0:T(8,128)(2,1)S(1)}, bf16[768,256]{1,0:T(8,128)(2,1)}, u32[]{:S(2)}) copy-start(bf16[768,256]{1,0:T(8,128)(2,1)} %get-tuple-element.20.cos_t_ref) | copy-start | bytes 1179652
  17.7 31.5 %copy-start.10 = (bf16[768,256]{1,0:T(8,128)(2,1)S(1)}, bf16[768,256]{1,0:T(8,128)(2,1)}, u32[]{:S(2)}) copy-start(bf16[768,256]{1,0:T(8,128)(2,1)} %get-tuple-element.21.sin_t_ref) | copy-start | bytes 1179652
  17.7 31.5 %copy-start.14 = (f32[16,512]{1,0:T(8,128)S(1)}, f32[16,512]{1,0:T(8,128)}, u32[]{:S(2)}) copy-start(f32[16,512]{1,0:T(8,128)} %get-tuple-element.23.bias_ref) | copy-start | bytes 98308
  17.7 31.5 %copy-start.15 = (f32[1,768]{1,0:T(1,128)S(1)}, f32[1,768]{1,0:T(1,128)}, u32[]{:S(2)}) copy-start(f32[1,768]{1,0:T(1,128)} %get-tuple-element.27.scale_ref) | copy-start | bytes 9220
  60.5 25.6 %copy-start = (f32[32,32,256]{2,1,0:T(8,128)S(1)}, f32[32,32,256]{2,1,0:T(8,128)}, u32[]{:S(2)}) copy-start(f32[32,32,256]{2,1,0:T(8,128)} %get-tuple-element.32.coupling_ref) | copy-start | bytes 3145732
